TPU v7x, 128 devices: a whole 4x4x4 slice. The times are simulated.
128 devices in a mesh: section: 2 (over core), ctx: 16 (over z, y), tp: 4 (over x).
Axes of the slice: x: 4, y: 4, z: 4, core: 2. Of those that a mesh axis runs over, the one named last changes fastest.
Arguments:
- block_input: bfloat16 [2, 8192, 512], P(None, ('ctx', 'tp')), may hold values from -6 to 6
- output_grad: bfloat16 [2, 8192, 512], P(None, ('ctx', 'tp')), may hold values from -6 to 6
- sequence_lengths: int32 [2, 4], replicated, may hold values from 1 to 7680, as said below
- norm_gain: float32 [2, 2, 512], P('section'), may hold values from 0.1 to 1.9
- norm_bias: float32 [2, 2, 512], P('section'), may hold values from -1.8 to 1.8
- attention_weight: bfloat16 [2, 3, 512, 512], P('section', None, None, 'tp'), may hold values from -0.25 to 0.25
- attention_bias: float32 [2, 3, 512], P('section', None, 'tp'), may hold values from -0.6 to 0.6
- output_weight: bfloat16 [2, 512, 512], P('section', 'tp'), may hold values from -3 to 3
- up_weight: bfloat16 [2, 512, 2048], P('section', None, 'tp'), may hold values from -0.25 to 0.25
- up_bias: float32 [2, 2048], P('section', 'tp'), may hold values from -1.8 to 1.8
- down_weight: bfloat16 [2, 2048, 512], P('section', 'tp'), may hold values from -0.125 to 0.125
- branch_bias: float32 [2, 512], P('section'), may hold values from -1.8 to 1.8
Outputs:
- section_output: bfloat16 [2, 2, 8192, 512], P('section', None, ('ctx', 'tp'))
- section_input_grad: bfloat16 [2, 2, 8192, 512], P('section', None, ('ctx', 'tp'))
- norm_gain_grad: float32 [2, 2, 512], P('section')
- norm_bias_grad: float32 [2, 2, 512], P('section')
- attention_weight_grad: float32 [2, 3, 512, 512], P('section', None, None, 'tp')
- attention_bias_grad: float32 [2, 3, 512], P('section', None, 'tp')
- output_weight_grad: float32 [2, 512, 512], P('section', 'tp')
- up_weight_grad: float32 [2, 512, 2048], P('section', None, 'tp')
- up_bias_grad: float32 [2, 2048], P('section', 'tp')
- down_weight_grad: float32 [2, 2048, 512], P('section', 'tp')
- branch_bias_grad: float32 [2, 512], P('section')
Inputs may be any that keep to these rules, and one draw needn't show every extreme that they name: `sequence_lengths`: row m holds the lengths of the 4 sequences packed in order into micro-batch m; they sum to 8192. The second sequence is the longest, exactly 7680 tokens; it begins within the first 512 tokens and ends within the last 512.
All inputs are finite; a program needn't handle non-finite values.
Results may differ from a plain program's by a relative error of at most 0.028.
Values may be sent and summed in bfloat16 or wider, within the bound.
A program may use at most 128 MiB of HBM per device.

v0:
```python
from functools import partial

import jax
import jax.numpy as jnp
from jax import lax
from jax.sharding import PartitionSpec as P

HEAD_DIM = 64
ROT = 16


def from_behind(value, axis, steps):
    count = lax.axis_size(axis)
    first, last = (max(0, -steps), min(count, count - steps))
    return lax.ppermute(value, axis, [(source, source + steps) for source in range(first, last)])


def norm_pair(rows, gains, biases):
    centre = rows - jnp.mean(rows, axis=-1, keepdims=True)
    spread = jnp.mean(centre * centre, axis=-1, keepdims=True)
    normed = centre * lax.rsqrt(spread + 1e-05)
    return (normed * gains[0] + biases[0], normed * gains[1] + biases[1])


def sequence_starts(lengths, positions):
    ends = jnp.cumsum(lengths).astype(jnp.int32)
    before = jnp.where(ends[None, :] <= positions[:, None], lengths[None, :], 0)
    return jnp.sum(before, axis=1).astype(jnp.int32)


def rotary_tables(offsets):
    rates = 1.0 / 10000.0 ** (jnp.arange(0, ROT, 2).astype(jnp.float32) / ROT)
    angles = offsets.astype(jnp.float32)[:, None] * rates[None, :]
    return (jnp.cos(angles), jnp.sin(angles))


def rotate(values, cosine, sine):
    width = cosine.shape[-1]
    first = values[..., :width]
    second = values[..., width : 2 * width]
    rest = values[..., 2 * width :]
    cos_rows = cosine[:, None, :]
    sin_rows = sine[:, None, :]
    return jnp.concatenate(
        [first * cos_rows - second * sin_rows, second * cos_rows + first * sin_rows, rest], axis=-1
    )


def block_view(keys_all, values_all, index, width):
    keys = lax.dynamic_slice_in_dim(keys_all, index * width, width, 0)
    values = lax.dynamic_slice_in_dim(values_all, index * width, width, 0)
    return (keys, values)


def block_scores(queries, keys, query_place, query_start, first_key):
    scale = queries.shape[2] ** (-0.5)
    scores = jnp.einsum("qhd,khd->hqk", queries, keys, preferred_element_type=jnp.float32) * scale
    key_place = first_key + jnp.arange(keys.shape[0], dtype=jnp.int32)
    allowed = (key_place[None, :] <= query_place[:, None]) & (
        key_place[None, :] >= query_start[:, None]
    )
    return (scores, allowed[None])


def block_needed(query_place, query_start, first_key, width, active):
    return active & (first_key <= query_place[-1]) & (first_key + width > query_start[0])


def attend(queries, query_place, query_start, keys_all, values_all, width, active):
    blocks = keys_all.shape[0] // width
    heads = queries.shape[1]
    count = queries.shape[0]

    def collect_stats(index, carry):

        def update(state):
            top, total = state
            keys, values = block_view(keys_all, values_all, index, width)
            scores, allowed = block_scores(queries, keys, query_place, query_start, index * width)
            block_top = jnp.max(jnp.where(allowed, scores, -1e30), axis=-1)
            new_top = jnp.maximum(top, block_top)
            weights = jnp.where(allowed, jnp.exp(scores - new_top[..., None]), 0.0)
            return (new_top, total * jnp.exp(top - new_top) + jnp.sum(weights, axis=-1))

        return lax.cond(
            block_needed(query_place, query_start, index * width, width, active),
            update,
            lambda state: state,
            carry,
        )

    start_top = jnp.full((heads, count), -1e30, jnp.float32)
    top, total = lax.fori_loop(
        0, blocks, collect_stats, (start_top, jnp.zeros((heads, count), jnp.float32))
    )
    log_total = top + jnp.log(jnp.where(active, total, 1.0))

    def collect_values(index, result):

        def update(state):
            keys, values = block_view(keys_all, values_all, index, width)
            scores, allowed = block_scores(queries, keys, query_place, query_start, index * width)
            weights = jnp.where(allowed, jnp.exp(scores - log_total[..., None]), 0.0).astype(
                jnp.bfloat16
            )
            return state + jnp.einsum(
                "hqk,khd->qhd", weights, values, preferred_element_type=jnp.float32
            )

        return lax.cond(
            block_needed(query_place, query_start, index * width, width, active),
            update,
            lambda state: state,
            result,
        )

    outputs = lax.fori_loop(0, blocks, collect_values, jnp.zeros(queries.shape, jnp.float32))
    return (outputs, log_total)


def row_delta(out_grads, outputs):
    return jnp.sum(out_grads.astype(jnp.float32) * outputs, axis=-1).T


def attend_back(
    queries,
    out_grads,
    delta,
    log_total,
    query_place,
    query_start,
    keys_all,
    values_all,
    width,
    active,
    key_grads,
    value_grads,
):
    blocks = keys_all.shape[0] // width
    scale = queries.shape[2] ** (-0.5)

    def visit(index, carry):

        def update(state):
            query_grad, key_total, value_total = state
            keys, values = block_view(keys_all, values_all, index, width)
            scores, allowed = block_scores(queries, keys, query_place, query_start, index * width)
            weights = jnp.where(allowed, jnp.exp(scores - log_total[..., None]), 0.0)
            weight_grad = jnp.einsum(
                "qhd,khd->hqk", out_grads, values, preferred_element_type=jnp.float32
            )
            score_grad = (weights * (weight_grad - delta[..., None])).astype(jnp.bfloat16)
            query_grad = (
                query_grad
                + jnp.einsum("hqk,khd->qhd", score_grad, keys, preferred_element_type=jnp.float32)
                * scale
            )
            key_part = (
                jnp.einsum("hqk,qhd->khd", score_grad, queries, preferred_element_type=jnp.float32)
                * scale
            )
            value_part = jnp.einsum(
                "hqk,qhd->khd",
                weights.astype(jnp.bfloat16),
                out_grads,
                preferred_element_type=jnp.float32,
            )
            first = index * width
            key_total = lax.dynamic_update_slice_in_dim(
                key_total, lax.dynamic_slice_in_dim(key_total, first, width, 0) + key_part, first, 0
            )
            value_total = lax.dynamic_update_slice_in_dim(
                value_total,
                lax.dynamic_slice_in_dim(value_total, first, width, 0) + value_part,
                first,
                0,
            )
            return (query_grad, key_total, value_total)

        return lax.cond(
            block_needed(query_place, query_start, index * width, width, active),
            update,
            lambda state: state,
            carry,
        )

    return lax.fori_loop(
        0, blocks, visit, (jnp.zeros(queries.shape, jnp.float32), key_grads, value_grads)
    )


def layer_forward(rows, lengths, active, params):
    (
        gains,
        biases,
        attention_weight,
        attention_bias,
        output_weight,
        up_weight,
        up_bias,
        down_weight,
        branch_bias,
    ) = params
    shard_index = lax.axis_index("ctx")
    width = rows.shape[0] * lax.axis_size("tp")
    heads = attention_weight.shape[2] // HEAD_DIM
    shaped = (width, heads, HEAD_DIM)
    attention_in, feed_in = norm_pair(rows, gains, biases)
    attention_in, feed_in = (
        lax.all_gather(attention_in.astype(jnp.bfloat16), "tp", axis=0, tiled=True),
        lax.all_gather(feed_in.astype(jnp.bfloat16), "tp", axis=0, tiled=True),
    )
    projected = (
        jnp.einsum(
            "rd,kdc->krc", attention_in, attention_weight, preferred_element_type=jnp.float32
        )
        + attention_bias[:, None, :]
    )
    positions = shard_index * width + jnp.arange(width, dtype=jnp.int32)
    starts = sequence_starts(lengths, positions)
    cosine, sine = rotary_tables(positions - starts)
    queries = rotate(projected[0].reshape(shaped), cosine, sine).astype(jnp.bfloat16)
    keys = rotate(projected[1].reshape(shaped), cosine, sine).astype(jnp.bfloat16)
    values = projected[2].astype(jnp.bfloat16)
    keys_all, values_all = (
        lax.all_gather(keys.reshape(width, -1), "ctx", axis=0, tiled=True),
        lax.all_gather(values, "ctx", axis=0, tiled=True),
    )
    keys_all = keys_all.reshape(-1, heads, HEAD_DIM)
    values_all = values_all.reshape(-1, heads, HEAD_DIM)
    kept = {
        "rows": rows,
        "attention_in": attention_in,
        "feed_in": feed_in,
        "queries": queries,
        "keys_all": keys_all,
        "values_all": values_all,
        "positions": positions,
        "starts": starts,
        "cosine": cosine,
        "sine": sine,
        "lengths": lengths,
    }
    full_out, full_log = attend(queries, positions, starts, keys_all, values_all, width, active)
    attention = full_out.astype(jnp.bfloat16)
    kept.update({"full_out": full_out, "full_log": full_log})
    up_pre = jnp.dot(feed_in, up_weight, preferred_element_type=jnp.float32) + up_bias
    hidden = jax.nn.gelu(up_pre, approximate=False).astype(jnp.bfloat16)
    flat_attention = attention.reshape(width, -1)
    count = rows.shape[0] * lax.axis_size("tp")
    left = jnp.dot(
        lax.slice_in_dim(flat_attention, 0, count, axis=0),
        output_weight,
        preferred_element_type=jnp.float32,
    )
    right = jnp.dot(
        lax.slice_in_dim(hidden, 0, count, axis=0), down_weight, preferred_element_type=jnp.float32
    )
    branch = lax.psum_scatter(
        (left + right).astype(jnp.bfloat16), "tp", scatter_dimension=0, tiled=True
    ).astype(jnp.float32)
    kept.update({"attention": flat_attention, "up_pre": up_pre, "hidden": hidden})
    return (rows + branch + branch_bias, kept)


def layer_backward(grad_rows, active, params, kept):
    (
        gains,
        biases,
        attention_weight,
        attention_bias,
        output_weight,
        up_weight,
        up_bias,
        down_weight,
        branch_bias,
    ) = params
    width = grad_rows.shape[0] * lax.axis_size("tp")
    heads = attention_weight.shape[2] // HEAD_DIM
    shaped = (width, heads, HEAD_DIM)
    keys_all = kept["keys_all"]
    values_all = kept["values_all"]
    cosine = kept["cosine"]
    sine = kept["sine"]
    grad_full = lax.all_gather(grad_rows.astype(jnp.bfloat16), "tp", axis=0, tiled=True)
    output_weight_grad = jnp.einsum(
        "rc,rd->cd", kept["attention"], grad_full, preferred_element_type=jnp.float32
    )
    down_weight_grad = jnp.einsum(
        "rf,rd->fd", kept["hidden"], grad_full, preferred_element_type=jnp.float32
    )
    attention_grad = (
        jnp.einsum("rd,cd->rc", grad_full, output_weight, preferred_element_type=jnp.float32)
        .astype(jnp.bfloat16)
        .reshape(shaped)
    )
    hidden_grad = jnp.einsum(
        "rd,fd->rf", grad_full, down_weight, preferred_element_type=jnp.float32
    )
    _, gelu_back = jax.vjp(partial(jax.nn.gelu, approximate=False), kept["up_pre"])
    up_grad = gelu_back(hidden_grad)[0].astype(jnp.bfloat16)
    up_bias_grad = jnp.sum(up_grad.astype(jnp.float32), axis=0)
    up_weight_grad = jnp.einsum(
        "rd,rf->df", kept["feed_in"], up_grad, preferred_element_type=jnp.float32
    )
    feed_in_grad = jnp.einsum("rf,df->rd", up_grad, up_weight, preferred_element_type=jnp.float32)
    total_rows = keys_all.shape[0]
    key_grads = jnp.zeros((total_rows, heads, HEAD_DIM), jnp.float32)
    value_grads = jnp.zeros((total_rows, heads, HEAD_DIM), jnp.float32)
    full_delta = row_delta(attention_grad, kept["full_out"])
    full_query, key_grads, value_grads = attend_back(
        kept["queries"],
        attention_grad,
        full_delta,
        kept["full_log"],
        kept["positions"],
        kept["starts"],
        keys_all,
        values_all,
        width,
        active,
        key_grads,
        value_grads,
    )
    query_grad = rotate(full_query, cosine, -sine).astype(jnp.bfloat16)
    key_grad, value_grad = (
        lax.psum_scatter(
            key_grads.reshape(total_rows, -1).astype(jnp.bfloat16),
            "ctx",
            scatter_dimension=0,
            tiled=True,
        ).astype(jnp.float32),
        lax.psum_scatter(
            value_grads.reshape(total_rows, -1).astype(jnp.bfloat16),
            "ctx",
            scatter_dimension=0,
            tiled=True,
        ).astype(jnp.float32),
    )
    key_grad = rotate(key_grad.reshape(shaped), cosine, -sine).astype(jnp.bfloat16)
    projection_grad = jnp.stack(
        [
            query_grad.reshape(width, -1),
            key_grad.reshape(width, -1),
            value_grad.astype(jnp.bfloat16),
        ]
    )
    attention_weight_grad = jnp.einsum(
        "rd,krc->kdc", kept["attention_in"], projection_grad, preferred_element_type=jnp.float32
    )
    attention_bias_grad = jnp.sum(projection_grad.astype(jnp.float32), axis=1)
    attention_in_grad = jnp.einsum(
        "krc,kdc->rd", projection_grad, attention_weight, preferred_element_type=jnp.float32
    )
    attention_part, feed_part = (
        lax.psum_scatter(
            attention_in_grad.astype(jnp.bfloat16), "tp", scatter_dimension=0, tiled=True
        ).astype(jnp.float32),
        lax.psum_scatter(
            feed_in_grad.astype(jnp.bfloat16), "tp", scatter_dimension=0, tiled=True
        ).astype(jnp.float32),
    )
    _, norm_back = jax.vjp(norm_pair, kept["rows"], gains, biases)
    rows_grad, gains_grad, biases_grad = norm_back((attention_part, feed_part))
    input_grad = grad_rows + rows_grad
    wide = (
        attention_weight_grad,
        attention_bias_grad,
        output_weight_grad,
        up_weight_grad,
        up_bias_grad,
        down_weight_grad,
    )
    small = (gains_grad, biases_grad, jnp.sum(grad_rows, axis=0))
    return (input_grad, wide, small)


def local(
    block_input,
    output_grad,
    sequence_lengths,
    norm_gain,
    norm_bias,
    attention_weight,
    attention_bias,
    output_weight,
    up_weight,
    up_bias,
    down_weight,
    branch_bias,
):
    params = (
        norm_gain[0],
        norm_bias[0],
        attention_weight[0],
        attention_bias[0],
        output_weight[0],
        up_weight[0],
        up_bias[0],
        down_weight[0],
        branch_bias[0],
    )
    first_section = lax.axis_index("section") == 0
    micro = block_input.shape[0]
    empty = jnp.zeros(block_input.shape[1:], jnp.bfloat16)
    sent = empty
    outputs = []
    saved = []
    for tick in range(micro + 1):
        arrived = empty if tick == 0 else from_behind(sent, "section", 1)
        rows = jnp.where(first_section, block_input[min(tick, micro - 1)], arrived).astype(
            jnp.float32
        )
        lengths = jnp.where(
            first_section,
            sequence_lengths[min(tick, micro - 1)],
            sequence_lengths[max(tick - 1, 0)],
        )
        active = jnp.where(first_section, tick < micro, tick >= 1)
        result, kept = layer_forward(rows, lengths, active, params)
        sent = result.astype(jnp.bfloat16)
        outputs.append(sent)
        saved.append((active, kept))
    returned = empty
    input_grads = []
    wide_total = None
    small_total = None
    for tick in range(micro + 1):
        active, kept = saved[micro - tick]
        arrived = empty if tick == 0 else from_behind(returned, "section", -1)
        given = output_grad[max(micro - 1 - tick, 0)] if tick < micro else empty
        cotangent = jnp.where(first_section, arrived, given).astype(jnp.float32)
        input_grad, wide, small = layer_backward(cotangent, active, params, kept)
        returned = input_grad.astype(jnp.bfloat16)
        input_grads.append(returned)
        wide = (
            lax.psum(wide[0].astype(jnp.bfloat16), "ctx").astype(jnp.float32),
            lax.psum(wide[1].astype(jnp.bfloat16), "ctx").astype(jnp.float32),
            lax.psum(wide[2].astype(jnp.bfloat16), "ctx").astype(jnp.float32),
            lax.psum(wide[3].astype(jnp.bfloat16), "ctx").astype(jnp.float32),
            lax.psum(wide[4].astype(jnp.bfloat16), "ctx").astype(jnp.float32),
            lax.psum(wide[5].astype(jnp.bfloat16), "ctx").astype(jnp.float32),
        )
        wide_total = wide if wide_total is None else jax.tree.map(jnp.add, wide_total, wide)
        small_total = small if small_total is None else jax.tree.map(jnp.add, small_total, small)
    small_total = lax.psum(small_total, ("ctx", "tp"))
    section_output = jnp.stack(
        [jnp.where(first_section, outputs[index], outputs[index + 1]) for index in range(micro)]
    )[None]
    section_input_grad = jnp.stack(
        [
            jnp.where(first_section, input_grads[micro - index], input_grads[micro - 1 - index])
            for index in range(micro)
        ]
    )[None]
    return (
        section_output,
        section_input_grad,
        small_total[0][None],
        small_total[1][None],
        wide_total[0][None],
        wide_total[1][None],
        wide_total[2][None],
        wide_total[3][None],
        wide_total[4][None],
        wide_total[5][None],
        small_total[2][None],
    )


def solution(mesh):
    placed = (
        P(None, ("ctx", "tp"), None),
        P(None, ("ctx", "tp"), None),
        P(),
        P("section", None, None),
        P("section", None, None),
        P("section", None, None, "tp"),
        P("section", None, "tp"),
        P("section", "tp", None),
        P("section", None, "tp"),
        P("section", "tp"),
        P("section", "tp", None),
        P("section", None),
    )
    return jax.shard_map(
        local,
        mesh=mesh,
        in_specs=placed,
        out_specs=(
            P("section", None, ("ctx", "tp"), None),
            P("section", None, ("ctx", "tp"), None),
            P("section", None, None),
            P("section", None, None),
            P("section", None, None, "tp"),
            P("section", None, "tp"),
            P("section", "tp", None),
            P("section", None, "tp"),
            P("section", "tp"),
            P("section", "tp", None),
            P("section", None),
        ),
        check_vma=False,
    )
```

profile of v0, /device:TPU:0, one launch (start us, length us, event | category | flops | bytes accessed | tf_op | source)
XLA Modules:
  0.0 2314.0 jit_solution(18312193607361552879)
XLA Ops:
  13.5 13.2 all_gather.45
  31.2 12.8 all_gather.48
  44.0 3.7 multiply_convert_fusion.2
  47.7 33.0 %all-gather.11.cloned.1.call-done = bf16[8192,128]{0,1:T(8,128)(2,1)} async-done(((bf16[512,128]{0,1:T(8,128)(2,1)}), bf16[8192,128]{0,1:T(8,128)(2,1)}) %all-gather.11.cloned.1.call-update) | async-done | bytes 2097168 | tf_op jit(solution)/shard_map/all_gather | solution.py:226
  80.7 41.5 %while.144 = (s32[]{:T(128)}, f32[2,512]{1,0:T(2,128)S(1)}, f32[2,512]{1,0:T(2,128)S(1)}, s32[512]{0:T(512)S(1)}, pred[]{:T(512)}, /*index=5*/s32[512]{0:T(512)S...) while((s32[]{:T(128)}, f32[2,512]{1,0:T(2,128)S(1)}, ...), condition=%wide.region_9.10_spmd, body=%wide.region_4.9_spmd.sunk | while | flops 71567880 | bytes 5304640 | solution.py:93
  83.1 2.4 conditional.18
  122.3 8.2 all-gather.17.cloned.1.call-done
  130.5 41.3 %while.145 = (s32[]{:T(128)}, f32[512,2,64]{0,2,1:T(8,128)S(1)}, s32[512]{0:T(512)S(1)}, pred[]{:T(512)}, s32[512]{0:T(512)S(1)}, /*index=5*/bf16[8192,2,64]{0,2...) while((s32[]{:T(128)}, f32[512,2,64]{0,2,1:T(8,128)S(1)}, ...), condition=%wide.region_13.14_spmd, body=%wide.region_10.13_spmd.sunk | while | flops 137167360 | bytes 1455404 | solution.py:117
  175.3 79.8 %reduce-scatter.16.cloned.1.call-done = bf16[128,512]{1,0:T(8,128)(2,1)} async-done(((bf16[512,512]{1,0:T(8,128)(2,1)}), bf16[128,512]{1,0:T(8,128)(2,1)}) %reduce-scatter.16.cloned.1.call-update) | async-done | bytes 131088 | tf_op jit(solution)/shard_map/reduce_scatter | solution.py:259
  258.9 13.5 all_gather.49
  276.8 13.0 all_gather.52
  289.8 3.8 multiply_convert_fusion.1
  293.6 29.2 %all-gather.13.cloned.1.call-done = bf16[8192,128]{0,1:T(8,128)(2,1)} async-done(((bf16[512,128]{0,1:T(8,128)(2,1)}), bf16[8192,128]{0,1:T(8,128)(2,1)}) %all-gather.13.cloned.1.call-update) | async-done | bytes 2097168 | tf_op jit(solution)/shard_map/all_gather | solution.py:226
  322.8 41.5 %while.146 = (s32[]{:T(128)}, f32[2,512]{1,0:T(2,128)S(1)}, f32[2,512]{1,0:T(2,128)S(1)}, s32[512]{0:T(512)S(1)}, s32[512]{0:T(512)S(1)}, /*index=5*/bf16[8192,2...) while((s32[]{:T(128)}, f32[2,512]{1,0:T(2,128)S(1)}, f32[2,512]{1,0:T(2,128)S(1)}, ...), condition=%wide.region_24.25_spmd, body=%wide.region_19.24_spmd.sunk | while | flops 71567880 | bytes 5304629 | solution.py:93
  325.2 2.4 conditional.20
  364.3 7.6 all-gather.19.cloned.1.call-done
  371.9 41.3 %while.147 = (s32[]{:T(128)}, f32[512,2,64]{0,2,1:T(8,128)S(1)}, s32[512]{0:T(512)S(1)}, s32[512]{0:T(512)S(1)}, bf16[8192,2,64]{0,2,1:T(8,128)(2,1)}, /*index=5...) while((s32[]{:T(128)}, f32[512,2,64]{0,2,1:T(8,128)S(1)}, ...), condition=%wide.region_28.29_spmd, body=%wide.region_25.28_spmd.sunk | while | flops 137167360 | bytes 1455393 | solution.py:117
  417.2 80.5 %reduce-scatter.18.cloned.1.call-done = bf16[128,512]{1,0:T(8,128)(2,1)} async-done(((bf16[512,512]{1,0:T(8,128)(2,1)}), bf16[128,512]{1,0:T(8,128)(2,1)}) %reduce-scatter.18.cloned.1.call-update) | async-done | bytes 131088 | tf_op jit(solution)/shard_map/reduce_scatter | solution.py:259
  502.8 13.5 all_gather.53
  521.0 12.8 all-gather.3
  533.8 32.5 %all-gather.15.cloned.1.call-done = bf16[8192,128]{0,1:T(8,128)(2,1)} async-done(((bf16[512,128]{0,1:T(8,128)(2,1)}), bf16[8192,128]{0,1:T(8,128)(2,1)}) %all-gather.15.cloned.1.call-update) | async-done | bytes 2097168 | tf_op jit(solution)/shard_map/all_gather | solution.py:226
  566.3 43.0 %while.148 = (s32[]{:T(128)}, f32[2,512]{1,0:T(2,128)S(1)}, f32[2,512]{1,0:T(2,128)S(1)}, s32[512]{0:T(512)S(1)}, pred[]{:T(512)}, /*index=5*/s32[512]{0:T(512)S...) while((s32[]{:T(128)}, f32[2,512]{1,0:T(2,128)S(1)}, ...), condition=%wide.region_39.40_spmd, body=%wide.region_34.39_spmd.sunk | while | flops 71567880 | bytes 5304640 | solution.py:93
  609.3 6.2 all-gather.21.cloned.1.call-done
  615.5 39.1 %while.149 = (s32[]{:T(128)}, f32[512,2,64]{0,2,1:T(8,128)S(1)}, s32[512]{0:T(512)S(1)}, pred[]{:T(512)}, s32[512]{0:T(512)S(1)}, /*index=5*/bf16[8192,2,64]{0,2...) while((s32[]{:T(128)}, f32[512,2,64]{0,2,1:T(8,128)S(1)}, ...), condition=%wide.region_43.44_spmd, body=%wide.region_40.43_spmd.sunk | while | flops 137167360 | bytes 1455404 | solution.py:117
  655.5 2.5 broadcast.906.clone
  658.0 2.5 broadcast.906.clone.1
  660.5 39.2 %while.150 = (s32[]{:T(128)}, f32[512,2,64]{0,2,1:T(8,128)S(1)}, f32[8192,2,64]{0,2,1:T(8,128)}, f32[8192,2,64]{0,2,1:T(8,128)}, s32[512]{0:T(512)S(1)}, /*index...) while((s32[]{:T(128)}, f32[512,2,64]{0,2,1:T(8,128)S(1)}, ...), condition=%wide.region_50.51_spmd, body=%wide.region_47.50_spmd.sunk | while | flops 340328960 | bytes 12468656 | solution.py:187
  699.7 3.7 convert_element_type.577
  703.5 2.4 convert_element_type.580
  706.0 2.5 copy.100
  709.3 13.1 all_gather.56
  722.4 8.2 multiply_convert_fusion
  733.4 249.7 %reduce-scatter.24.cloned.1.call-done = bf16[512,128]{0,1:T(8,128)(2,1)} async-done(((bf16[8192,128]{0,1:T(8,128)(2,1)}), bf16[512,128]{0,1:T(8,128)(2,1)}) %reduce-scatter.24.cloned.1.call-update) | async-done | bytes 131088 | tf_op jit(solution)/shard_map/reduce_scatter | solution.py:327
  985.4 75.0 %reduce-scatter.26.cloned.1.call-done = bf16[512,128]{1,0:T(8,128)(2,1)} async-done(((bf16[8192,128]{1,0:T(8,128)(2,1)}), bf16[512,128]{1,0:T(8,128)(2,1)}) %reduce-scatter.26.cloned.1.call-update) | async-done | bytes 131088 | tf_op jit(solution)/shard_map/reduce_scatter | solution.py:333
  1062.7 20.6 reduce-scatter.22.cloned.1.call-done
  1083.2 23.4 %reduce-scatter.28.cloned.1.call-done = bf16[128,512]{1,0:T(8,128)(2,1)} async-done(((bf16[512,512]{1,0:T(8,128)(2,1)}), bf16[128,512]{1,0:T(8,128)(2,1)}) %reduce-scatter.28.cloned.1.call-update) | async-done | bytes 131088 | tf_op jit(solution)/shard_map/reduce_scatter | solution.py:356
  1113.7 13.5 all_gather.58
  1127.5 2.5 broadcast.906.clone.2
  1130.0 2.5 broadcast.906.clone.3
  1132.5 48.0 %while.151 = (s32[]{:T(128)}, f32[512,2,64]{0,2,1:T(8,128)S(1)}, f32[8192,2,64]{0,2,1:T(8,128)}, f32[8192,2,64]{0,2,1:T(8,128)}, s32[512]{0:T(512)S(1)}, /*index...) while((s32[]{:T(128)}, f32[512,2,64]{0,2,1:T(8,128)S(1)}, ...), condition=%wide.region_61.62_spmd, body=%wide.region_58.61_spmd.sunk | while | flops 340328960 | bytes 12468645 | solution.py:187
  1134.9 8.9 conditional.25
  1180.5 3.8 convert_element_type.592
  1184.4 2.4 convert_element_type.595
  1186.8 2.5 copy.103
  1190.5 2.8 fusion.262
  1194.7 196.1 %reduce-scatter.32.cloned.1.call-done = bf16[512,128]{0,1:T(8,128)(2,1)} async-done(((bf16[8192,128]{0,1:T(8,128)(2,1)}), bf16[512,128]{0,1:T(8,128)(2,1)}) %reduce-scatter.32.cloned.1.call-update) | async-done | bytes 131088 | tf_op jit(solution)/shard_map/reduce_scatter | solution.py:327
  1393.0 75.1 %reduce-scatter.34.cloned.1.call-done = bf16[512,128]{1,0:T(8,128)(2,1)} async-done(((bf16[8192,128]{1,0:T(8,128)(2,1)}), bf16[512,128]{1,0:T(8,128)(2,1)}) %reduce-scatter.34.cloned.1.call-update) | async-done | bytes 131088 | tf_op jit(solution)/shard_map/reduce_scatter | solution.py:333
  1470.4 20.5 reduce-scatter.30.cloned.1.call-done
  1490.9 23.4 %reduce-scatter.36.cloned.1.call-done = bf16[128,512]{1,0:T(8,128)(2,1)} async-done(((bf16[512,512]{1,0:T(8,128)(2,1)}), bf16[128,512]{1,0:T(8,128)(2,1)}) %reduce-scatter.36.cloned.1.call-update) | async-done | bytes 131088 | tf_op jit(solution)/shard_map/reduce_scatter | solution.py:356
  1522.0 13.7 all_gather.59
  1536.0 2.5 broadcast.906
  1538.4 2.5 broadcast.906.clone.4
  1541.0 48.1 %while.152 = (s32[]{:T(128)}, f32[512,2,64]{0,2,1:T(8,128)S(1)}, f32[8192,2,64]{0,2,1:T(8,128)}, f32[8192,2,64]{0,2,1:T(8,128)}, s32[512]{0:T(512)S(1)}, /*index...) while((s32[]{:T(128)}, f32[512,2,64]{0,2,1:T(8,128)S(1)}, ...), condition=%wide.region_72.73_spmd, body=%wide.region_69.72_spmd.sunk | while | flops 340328960 | bytes 12468656 | solution.py:187
  1543.4 8.9 conditional.26
  1589.0 3.7 convert_element_type.607
  1592.8 2.4 convert_element_type.610
  1595.3 2.5 copy.106
  1614.7 184.5 %reduce-scatter.40.cloned.1.call-done = bf16[512,128]{0,1:T(8,128)(2,1)} async-done(((bf16[8192,128]{0,1:T(8,128)(2,1)}), bf16[512,128]{0,1:T(8,128)(2,1)}) %reduce-scatter.40.cloned.1.call-update) | async-done | bytes 131088 | tf_op jit(solution)/shard_map/reduce_scatter | solution.py:327
  1801.5 74.9 %reduce-scatter.42.cloned.1.call-done = bf16[512,128]{1,0:T(8,128)(2,1)} async-done(((bf16[8192,128]{1,0:T(8,128)(2,1)}), bf16[512,128]{1,0:T(8,128)(2,1)}) %reduce-scatter.42.cloned.1.call-update) | async-done | bytes 131088 | tf_op jit(solution)/shard_map/reduce_scatter | solution.py:333
  1886.0 13.9 reduce-scatter.20.cloned.1.call-done
  1901.9 41.1 %all-reduce.13 = (bf16[3,128]{1,0:T(4,128)(2,1)S(1)}, bf16[3,128]{1,0:T(4,128)(2,1)S(1)}, bf16[3,128]{1,0:T(4,128)(2,1)S(1)}, bf16[512]{0:T(512)(128)(2,1)S(1)},...) all-reduce(bf16[3,128]{1,0:T(4,128)(2,1)S(1)} %fusion.245, ...), channel_id=1, replica_groups=mesh['section'=2,'ctx'=16,'tp'=4] {'ctx'}, use_global_device_ids=true, to_apply=%region_100.101 | all-reduce | flops 2688 | bytes 10752 | tf_op jit(solution)/shard_map/psum | solution.py:438
  1944.2 3.7 reduce-scatter.44.cloned.1.call-done
  1950.5 347.4 %all-reduce.12 = (f32[1,2,512]{2,1,0:T(2,128)}, f32[1,2,512]{2,1,0:T(2,128)}, f32[1,512]{1,0:T(1,128)}) all-reduce(f32[1,2,512]{2,1,0:T(2,128)S(1)} %add_bitcast_fusion.8, f32[1,2,512]{2,1,0:T(2,128)S(1)} %add_bitcast_fusion.7, f32[1,512]{1,0:T(1,128)S(1)} %bitcast.661), channel_id=1, replica_groups=mesh['section'=2,'ctx'=16,'tp'=4] {'ctx','tp'}, use_global_device_ids=true, to_apply=%region_84.85 | all-reduce | flops 2560 | bytes 20480 | tf_op jit(solution)/shard_map/psum | solution.py:446
  2302.4 2.4 add_bitcast_fusion
  (1024 shorter events, 299.8 us)
Async XLA Ops:
  7.2 73.5 %all-gather.11.cloned.1.call-start = ((), (), s32[]{:S(2)}) async-start(), calls=%async_computation.15 | async-start | bytes 2228224 | tf_op jit(solution)/shard_map/all_gather | solution.py:226
  30.4 100.1 %all-gather.17.cloned.1.call-start = ((), (), s32[]{:S(2)}) async-start(), calls=%async_computation.33 | async-start | bytes 2228224 | tf_op jit(solution)/shard_map/all_gather | solution.py:227
  31.1 224.0 %reduce-scatter.16.cloned.1.call-start = ((), (), s32[]{:S(2)}) async-start(), calls=%async_computation.16 | async-start | bytes 655360 | tf_op jit(solution)/shard_map/reduce_scatter | solution.py:259
  175.3 98.0 %copy-start.120 = (f32[1,3,128]{2,1,0:T(4,128)S(1)}, f32[1,3,128]{2,1,0:T(4,128)}, u32[]{:S(2)}) copy-start(f32[1,3,128]{2,1,0:T(4,128)} %copy-done.119) | copy-start | bytes 4612
  175.3 147.5 %all-gather.13.cloned.1.call-start = ((), (), s32[]{:S(2)}) async-start(), calls=%async_computation.17 | async-start | bytes 2228224 | tf_op jit(solution)/shard_map/all_gather | solution.py:226
  256.1 2.3 collective-permute-start
  258.5 239.2 %copy-start.17 = (bf16[128,512]{1,0:T(8,128)(2,1)}, bf16[128,512]{1,0:T(8,128)(2,1)S(1)}, u32[]{:S(2)}) copy-start(bf16[128,512]{1,0:T(8,128)(2,1)S(1)} %get-tuple-element.2209) | copy-start | bytes 393220
  275.1 96.8 %all-gather.19.cloned.1.call-start = ((), (), s32[]{:S(2)}) async-start(), calls=%async_computation.34 | async-start | bytes 2228224 | tf_op jit(solution)/shard_map/all_gather | solution.py:227
  276.8 221.0 %reduce-scatter.18.cloned.1.call-start = ((), (), s32[]{:S(2)}) async-start(), calls=%async_computation.18 | async-start | bytes 655360 | tf_op jit(solution)/shard_map/reduce_scatter | solution.py:259
  414.8 87.1 %copy-start.93 = (f32[1,1,512]{2,1,0:T(1,128)S(1)}, f32[1,1,512]{2,1,0:T(1,128)}, u32[]{:S(2)}) copy-start(f32[1,1,512]{2,1,0:T(1,128)} %copy-done.91) | copy-start | bytes 6148
  414.9 87.1 %copy-start.97 = (f32[1,1,512]{2,1,0:T(1,128)S(1)}, f32[1,1,512]{2,1,0:T(1,128)}, u32[]{:S(2)}) copy-start(f32[1,1,512]{2,1,0:T(1,128)} %copy-done.95) | copy-start | bytes 6148
  414.9 87.1 %copy-start.124 = (f32[1,1,512]{2,1,0:T(1,128)S(1)}, f32[1,1,512]{2,1,0:T(1,128)}, u32[]{:S(2)}) copy-start(f32[1,1,512]{2,1,0:T(1,128)} %copy-done.122) | copy-start | bytes 6148
  417.2 99.6 %copy-start.121 = (f32[1,3,128]{2,1,0:T(4,128)S(1)}, f32[1,3,128]{2,1,0:T(4,128)}, u32[]{:S(2)}) copy-start(f32[1,3,128]{2,1,0:T(4,128)} %copy-done.119) | copy-start | bytes 4612
  417.2 149.1 %all-gather.15.cloned.1.call-start = ((), (), s32[]{:S(2)}) async-start(), calls=%async_computation.19 | async-start | bytes 2228224 | tf_op jit(solution)/shard_map/all_gather | solution.py:226
  499.3 2.3 collective-permute-start.1
  518.6 97.0 %all-gather.21.cloned.1.call-start = ((), (), s32[]{:S(2)}) async-start(), calls=%async_computation.35 | async-start | bytes 2228224 | tf_op jit(solution)/shard_map/all_gather | solution.py:227
  520.3 462.8 %reduce-scatter.24.cloned.1.call-start = ((), (), s32[]{:S(2)}) async-start(), calls=%async_computation.22 | async-start | bytes 2228224 | tf_op jit(solution)/shard_map/reduce_scatter | solution.py:327
  533.7 121.0 %copy-start.9 = (bf16[1,512,512]{2,1,0:T(8,128)(2,1)}, bf16[1,512,512]{2,1,0:T(8,128)(2,1)S(1)}, u32[]{:S(2)}) copy-start(bf16[1,512,512]{2,1,0:T(8,128)(2,1)S(1)} %all-gather.3) | copy-start | bytes 1572868
  703.5 356.9 %reduce-scatter.26.cloned.1.call-start = ((), (), s32[]{:S(2)}) async-start(), calls=%async_computation.23 | async-start | bytes 2228224 | tf_op jit(solution)/shard_map/reduce_scatter | solution.py:333
  708.5 374.8 %reduce-scatter.22.cloned.1.call-start = ((), (), s32[]{:S(2)}) async-start(), calls=%async_computation.21 | async-start | bytes 655360 | tf_op jit(solution)/shard_map/reduce_scatter | solution.py:359
  732.0 330.6 %copy-start.47 = (bf16[512,512]{1,0:T(8,128)(2,1)}, bf16[512,512]{1,0:T(8,128)(2,1)S(1)}, u32[]{:S(2)}) copy-start(bf16[512,512]{1,0:T(8,128)(2,1)S(1)} %get-tuple-element.2305) | copy-start | bytes 1572868
  732.0 253.0 %copy-start.105 = (f32[512,8]{0,1:T(8,128)S(1)}, f32[512,8]{0,1:T(8,128)}, u32[]{:S(2)}) copy-start(f32[512,8]{0,1:T(8,128)} %get-tuple-element.2287) | copy-start | bytes 49156
  732.0 253.0 %copy-start.116 = (f32[512,8]{0,1:T(8,128)S(1)}, f32[512,8]{0,1:T(8,128)}, u32[]{:S(2)}) copy-start(f32[512,8]{0,1:T(8,128)} %get-tuple-element.2288) | copy-start | bytes 49156
  732.0 328.3 %copy-start.87 = (bf16[1,3,512,128]{3,2,1,0:T(8,128)(2,1)S(1)}, bf16[1,3,512,128]{3,2,1,0:T(8,128)(2,1)}, u32[]{:S(2)}) copy-start(bf16[1,3,512,128]{3,2,1,0:T(8,128)(2,1)} %param.53) | copy-start | bytes 1179652
  733.3 373.3 %reduce-scatter.28.cloned.1.call-start = ((), (), s32[]{:S(2)}) async-start(), calls=%async_computation.24 | async-start | bytes 655360 | tf_op jit(solution)/shard_map/reduce_scatter | solution.py:356
  983.1 123.5 %copy-start.7 = (bf16[128,512]{1,0:T(8,128)(2,1)S(1)}, bf16[128,512]{1,0:T(8,128)(2,1)}, u32[]{:S(2)}) copy-start(bf16[128,512]{1,0:T(8,128)(2,1)} %copy-done.6) | copy-start | bytes 393220
  983.1 123.5 %copy-start.94 = (f32[1,1,512]{2,1,0:T(1,128)S(1)}, f32[1,1,512]{2,1,0:T(1,128)}, u32[]{:S(2)}) copy-start(f32[1,1,512]{2,1,0:T(1,128)} %copy-done.91) | copy-start | bytes 6148
  983.1 123.5 %copy-start.98 = (f32[1,1,512]{2,1,0:T(1,128)S(1)}, f32[1,1,512]{2,1,0:T(1,128)}, u32[]{:S(2)}) copy-start(f32[1,1,512]{2,1,0:T(1,128)} %copy-done.95) | copy-start | bytes 6148
  983.1 123.5 %copy-start.136 = (f32[128]{0:T(128)S(1)}, f32[128]{0:T(128)}, u32[]{:S(2)}) copy-start(f32[128]{0:T(128)} %copy-done.135) | copy-start | bytes 1540
  983.1 123.5 %copy-start.153 = (f32[128]{0:T(128)S(1)}, f32[128]{0:T(128)}, u32[]{:S(2)}) copy-start(f32[128]{0:T(128)} %copy-done.152) | copy-start | bytes 1540
  984.1 124.4 %copy-start.167 = (f32[128]{0:T(128)S(1)}, f32[128]{0:T(128)}, u32[]{:S(2)}) copy-start(f32[128]{0:T(128)} %copy-done.166) | copy-start | bytes 1540
  985.1 124.6 %copy-start.34 = (bf16[1,128,512]{2,1,0:T(8,128)(2,1)S(1)}, bf16[1,128,512]{2,1,0:T(8,128)(2,1)}, u32[]{:S(2)}) copy-start(bf16[1,128,512]{2,1,0:T(8,128)(2,1)} %copy-done.33) | copy-start | bytes 393220
  985.2 123.3 %copy-start.63 = (bf16[1,512,128]{2,1,0:T(8,128)(2,1)}, bf16[1,512,128]{2,1,0:T(8,128)(2,1)S(1)}, u32[]{:S(2)}) copy-start(bf16[1,512,128]{2,1,0:T(8,128)(2,1)S(1)} %copy.101) | copy-start | bytes 393220
  985.2 127.8 %copy-start.90 = (bf16[2,128,512]{2,1,0:T(8,128)(2,1)S(1)}, bf16[2,128,512]{2,1,0:T(8,128)(2,1)}, u32[]{:S(2)}) copy-start(bf16[2,128,512]{2,1,0:T(8,128)(2,1)} %param.49) | copy-start | bytes 786436
  985.4 123.1 %copy-start.65 = (bf16[1,512,128]{2,1,0:T(8,128)(2,1)}, bf16[1,512,128]{2,1,0:T(8,128)(2,1)S(1)}, u32[]{:S(2)}) copy-start(bf16[1,512,128]{2,1,0:T(8,128)(2,1)S(1)} %copy.102) | copy-start | bytes 393220
  1062.6 328.2 %reduce-scatter.32.cloned.1.call-start = ((), (), s32[]{:S(2)}) async-start(), calls=%async_computation.26 | async-start | bytes 2228224 | tf_op jit(solution)/shard_map/reduce_scatter | solution.py:327
  1109.8 3.2 collective-permute-start.2
  1184.3 283.8 %reduce-scatter.34.cloned.1.call-start = ((), (), s32[]{:S(2)}) async-start(), calls=%async_computation.27 | async-start | bytes 2228224 | tf_op jit(solution)/shard_map/reduce_scatter | solution.py:333
  1189.3 301.6 %reduce-scatter.30.cloned.1.call-start = ((), (), s32[]{:S(2)}) async-start(), calls=%async_computation.25 | async-start | bytes 655360 | tf_op jit(solution)/shard_map/reduce_scatter | solution.py:359
  1193.3 277.0 %copy-start.49 = (bf16[512,512]{1,0:T(8,128)(2,1)}, bf16[512,512]{1,0:T(8,128)(2,1)S(1)}, u32[]{:S(2)}) copy-start(bf16[512,512]{1,0:T(8,128)(2,1)S(1)} %get-tuple-element.2303) | copy-start | bytes 1572868
  1193.3 199.4 %copy-start.103 = (f32[512,8]{0,1:T(8,128)S(1)}, f32[512,8]{0,1:T(8,128)}, u32[]{:S(2)}) copy-start(f32[512,8]{0,1:T(8,128)} %get-tuple-element.2290) | copy-start | bytes 49156
  1193.3 199.4 %copy-start.115 = (f32[512,8]{0,1:T(8,128)S(1)}, f32[512,8]{0,1:T(8,128)}, u32[]{:S(2)}) copy-start(f32[512,8]{0,1:T(8,128)} %get-tuple-element.2291) | copy-start | bytes 49156
  1193.3 274.8 %copy-start.88 = (bf16[1,3,512,128]{3,2,1,0:T(8,128)(2,1)S(1)}, bf16[1,3,512,128]{3,2,1,0:T(8,128)(2,1)}, u32[]{:S(2)}) copy-start(bf16[1,3,512,128]{3,2,1,0:T(8,128)(2,1)} %param.53) | copy-start | bytes 1179652
  1194.6 319.6 %reduce-scatter.36.cloned.1.call-start = ((), (), s32[]{:S(2)}) async-start(), calls=%async_computation.28 | async-start | bytes 655360 | tf_op jit(solution)/shard_map/reduce_scatter | solution.py:356
  1390.8 123.5 %copy-start.18 = (bf16[128,512]{1,0:T(8,128)(2,1)S(1)}, bf16[128,512]{1,0:T(8,128)(2,1)}, u32[]{:S(2)}) copy-start(bf16[128,512]{1,0:T(8,128)(2,1)} %copy-done.17) | copy-start | bytes 393220
  1390.8 123.5 %copy-start.99 = (f32[1,1,512]{2,1,0:T(1,128)S(1)}, f32[1,1,512]{2,1,0:T(1,128)}, u32[]{:S(2)}) copy-start(f32[1,1,512]{2,1,0:T(1,128)} %copy-done.95) | copy-start | bytes 6148
  1390.8 123.5 %copy-start.134 = (f32[128]{0:T(128)S(1)}, f32[128]{0:T(128)}, u32[]{:S(2)}) copy-start(f32[128]{0:T(128)} %copy-done.133) | copy-start | bytes 1540
  1390.8 123.5 %copy-start.151 = (f32[128]{0:T(128)S(1)}, f32[128]{0:T(128)}, u32[]{:S(2)}) copy-start(f32[128]{0:T(128)} %copy-done.150) | copy-start | bytes 1540
  1391.7 124.3 %copy-start.165 = (f32[128]{0:T(128)S(1)}, f32[128]{0:T(128)}, u32[]{:S(2)}) copy-start(f32[128]{0:T(128)} %copy-done.164) | copy-start | bytes 1540
  1392.7 124.6 %copy-start.43 = (bf16[128,512]{1,0:T(8,128)(2,1)S(1)}, bf16[128,512]{1,0:T(8,128)(2,1)}, u32[]{:S(2)}) copy-start(bf16[128,512]{1,0:T(8,128)(2,1)} %copy-done.42) | copy-start | bytes 393220
  1392.7 124.6 %copy-start.82 = (bf16[128,512]{1,0:T(8,128)(2,1)S(1)}, bf16[128,512]{1,0:T(8,128)(2,1)}, u32[]{:S(2)}) copy-start(bf16[128,512]{1,0:T(8,128)(2,1)} %copy-done.81) | copy-start | bytes 393220
  1393.0 125.1 %copy-start.69 = (bf16[1,512,128]{2,1,0:T(8,128)(2,1)}, bf16[1,512,128]{2,1,0:T(8,128)(2,1)S(1)}, u32[]{:S(2)}) copy-start(bf16[1,512,128]{2,1,0:T(8,128)(2,1)S(1)} %copy.105) | copy-start | bytes 393220
  1470.3 328.9 %reduce-scatter.40.cloned.1.call-start = ((), (), s32[]{:S(2)}) async-start(), calls=%async_computation.30 | async-start | bytes 2228224 | tf_op jit(solution)/shard_map/reduce_scatter | solution.py:327
  1518.1 3.2 collective-permute-start.3
  1592.8 283.6 %reduce-scatter.42.cloned.1.call-start = ((), (), s32[]{:S(2)}) async-start(), calls=%async_computation.31 | async-start | bytes 2228224 | tf_op jit(solution)/shard_map/reduce_scatter | solution.py:333
  1597.8 302.1 %reduce-scatter.20.cloned.1.call-start = ((), (), s32[]{:S(2)}) async-start(), calls=%async_computation.20 | async-start | bytes 655360 | tf_op jit(solution)/shard_map/reduce_scatter | solution.py:259
  1604.0 340.2 %reduce-scatter.38.cloned.1.call-start = ((), (), s32[]{:S(2)}) async-start(), calls=%async_computation.29 | async-start | bytes 655360 | tf_op jit(solution)/shard_map/reduce_scatter | solution.py:359
  1611.4 336.5 %reduce-scatter.44.cloned.1.call-start = ((), (), s32[]{:S(2)}) async-start(), calls=%async_computation.32 | async-start | bytes 655360 | tf_op jit(solution)/shard_map/reduce_scatter | solution.py:356
  1612.4 188.8 %copy-start.101 = (f32[512,8]{0,1:T(8,128)S(1)}, f32[512,8]{0,1:T(8,128)}, u32[]{:S(2)}) copy-start(f32[512,8]{0,1:T(8,128)} %copy-done.100) | copy-start | bytes 49156
  1612.4 188.8 %copy-start.114 = (f32[512,8]{0,1:T(8,128)S(1)}, f32[512,8]{0,1:T(8,128)}, u32[]{:S(2)}) copy-start(f32[512,8]{0,1:T(8,128)} %get-tuple-element.2272) | copy-start | bytes 49156
  1878.8 421.0 %all-reduce.17.cloned.1.call-start = ((), (), s32[]{:S(2)}) async-start(), calls=%async_computation.36 | async-start | bytes 9437184 | tf_op jit(solution)/shard_map/psum | solution.py:437
  1885.9 412.0 %copy-start.36 = (bf16[128,512]{1,0:T(8,128)(2,1)S(1)}, bf16[128,512]{1,0:T(8,128)(2,1)}, u32[]{:S(2)}) copy-start(bf16[128,512]{1,0:T(8,128)(2,1)} %copy-done.35) | copy-start | bytes 393220
  1885.9 411.9 %copy-start.80 = (bf16[128,512]{1,0:T(8,128)(2,1)S(1)}, bf16[128,512]{1,0:T(8,128)(2,1)}, u32[]{:S(2)}) copy-start(bf16[128,512]{1,0:T(8,128)(2,1)} %copy-done.79) | copy-start | bytes 393220
  1885.9 413.1 %copy-start.86 = (bf16[1,128,512]{2,1,0:T(8,128)(2,1)S(1)}, bf16[1,128,512]{2,1,0:T(8,128)(2,1)}, u32[]{:S(2)}) copy-start(bf16[1,128,512]{2,1,0:T(8,128)(2,1)} %get-tuple-element.2194) | copy-start | bytes 393220
  (135 other events, 3182.0 us)
Sparse Core Ops, SparseCore 0:
  30.5 50.2 all-gather.10
  83.4 47.0 all-gather.16
  175.4 79.6 reduce-scatter.15
  275.2 47.5 all-gather.12
  324.8 47.0 all-gather.18
  417.3 80.3 reduce-scatter.17
  518.7 47.5 all-gather.14
  568.4 47.0 all-gather.20
  703.6 279.4 reduce-scatter.23
  986.6 73.7 reduce-scatter.25
  1062.7 20.4 reduce-scatter.21
  1085.5 21.1 reduce-scatter.27
  1184.4 206.2 reduce-scatter.31
  1394.2 73.8 reduce-scatter.33
  1470.3 20.4 reduce-scatter.29
  1493.1 21.1 reduce-scatter.35
  1592.9 206.2 reduce-scatter.39
  1802.7 73.6 reduce-scatter.41
  1879.3 20.4 reduce-scatter.19
  1902.7 21.0 reduce-scatter.37
  1926.7 21.1 reduce-scatter.43
  1952.9 111.1 all-reduce.16
where the time goes:
time: 2330 us; the launch traced here: 2310 us
  waiting for transfers between devices  1240 us (53%)
  blocking collectives  508 us (22%)
  local copies, waits for them, and re-layouts  202 us (9%)
  loops' own time  196 us (8%)
  matrix products  83.2 us (4%)
  other arithmetic  57.8 us (2%)
    reduce_scatter x3, waiting for transfers between devices, layer_backward(): lax.psum_scatter(key_grads.reshape(total_rows, -1).astype(jnp.bfloat16),...  630 us
    psum x1, blocking collectives, local(): small_total = lax.psum(small_total, ('ctx', 'tp'))  347 us
    reduce_scatter x3, waiting for transfers between devices, layer_backward(): lax.psum_scatter(value_grads.reshape(total_rows, -1).astype(jnp.bfloat16)...  225 us
    reduce_scatter x3, waiting for transfers between devices, layer_forward(): lax.psum_scatter((left + right).astype(jnp.bfloat16), 'tp', scatter_dimen...  174 us
    all_gather x3, waiting for transfers between devices, layer_forward(): lax.all_gather(keys.reshape(width, -1), 'ctx', axis=0, tiled=True)  94.7 us
    slice x144, local copies, waits for them, and re-layouts, block_needed(): query_place[-1]  85.1 us
    slice x144, local copies, waits for them, and re-layouts, block_needed(): query_start[0]  75.1 us
    another operation x3, loops' own time, attend(): lax.fori_loop(0, blocks, collect_stats, (start_top, jnp.zeros((heads, cou...  65.7 us
  transfers between devices with their start and end apart: 26, of which 24 were waited for; matrix products, arithmetic and copies ran while one was open for 6% of the time, Pallas kernels for 0%

commit v1 on v0

v1 whole, which is shorter than its diff:
```python
from functools import partial

import jax
import jax.numpy as jnp
from jax import lax
from jax.experimental import pallas as pl
from jax.experimental.pallas import tpu as pltpu
from jax.sharding import PartitionSpec as P

HEAD_DIM = 64
ROT = 16
MESH = pl.DeviceIdType.MESH
F32 = jnp.float32
BF16 = jnp.bfloat16
VMEM_LIMIT = 56 * 1024 * 1024
NCTX = 16
NTP = 4
BLK = 512
OWN = 128
MASKED = -1e30
LOWEST = -1e29


def dot_nn(a, b):
    return lax.dot_general(a, b, (((1,), (0,)), ((), ())), preferred_element_type=F32)


def dot_nt(a, b):
    return lax.dot_general(a, b, (((1,), (1,)), ((), ())), preferred_element_type=F32)


def dot_tn(a, b):
    return lax.dot_general(a, b, (((0,), (0,)), ((), ())), preferred_element_type=F32)


def phi(v):
    return 0.5 * (1.0 + lax.erf(v * (0.5**0.5)))


def gelu(v):
    return v * phi(v)


def gelu_slope(v):
    return phi(v) + v * jnp.exp(-0.5 * v * v) * 0.3989422804014327


def normed(rows):
    centre = rows - jnp.mean(rows, axis=-1, keepdims=True)
    spread = jnp.mean(centre * centre, axis=-1, keepdims=True)
    inverse = lax.rsqrt(spread + 1e-05)
    return centre * inverse, inverse


def greet(peers):
    barrier = pltpu.get_barrier_semaphore()
    for peer in peers:
        pl.semaphore_signal(barrier, inc=1, device_id=peer, device_id_type=MESH)
    pl.semaphore_wait(barrier, len(peers))


def ctx_peers(c):
    return [{"ctx": lax.rem(c + r, NCTX)} for r in range(1, NCTX)]


def tp_peers(t):
    return [{"tp": lax.rem(t + r, NTP)} for r in range(1, NTP)]


def remote(src, dst, send, recv, peer):
    return pltpu.make_async_remote_copy(
        src_ref=src, dst_ref=dst, send_sem=send, recv_sem=recv, device_id=peer, device_id_type=MESH
    )


def lanes(shape):
    return lax.broadcasted_iota(jnp.int32, shape, 1)


def turn(tile, table, sign):
    back = pltpu.roll(tile, tile.shape[1] - 8, 1)
    ahead = pltpu.roll(tile, 8, 1)
    return tile * table[0] + (back * table[1] + ahead * table[2]) * sign


def turn_left(tile, table, sign):
    back = pltpu.roll(tile, tile.shape[1] - 8, 1)
    ahead = pltpu.roll(tile, 8, 1)
    left = lanes(tile.shape) < HEAD_DIM
    return jnp.where(left, tile * table[0] + (back * table[1] + ahead * table[2]) * sign, tile)


def my_head(tile, group, place):
    swapped = pltpu.roll(tile, HEAD_DIM, 1)
    chosen = jnp.where(group == place, tile, swapped)
    half = lanes(tile.shape) // HEAD_DIM
    return jnp.where(half == place, chosen, 0.0)


def top_block(d):
    return jnp.maximum(d, NCTX - 1 - d)


def key_mask(key_block, first, shape, place_ref, slot, columns):
    key = key_block * BLK + first + lax.broadcasted_iota(jnp.int32, shape, 0)
    return (key <= place_ref[slot, 0:1, columns]) & (key >= place_ref[slot, 1:2, columns])


def needs_mask(key_block, query_block):
    return (key_block == 0) | (key_block == query_block) | (query_block == NCTX - 1)


def forward_kernel(
    x_ref,
    watt,
    batt,
    wo,
    wup,
    bup,
    wdn,
    bbr,
    gains,
    biases,
    rot,
    place,
    out_ref,
    xg,
    qpad,
    kvall,
    ot,
    lse,
    att,
    hid,
    kvs,
    qs,
    qin,
    kvt,
    acc,
    top,
    oout,
    oin,
    ffo,
    br,
    rsin,
    xsend,
    xrecv,
    kvsend,
    kvrecv,
    psend,
    precv,
    rsend,
    rrecv,
):
    c = lax.axis_index("ctx")
    t = lax.axis_index("tp")
    group = c // (NCTX // 2)
    partner = NCTX - 1 - c
    greet(tp_peers(t) + ctx_peers(c))

    gathers = [
        remote(x_ref, xg.at[t], xsend.at[r], xrecv.at[r], peer)
        for r, peer in enumerate(tp_peers(t))
    ]
    for copy in gathers:
        copy.start()
    xg[t] = x_ref[...]

    def project(part):
        xhat, _ = normed(xg[part].astype(F32))
        attention_in = (xhat * gains[0:1] + biases[0:1]).astype(BF16)
        pre = dot_nn(attention_in, watt[...]) + batt[...]
        rows = pl.ds(pl.multiple_of(part * OWN, OWN), OWN)
        table = [rot[0, j, rows, :] for j in range(3)]
        qs[rows, :] = (turn(pre[:, 0:128], table, 1.0) * 0.125).astype(BF16)
        kvs[0, rows, :] = turn_left(pre[:, 128:256], table, 1.0).astype(BF16)
        kvs[1, rows, :] = turn_left(pre[:, 256:384], table, 1.0).astype(BF16)

    project(t)
    for r, copy in enumerate(gathers):
        copy.wait_recv()
        project(lax.rem(t + NTP - 1 - r, NTP))

    query_copy = remote(qs, qin, psend.at[0], precv.at[0], {"ctx": partner})
    query_copy.start()

    def key_copy(r):
        d = lax.rem(c + r, NCTX)
        return c <= top_block(d), remote(
            kvs.at[d // (NCTX // 2)], kvall.at[c], kvsend.at[d], kvrecv.at[c], {"ctx": d}
        )

    @pl.loop(1, NCTX)
    def _(r):
        wanted, copy = key_copy(r)

        @pl.when(wanted)
        def _():
            copy.start()

    kvall[c] = kvs[group]

    @pl.loop(0, NTP)
    def _(part):
        xhat, _ = normed(xg[part].astype(F32))
        feed_in = (xhat * gains[1:2] + biases[1:2]).astype(BF16)
        hidden = gelu(dot_nn(feed_in, wup[...]) + bup[...]).astype(BF16)
        hid[part] = hidden
        ffo[part] = dot_nn(hidden, wdn[...])

    qpad[0] = my_head(qs[...].astype(F32), group, 0).astype(BF16)
    query_copy.wait_recv()
    qpad[1] = my_head(qin[...].astype(F32), group, 0).astype(BF16)
    acc[...] = jnp.zeros_like(acc)
    top[...] = jnp.full_like(top, LOWEST)

    def visit(key_block, slot, masked):
        scores = dot_nt(kvall[key_block], qpad[slot])
        if masked:
            allowed = key_mask(key_block, 0, scores.shape, place, slot, slice(None))
            scores = jnp.where(allowed, scores, MASKED)
        old = top[slot]
        new = jnp.maximum(old, jnp.max(scores, axis=0, keepdims=True))
        weights = jnp.exp(scores - new).astype(BF16)
        top[slot] = new
        acc[slot] = acc[slot] * jnp.exp(old - new) + dot_nn(kvt[...], weights)

    @pl.loop(0, NCTX)
    def _(r):
        key_block = lax.rem(c + NCTX - r, NCTX)

        @pl.when(key_block <= top_block(c))
        def _():
            @pl.when(r > 0)
            def _():
                remote(
                    kvs.at[0],
                    kvall.at[key_block],
                    kvsend.at[0],
                    kvrecv.at[key_block],
                    {"ctx": partner},
                ).wait_recv()

            turned = kvall[key_block].astype(F32).T
            row = lax.broadcasted_iota(jnp.int32, turned.shape, 0)
            kvt[...] = jnp.where(row < HEAD_DIM, 1.0, turned).astype(BF16)

            @pl.loop(0, 2)
            def _(slot):
                query_block = jnp.where(slot == 0, c, partner)
                reached = key_block <= query_block
                edge = needs_mask(key_block, query_block)

                @pl.when(reached & edge)
                def _():
                    visit(key_block, slot, True)

                @pl.when(reached & jnp.logical_not(edge))
                def _():
                    visit(key_block, slot, False)

    def finish(slot):
        total = acc[slot, 0:HEAD_DIM, :]
        mean = acc[slot, HEAD_DIM:, :] / total
        ot[slot] = mean
        lse[slot] = top[slot] + jnp.log(total[0:1])
        blank = jnp.zeros_like(mean)
        first = jnp.where(group == 0, mean, blank)
        second = jnp.where(group == 0, blank, mean)
        return jnp.concatenate([first, second], axis=0).T.astype(BF16)

    oout[...] = finish(1)
    out_copy = remote(oout, oin, psend.at[1], precv.at[1], {"ctx": partner})
    out_copy.start()
    own_out = finish(0)
    out_copy.wait_recv()
    att[...] = own_out + oin[...]

    def branch(part):
        rows = pl.ds(pl.multiple_of(part * OWN, OWN), OWN)
        return dot_nn(att[rows, :], wo[...]) + ffo[part]

    scatters = []
    for r in range(1, NTP):
        d = lax.rem(t + r, NTP)
        br[r - 1] = branch(d).astype(BF16)
        copy = remote(br.at[r - 1], rsin.at[r - 1], rsend.at[r - 1], rrecv.at[r - 1], {"tp": d})
        copy.start()
        scatters.append(copy)
    result = x_ref[...].astype(F32) + bbr[...] + branch(t)
    for r, copy in enumerate(scatters):
        copy.wait_recv()
        result = result + rsin[r].astype(F32)
    out_ref[...] = result.astype(BF16)

    for copy in gathers + scatters + [query_copy, out_copy]:
        copy.wait_send()

    @pl.loop(1, NCTX)
    def _(r):
        wanted, copy = key_copy(r)

        @pl.when(wanted)
        def _():
            copy.wait_send()


def whole(count):
    return [pl.BlockSpec(memory_space=pltpu.VMEM)] * count


def dma(*shape):
    return pltpu.SemaphoreType.DMA(shape)


def layer_forward(layer, x, weights, rot, place):
    d = x.shape[1]
    shapes = [
        ((OWN, d), BF16),
        ((NTP, OWN, d), BF16),
        ((2, BLK, 128), BF16),
        ((NCTX, BLK, 128), BF16),
        ((2, HEAD_DIM, BLK), F32),
        ((2, 1, BLK), F32),
        ((BLK, 128), BF16),
        ((NTP, OWN, d), BF16),
    ]
    operands = (x, *weights, rot, place)
    return pl.pallas_call(
        forward_kernel,
        out_shape=[jax.ShapeDtypeStruct(s, k) for s, k in shapes],
        in_specs=whole(len(operands)),
        out_specs=whole(len(shapes)),
        scratch_shapes=[
            pltpu.VMEM((2, BLK, 128), BF16),
            pltpu.VMEM((BLK, 128), BF16),
            pltpu.VMEM((BLK, 128), BF16),
            pltpu.VMEM((128, BLK), BF16),
            pltpu.VMEM((2, 128, BLK), F32),
            pltpu.VMEM((2, 1, BLK), F32),
            pltpu.VMEM((BLK, 128), BF16),
            pltpu.VMEM((BLK, 128), BF16),
            pltpu.VMEM((NTP, OWN, d), F32),
            pltpu.VMEM((NTP - 1, OWN, d), BF16),
            pltpu.VMEM((NTP - 1, OWN, d), BF16),
            dma(3),
            dma(3),
            dma(NCTX),
            dma(NCTX),
            dma(2),
            dma(2),
            dma(3),
            dma(3),
        ],
        compiler_params=pltpu.CompilerParams(
            collective_id=1 + layer, has_side_effects=True, vmem_limit_bytes=VMEM_LIMIT
        ),
        name=f"layer_forward_{layer}",
    )(*operands)


def backward_kernel(
    g_ref,
    xg,
    qpad,
    kvall,
    ot,
    lse,
    att,
    hid,
    watt,
    wo,
    wup,
    bup,
    wdn,
    gains,
    biases,
    rot,
    place,
    out_ref,
    gw,
    gv,
    gg,
    dos,
    doin,
    dopad,
    delta,
    dqt,
    dkva,
    dkvo,
    dkvi,
    dqs,
    dqi,
    ain,
    fin,
    ugs,
    dxh,
    dproj,
    dxs,
    rsin,
    kvt,
    xsend,
    xrecv,
    kvsend,
    kvrecv,
    psend,
    precv,
    rsend,
    rrecv,
):
    c = lax.axis_index("ctx")
    t = lax.axis_index("tp")
    group = c // (NCTX // 2)
    partner = NCTX - 1 - c
    d_model = g_ref.shape[1]
    greet(tp_peers(t) + ctx_peers(c))

    gathers = [
        remote(g_ref, gg.at[t], xsend.at[r], xrecv.at[r], peer)
        for r, peer in enumerate(tp_peers(t))
    ]
    for copy in gathers:
        copy.start()
    gg[t] = g_ref[...]

    def attention_grad(part):
        rows = pl.ds(pl.multiple_of(part * OWN, OWN), OWN)
        dos[rows, :] = dot_nt(gg[part], wo[...]).astype(BF16)

    gv[...] = jnp.zeros_like(gv)
    gv[4:5, :] = jnp.sum(g_ref[...].astype(F32), axis=0, keepdims=True)
    attention_grad(t)
    for r, copy in enumerate(gathers):
        copy.wait_recv()
        attention_grad(lax.rem(t + NTP - 1 - r, NTP))
    grad_copy = remote(dos, doin, psend.at[0], precv.at[0], {"ctx": partner})
    grad_copy.start()

    @pl.loop(0, NTP)
    def _(part):
        xhat, _ = normed(xg[part].astype(F32))
        ain[part] = (xhat * gains[0:1] + biases[0:1]).astype(BF16)
        feed_in = (xhat * gains[1:2] + biases[1:2]).astype(BF16)
        fin[part] = feed_in
        up_pre = dot_nn(feed_in, wup[...]) + bup[...]
        up_grad = (dot_nt(gg[part], wdn[...]) * gelu_slope(up_pre)).astype(BF16)
        ugs[part] = up_grad
        gv[5:6, :] += jnp.sum(up_grad.astype(F32), axis=0, keepdims=True)
        feed_grad = dot_nt(up_grad, wup[...])
        gv[1:2, :] += jnp.sum(xhat * feed_grad, axis=0, keepdims=True)
        gv[3:4, :] += jnp.sum(feed_grad, axis=0, keepdims=True)
        dxh[part] = feed_grad * gains[1:2]

    full_grad = gg[...].reshape(BLK, d_model)
    gw[0:128, :] = dot_tn(att[...], full_grad).astype(BF16)
    gw[128:640, :] = dot_tn(fin[...].reshape(BLK, d_model), ugs[...].reshape(BLK, -1)).astype(BF16)
    gw[640:1152, :] = dot_tn(hid[...].reshape(BLK, -1), full_grad).astype(BF16)

    def prepare(slot, tile):
        padded = my_head(tile, group, 1)
        dopad[slot] = padded.astype(BF16)
        delta[slot] = jnp.sum(padded.T[HEAD_DIM:, :] * ot[slot], axis=0, keepdims=True)

    prepare(0, dos[...].astype(F32))
    grad_copy.wait_recv()
    prepare(1, doin[...].astype(F32))
    dqt[...] = jnp.zeros_like(dqt)

    def visit(key_block, slot, masked):
        keys = kvall[key_block]
        scores = dot_nt(keys, qpad[slot])
        weights = jnp.exp(scores - lse[slot])
        if masked:
            allowed = key_mask(key_block, 0, scores.shape, place, slot, slice(None))
            weights = jnp.where(allowed, weights, 0.0)
        weight_grad = dot_nt(keys, dopad[slot])
        score_grad = (weights * (weight_grad - delta[slot])).astype(BF16)
        dkva[...] += dot_nn(weights.astype(BF16), dopad[slot]) + dot_nn(score_grad, qpad[slot])
        dqt[slot] += dot_nn(kvt[...], score_grad)

    def key_copy(key_block):
        return remote(
            dkvo.at[key_block],
            dkvi.at[c],
            kvsend.at[key_block],
            kvrecv.at[c],
            {"ctx": key_block},
        )

    @pl.loop(1, NCTX + 1)
    def _(r):
        key_block = lax.rem(c + r, NCTX)

        @pl.when(key_block <= top_block(c))
        def _():
            kvt[...] = kvall[key_block].astype(F32).T.astype(BF16)
            dkva[...] = jnp.zeros_like(dkva)

            @pl.loop(0, 2)
            def _(slot):
                query_block = jnp.where(slot == 0, c, partner)
                reached = key_block <= query_block
                edge = needs_mask(key_block, query_block)

                @pl.when(reached & edge)
                def _():
                    visit(key_block, slot, True)

                @pl.when(reached & jnp.logical_not(edge))
                def _():
                    visit(key_block, slot, False)

            dkvo[key_block] = dkva[...].astype(BF16)

            @pl.when(r < NCTX)
            def _():
                key_copy(key_block).start()

    def query_grad(slot):
        mean = dqt[slot, 0:HEAD_DIM, :] * 0.125
        blank = jnp.zeros_like(mean)
        first = jnp.where(group == 0, mean, blank)
        second = jnp.where(group == 0, blank, mean)
        tile = jnp.concatenate([first, second], axis=0).T
        return turn(tile, [rot[slot, j] for j in range(3)], -1.0).astype(BF16)

    dqs[...] = query_grad(1)
    query_copy = remote(dqs, dqi, psend.at[1], precv.at[1], {"ctx": partner})
    query_copy.start()
    own_query = query_grad(0)
    table = [rot[0, j] for j in range(3)]

    def key_grad(half):
        dkva[...] = jnp.zeros_like(dkva)

        @pl.loop(0, NCTX // 2)
        def _(step):
            source = half * (NCTX // 2) + step

            @pl.when(source == c)
            def _():
                dkva[...] += dkvo[c].astype(F32)

            @pl.when((c <= top_block(source)) & (source != c))
            def _():
                remote(
                    dkvo.at[0], dkvi.at[source], kvsend.at[0], kvrecv.at[source], {"ctx": partner}
                ).wait_recv()
                dkva[...] += dkvi[source].astype(F32)

        return turn_left(dkva[...], table, -1.0).astype(BF16)

    dproj[:, 128:256] = key_grad(0)
    dproj[:, 256:384] = key_grad(1)
    query_copy.wait_recv()
    dproj[:, 0:128] = own_query + dqi[...]
    gv[6:7, 0:384] = jnp.sum(dproj[...].astype(F32), axis=0, keepdims=True)

    def input_part(part):
        rows = pl.ds(pl.multiple_of(part * OWN, OWN), OWN)
        xhat, _ = normed(xg[part].astype(F32))
        grad = dot_nt(dproj[rows, :], watt[...])
        gv[0:1, :] += jnp.sum(xhat * grad, axis=0, keepdims=True)
        gv[2:3, :] += jnp.sum(grad, axis=0, keepdims=True)
        return dxh[part] + grad * gains[0:1]

    scatters = []
    for r in range(1, NTP):
        d = lax.rem(t + r, NTP)
        dxs[r - 1] = input_part(d).astype(BF16)
        copy = remote(dxs.at[r - 1], rsin.at[r - 1], rsend.at[r - 1], rrecv.at[r - 1], {"tp": d})
        copy.start()
        scatters.append(copy)
    total = input_part(t)
    gw[1152:1536, :] = dot_tn(dproj[...], ain[...].reshape(BLK, d_model)).astype(BF16)
    for r, copy in enumerate(scatters):
        copy.wait_recv()
        total = total + rsin[r].astype(F32)
    xhat, inverse = normed(xg[t].astype(F32))
    along = jnp.mean(total * xhat, axis=-1, keepdims=True)
    rows_grad = (total - jnp.mean(total, axis=-1, keepdims=True) - xhat * along) * inverse
    out_ref[...] = (g_ref[...].astype(F32) + rows_grad).astype(BF16)

    for copy in gathers + scatters + [grad_copy, query_copy]:
        copy.wait_send()

    @pl.loop(1, NCTX)
    def _(r):
        key_block = lax.rem(c + r, NCTX)

        @pl.when(key_block <= top_block(c))
        def _():
            key_copy(key_block).wait_send()


def layer_backward(layer, g, saved, weights, rot, place):
    d = g.shape[1]
    shapes = [((OWN, d), BF16), ((1536, d), BF16), ((8, d), F32)]
    watt, batt, wo, wup, bup, wdn, bbr, gains, biases = weights
    operands = (g, *saved, watt, wo, wup, bup, wdn, gains, biases, rot, place)
    return pl.pallas_call(
        backward_kernel,
        out_shape=[jax.ShapeDtypeStruct(s, k) for s, k in shapes],
        in_specs=whole(len(operands)),
        out_specs=whole(len(shapes)),
        scratch_shapes=[
            pltpu.VMEM((NTP, OWN, d), BF16),
            pltpu.VMEM((BLK, 128), BF16),
            pltpu.VMEM((BLK, 128), BF16),
            pltpu.VMEM((2, BLK, 128), BF16),
            pltpu.VMEM((2, 1, BLK), F32),
            pltpu.VMEM((2, 128, BLK), F32),
            pltpu.VMEM((BLK, 128), F32),
            pltpu.VMEM((NCTX, BLK, 128), BF16),
            pltpu.VMEM((NCTX, BLK, 128), BF16),
            pltpu.VMEM((BLK, 128), BF16),
            pltpu.VMEM((BLK, 128), BF16),
            pltpu.VMEM((NTP, OWN, d), BF16),
            pltpu.VMEM((NTP, OWN, d), BF16),
            pltpu.VMEM((NTP, OWN, d), BF16),
            pltpu.VMEM((NTP, OWN, d), F32),
            pltpu.VMEM((BLK, 384), BF16),
            pltpu.VMEM((NTP - 1, OWN, d), BF16),
            pltpu.VMEM((NTP - 1, OWN, d), BF16),
            pltpu.VMEM((128, BLK), BF16),
            dma(3),
            dma(3),
            dma(NCTX),
            dma(NCTX),
            dma(2),
            dma(2),
            dma(3),
            dma(3),
        ],
        compiler_params=pltpu.CompilerParams(
            collective_id=3 + layer, has_side_effects=True, vmem_limit_bytes=VMEM_LIMIT
        ),
        name=f"layer_backward_{layer}",
    )(*operands)


def swap_kernel(count, *refs):
    sources = refs[:count]
    results = refs[count : 2 * count]
    send, recv = refs[2 * count :]
    other = {"section": 1 - lax.axis_index("section")}
    greet([other])
    copies = [
        remote(source, result, send.at[i], recv.at[i], other)
        for i, (source, result) in enumerate(zip(sources, results))
    ]
    for copy in copies:
        copy.start()
    for copy in copies:
        copy.wait()


def swap(arrays):
    count = len(arrays)
    return pl.pallas_call(
        partial(swap_kernel, count),
        out_shape=[jax.ShapeDtypeStruct(a.shape, a.dtype) for a in arrays],
        in_specs=[pl.BlockSpec(memory_space=pl.ANY)] * count,
        out_specs=[pl.BlockSpec(memory_space=pl.ANY)] * count,
        scratch_shapes=[dma(count), dma(count)],
        compiler_params=pltpu.CompilerParams(collective_id=0, has_side_effects=True),
        name="swap_weights",
    )(*arrays)


def reduce_kernel(
    gw0,
    gw1,
    gv0,
    gv1,
    rows0,
    rows1,
    wide,
    small,
    rows_out,
    other_w,
    sums,
    chunk_in,
    mine,
    gathered,
    other_v,
    vec,
    vec_in,
    vec_tp,
    vec_tp_in,
    csend,
    crecv,
    ssend,
    srecv,
    asend,
    arecv,
    vsend,
    vrecv,
    tsend,
    trecv,
):
    s = lax.axis_index("section")
    c = lax.axis_index("ctx")
    t = lax.axis_index("tp")
    other = {"section": 1 - s}
    greet([other] + tp_peers(t) + ctx_peers(c))
    chunk = sums.shape[1]

    def cross(sources, results):
        return [
            remote(source, result, csend.at[i], crecv.at[i], other)
            for i, (source, result) in enumerate(zip(sources, results))
        ]

    results = (other_w, other_v, rows_out.at[s])

    @pl.when(s == 0)
    def _():
        for copy in cross((gw1, gv1, rows1), results):
            copy.start()
        rows_out[0] = rows0[...]

    @pl.when(s == 1)
    def _():
        for copy in cross((gw0, gv0, rows0), results):
            copy.start()
        rows_out[1] = rows1[...]

    crosses = cross((gw0, gv0, rows0), results)
    crosses[1].wait_recv()
    vec[...] = jnp.where(s == 0, gv0[...], gv1[...]) + other_v[...]

    def vec_copy(r):
        d = lax.rem(c + r, NCTX)
        return remote(vec, vec_in.at[r], vsend.at[r], vrecv.at[r], {"ctx": d})

    @pl.loop(1, NCTX)
    def _(r):
        vec_copy(r).start()

    crosses[0].wait_recv()

    @pl.loop(0, NCTX)
    def _(j):
        rows = pl.ds(pl.multiple_of(j * chunk, chunk), chunk)
        mine_part = jnp.where(s == 0, gw0[rows, :].astype(F32), gw1[rows, :].astype(F32))
        sums[j] = (mine_part + other_w[rows, :].astype(F32)).astype(BF16)

    def scatter(r):
        d = lax.rem(c + r, NCTX)
        return remote(sums.at[d], chunk_in.at[r], ssend.at[r], srecv.at[r], {"ctx": d})

    @pl.loop(1, NCTX)
    def _(r):
        scatter(r).start()

    total_vec = vec[...]
    for r in range(1, NCTX):
        vec_copy(r).wait_recv()
        total_vec = total_vec + vec_in[r]
    vec_tp[...] = total_vec
    tp_copies = [
        remote(vec_tp, vec_tp_in.at[r], tsend.at[r], trecv.at[r], peer)
        for r, peer in enumerate(tp_peers(t))
    ]
    for copy in tp_copies:
        copy.start()

    total = sums[c].astype(F32)
    for r in range(1, NCTX):
        scatter(r).wait_recv()
        total = total + chunk_in[r].astype(F32)
    mine[...] = total.astype(BF16)

    def gather(r):
        d = lax.rem(c + r, NCTX)
        return remote(mine, gathered.at[c], asend.at[r], arecv.at[r], {"ctx": d})

    @pl.loop(1, NCTX)
    def _(r):
        gather(r).start()

    rows = pl.ds(pl.multiple_of(c * chunk, chunk), chunk)
    wide[rows, :] = total
    shared = total_vec
    for r, copy in enumerate(tp_copies):
        copy.wait_recv()
        shared = shared + vec_tp_in[r]
    row = lax.broadcasted_iota(jnp.int32, shared.shape, 0)
    small[...] = jnp.where(row < 5, shared, total_vec)

    @pl.loop(1, NCTX)
    def _(r):
        source = lax.rem(c + NCTX - r, NCTX)
        remote(mine, gathered.at[source], asend.at[r], arecv.at[r], other).wait_recv()
        rows = pl.ds(pl.multiple_of(source * chunk, chunk), chunk)
        wide[rows, :] = gathered[source].astype(F32)

    crosses[2].wait_recv()
    for copy in tp_copies + crosses:
        copy.wait_send()

    @pl.loop(1, NCTX)
    def _(r):
        vec_copy(r).wait_send()
        scatter(r).wait_send()
        gather(r).wait_send()


def reduce_gradients(gw, gv, rows):
    total, d = gw[0].shape
    chunk = total // NCTX
    operands = (*gw, *gv, *rows)
    shapes = [((total, d), F32), ((8, d), F32), ((2, *rows[0].shape), BF16)]
    return pl.pallas_call(
        reduce_kernel,
        out_shape=[jax.ShapeDtypeStruct(s, k) for s, k in shapes],
        in_specs=whole(len(operands)),
        out_specs=whole(len(shapes)),
        scratch_shapes=[
            pltpu.VMEM((total, d), BF16),
            pltpu.VMEM((NCTX, chunk, d), BF16),
            pltpu.VMEM((NCTX, chunk, d), BF16),
            pltpu.VMEM((chunk, d), BF16),
            pltpu.VMEM((NCTX, chunk, d), BF16),
            pltpu.VMEM((8, d), F32),
            pltpu.VMEM((8, d), F32),
            pltpu.VMEM((NCTX, 8, d), F32),
            pltpu.VMEM((8, d), F32),
            pltpu.VMEM((NTP - 1, 8, d), F32),
            dma(3),
            dma(3),
            dma(NCTX),
            dma(NCTX),
            dma(NCTX),
            dma(NCTX),
            dma(NCTX),
            dma(NCTX),
            dma(3),
            dma(3),
        ],
        compiler_params=pltpu.CompilerParams(
            collective_id=5, has_side_effects=True, vmem_limit_bytes=VMEM_LIMIT
        ),
        name="reduce_gradients",
    )(*operands)


def sequence_starts(lengths, positions):
    ends = jnp.cumsum(lengths).astype(jnp.int32)
    before = jnp.where(ends[None, :] <= positions[:, None], lengths[None, :], 0)
    return jnp.sum(before, axis=1).astype(jnp.int32)


def rotary_lanes(offsets):
    rates = 1.0 / 10000.0 ** (jnp.arange(0, ROT, 2).astype(F32) / ROT)
    angles = offsets.astype(F32)[:, None] * rates[None, :]
    cosine, sine = jnp.cos(angles), jnp.sin(angles)
    zeros = jnp.zeros_like(sine)
    rest = jnp.zeros((offsets.shape[0], HEAD_DIM - ROT), F32)
    tables = (
        jnp.concatenate([cosine, cosine, rest + 1.0], axis=1),
        jnp.concatenate([-sine, zeros, rest], axis=1),
        jnp.concatenate([zeros, sine, rest], axis=1),
    )
    return jnp.stack([jnp.concatenate([table, table], axis=1) for table in tables])


def pack_attention(items):
    q, k, v = items
    half = HEAD_DIM
    return jnp.concatenate([q, k[:, :half], v[:, :half], k[:, half:], v[:, half:]], axis=1)


def local(
    block_input,
    output_grad,
    sequence_lengths,
    norm_gain,
    norm_bias,
    attention_weight,
    attention_bias,
    output_weight,
    up_weight,
    up_bias,
    down_weight,
    branch_bias,
):
    s = lax.axis_index("section")
    c = lax.axis_index("ctx")
    own = (
        pack_attention([attention_weight[0, k] for k in range(3)]),
        pack_attention([attention_bias[:, k] for k in range(3)]),
        output_weight[0],
        up_weight[0],
        up_bias,
        down_weight[0],
        branch_bias,
        norm_gain[0],
        norm_bias[0],
    )
    received = swap(own)
    first = [jnp.where(s == 0, a, b) for a, b in zip(own, received)]
    second = [jnp.where(s == 0, b, a) for a, b in zip(own, received)]

    x = lax.dynamic_index_in_dim(block_input, s, 0, keepdims=False)
    g = lax.dynamic_index_in_dim(output_grad, s, 0, keepdims=False)
    lengths = lax.dynamic_index_in_dim(sequence_lengths, s, 0, keepdims=False)
    steps = jnp.arange(BLK, dtype=jnp.int32)
    positions = jnp.concatenate([c * BLK + steps, (NCTX - 1 - c) * BLK + steps])
    starts = sequence_starts(lengths, positions)
    rot = rotary_lanes(positions - starts)
    rot = jnp.stack([rot[:, :BLK], rot[:, BLK:]])
    place = jnp.stack([positions.reshape(2, BLK), starts.reshape(2, BLK)], axis=1)

    early, *kept_first = layer_forward(0, x, first, rot, place)
    late, *kept_second = layer_forward(1, early, second, rot, place)
    middle, gw1, gv1 = layer_backward(1, g, kept_second, second, rot, place)
    given, gw0, gv0 = layer_backward(0, middle, kept_first, first, rot, place)

    wide, small, rows = reduce_gradients(
        (gw0, gw1),
        (gv0, gv1),
        (jnp.concatenate([early, given], axis=0), jnp.concatenate([late, middle], axis=0)),
    )
    packed = wide[1152:1536]
    half = HEAD_DIM
    query = packed[0:128]
    key = jnp.concatenate([packed[128 : 128 + half], packed[256 : 256 + half]], axis=0)
    value = jnp.concatenate([packed[128 + half : 256], packed[256 + half :]], axis=0)
    bias = small[6, 0:384]
    bias_parts = jnp.stack(
        [
            bias[0:128],
            jnp.concatenate([bias[128 : 128 + half], bias[256 : 256 + half]]),
            jnp.concatenate([bias[128 + half : 256], bias[256 + half :]]),
        ]
    )
    return (
        rows[None, :, 0:OWN],
        rows[None, :, OWN:],
        small[None, 0:2],
        small[None, 2:4],
        jnp.stack([query.T, key.T, value.T])[None],
        bias_parts[None],
        wide[None, 0:128],
        wide[None, 128:640],
        small[5:6],
        wide[None, 640:1152],
        small[4:5],
    )


def solution(mesh):
    placed = (
        P(None, ("ctx", "tp"), None),
        P(None, ("ctx", "tp"), None),
        P(),
        P("section", None, None),
        P("section", None, None),
        P("section", None, None, "tp"),
        P("section", None, "tp"),
        P("section", "tp", None),
        P("section", None, "tp"),
        P("section", "tp"),
        P("section", "tp", None),
        P("section", None),
    )
    return jax.shard_map(
        local,
        mesh=mesh,
        in_specs=placed,
        out_specs=(
            P("section", None, ("ctx", "tp"), None),
            P("section", None, ("ctx", "tp"), None),
            P("section", None, None),
            P("section", None, None),
            P("section", None, None, "tp"),
            P("section", None, "tp"),
            P("section", "tp", None),
            P("section", None, "tp"),
            P("section", "tp"),
            P("section", "tp", None),
            P("section", None),
        ),
        check_vma=False,
    )
```

time: 2330 us -> 376 us (0.16)
  waiting for transfers between devices: 1240 us -> 0 us
  blocking collectives: 508 us -> 0 us
  Pallas kernels: 0 us -> 338 us
  loops' own time: 196 us -> 0 us
  local copies, waits for them, and re-layouts: 202 us -> 21.2 us
  matrix products: 83.2 us -> 0 us
  other arithmetic: 57.8 us -> 14.7 us
    reduce_scatter x15 -> x0, waiting for transfers between devices: 1120 us -> none  [the longest x3 630 us: layer_backward(): lax.psum_scatter(key_grads.reshape(total_rows, -1).astype(jnp.bfloat16),...]
    psum x2 -> x0, blocking collectives: 388 us -> none  [the longest x1 347 us: local(): small_total = lax.psum(small_total, ('ctx', 'tp'))]
    pallas_call x0 -> x6, Pallas kernels: none -> 338 us  [the longest x2 142 us: layer_backward(): pl.pallas_call(backward_kernel, out_shape=[jax.ShapeDtypeStruct(s, k) for...]
    another operation x153 -> x0, loops' own time: 196 us -> none  [the longest x3 65.7 us: attend(): lax.fori_loop(0, blocks, collect_stats, (start_top, jnp.zeros((heads, cou...]
    slice x308 -> x6, local copies, waits for them, and re-layouts: 169 us -> 4.23 us  [the longest x1 1.38 us: local(): small[4:5]]
    all_gather x9 -> x0, blocking collectives: 119 us -> none  [the longest x3 40.3 us: layer_forward(): lax.all_gather(attention_in.astype(jnp.bfloat16), 'tp', axis=0, tiled=True)]
    all_gather x6 -> x0, waiting for transfers between devices: 117 us -> none  [the longest x3 94.7 us: layer_forward(): lax.all_gather(keys.reshape(width, -1), 'ctx', axis=0, tiled=True)]
    dot_general x47 -> x0, matrix products: 82 us -> none  [the longest x3 15.7 us: layer_forward(): jnp.dot(feed_in, up_weight, preferred_element_type=jnp.float32) + up_bias]
  transfers between devices with their start and end apart: 26 -> 0, of which waited for: 24 -> 0; matrix products, arithmetic and copies ran while one was open for 6% -> 0% of each run, Pallas kernels for 0% -> 0%
where the time goes in v1:
time: 376 us; the launch traced here: 374 us
  Pallas kernels  338 us (90%)
  local copies, waits for them, and re-layouts  21.2 us (6%)
  other arithmetic  14.7 us (4%)
    pallas_call x2, Pallas kernels, layer_backward(): pl.pallas_call(backward_kernel, out_shape=[jax.ShapeDtypeStruct(s, k) for...  142 us
    pallas_call x2, Pallas kernels, layer_forward(): pl.pallas_call(forward_kernel, out_shape=[jax.ShapeDtypeStruct(s, k) for...  130 us
    pallas_call x1, Pallas kernels, reduce_gradients(): pl.pallas_call(reduce_kernel, out_shape=[jax.ShapeDtypeStruct(s, k) for s...  61.4 us
    select_n x9, other arithmetic, local(): second = [jnp.where(s == 0, b, a) for a, b in zip(own, received)]  7.88 us

profile of v1, /device:TPU:0, one launch (start us, length us, event | category | flops | bytes accessed | tf_op | source)
XLA Modules:
  0.0 374.4 jit_solution(917948304165130927)
XLA Ops:
  0.7 0.7 fusion.2
  1.4 0.2 reduce-window.8
  1.5 0.7 slice_bitcast_fusion.17
  2.2 0.1 fusion.7
  2.3 0.7 concatenate.50.refs_1_
  3.0 0.1 select_reduce_fusion
  3.1 0.6 pad_add_fusion.place
  3.7 1.7 dynamic-slice_bitcast_fusion
  5.4 1.1 slice_bitcast_fusion.8
  6.4 0.1 fusion.4
  6.6 1.0 concatenate.49.refs_0_
  7.6 1.9 multiply_cosine_fusion
  9.5 1.3 concatenate.52
  10.9 1.1 concatenate.53
  12.0 1.1 concatenate.54
  13.2 0.1 pad_maximum_fusion
  13.3 0.1 slice_bitcast_fusion.3
  13.4 1.3 pad_maximum_fusion.1.rot
  14.7 0.0 copy-start.11
  14.7 0.0 copy-start.12
  14.7 0.0 copy-start.7
  14.7 0.0 copy-start.2
  14.8 4.0 %swap_weights.1 = (bf16[512,384]{1,0:T(8,128)(2,1)}, f32[1,384]{1,0:T(1,128)}, bf16[128,512]{1,0:T(8,128)(2,1)}, bf16[512,512]{1,0:T(8,128)(2,1)}, f32[1,512]{1,...) custom-call(bf16[512,384]{1,0:T(8,128)(2,1)} %concatenate.49.refs_0_, ...), custom_call_target="tpu_custom_call" | custom-call | tf_op jit(solution)/shard_map/swap_weights/pallas_call | solution.py:659
  18.8 0.0 copy-start.20
  18.8 0.0 copy-start.19
  18.8 0.0 copy-start.18
  18.8 0.0 copy-start.17
  18.8 0.0 copy-start.16
  18.8 0.0 copy-start.9
  18.8 0.0 copy-start.6
  18.9 0.0 copy-done
  18.9 2.1 broadcast_select_fusion.4
  21.0 0.6 broadcast_select_fusion.16
  21.6 0.6 broadcast_select_fusion.13
  22.2 0.0 copy-done.18
  22.2 0.6 broadcast_select_fusion.12
  22.8 0.6 broadcast_select_fusion.9
  23.4 0.6 broadcast_select_fusion.8
  24.0 0.0 copy-done.7
  24.0 0.7 broadcast_select_fusion.6
  24.7 1.0 broadcast_select_fusion.1
  25.8 0.0 copy-done.3
  25.8 1.0 broadcast_select_fusion
  26.8 66.9 %layer_forward_0.1 = (bf16[128,512]{1,0:T(8,128)(2,1)}, bf16[4,128,512]{2,1,0:T(8,128)(2,1)}, bf16[2,512,128]{2,1,0:T(8,128)(2,1)}, bf16[16,512,128]{2,1,0:T(8,1...) custom-call(bf16[128,512]{1,0:T(8,128)(2,1)} %get-tuple-element.171., ...), custom_call_target="tpu_custom_call" | custom-call | tf_op jit(solution)/shard_map/layer_forward_0/pallas_call | solution.py:328
  93.8 62.8 %layer_forward_1.1 = (bf16[128,512]{1,0:T(8,128)(2,1)}, bf16[4,128,512]{2,1,0:T(8,128)(2,1)}, bf16[2,512,128]{2,1,0:T(8,128)(2,1)}, bf16[16,512,128]{2,1,0:T(8,1...) custom-call(bf16[128,512]{1,0:T(8,128)(2,1)} %get-tuple-element.54.x, ...), custom_call_target="tpu_custom_call" | custom-call | tf_op jit(solution)/shard_map/layer_forward_1/pallas_call | solution.py:328
  156.6 74.4 %layer_backward_1.1 = (bf16[128,512]{1,0:T(8,128)(2,1)}, bf16[1536,512]{1,0:T(8,128)(2,1)}, f32[8,512]{1,0:T(8,128)}) custom-call(bf16[128,512]{1,0:T(8,128)(2,1)} %get-tuple-element.172.g_ref, bf16[4,128,512]{2,1,0:T(8,128)(2,1)} %get-tuple-element.55.xg, bf16[2,512,128]{2,1,0:T(8,128)(2,1)} %get-tuple-element.56.qpad, ...), custom_call_target="tpu_custom_call" | custom-call | tf_op jit(solution)/shard_map/layer_backward_1/pallas_call | solution.py:600
  231.0 67.9 %layer_backward_0.1 = (bf16[128,512]{1,0:T(8,128)(2,1)}, bf16[1536,512]{1,0:T(8,128)(2,1)}, f32[8,512]{1,0:T(8,128)}) custom-call(bf16[128,512]{1,0:T(8,128)(2,1)} %get-tuple-element.62.g_ref, bf16[4,128,512]{2,1,0:T(8,128)(2,1)} %get-tuple-element.63.xg, bf16[2,512,128]{2,1,0:T(8,128)(2,1)} %get-tuple-element.64.qpad, ...), custom_call_target="tpu_custom_call" | custom-call | tf_op jit(solution)/shard_map/layer_backward_0/pallas_call | solution.py:600
  299.0 1.6 pad_maximum_fusion.2.rows0
  300.6 0.0 copy-done.4
  300.6 0.7 pad_maximum_fusion.3.rows1
  301.3 61.4 %reduce_gradients.1 = (f32[1536,512]{1,0:T(8,128)}, f32[8,512]{1,0:T(8,128)}, bf16[2,256,512]{2,1,0:T(8,128)(2,1)}) custom-call(bf16[1536,512]{1,0:T(8,128)(2,1)} %get-tuple-element.70.gw0, bf16[1536,512]{1,0:T(8,128)(2,1)} %get-tuple-element.71.gw1, f32[8,512]{1,0:T(8,128)} %get-tuple-element.72.gv0, f32[8,512]{1,0:T(8,128)} %get-tuple-element.73.gv1, ...), custom_call_target="tpu_custom_call" | custom-call | tf_op jit(solution)/shard_map/reduce_gradients/pallas_call | solution.py:814
  362.7 2.0 slice_bitcast_fusion.6
  364.8 0.7 slice.155
  365.4 0.8 slice_bitcast_fusion.16
  366.3 0.1 maximum_bitcast_fusion.4
  366.3 0.1 maximum_bitcast_fusion.5
  366.4 0.6 copy.29
  367.0 1.4 fusion.6
  368.4 1.4 slice_bitcast_fusion.11
  369.8 1.1 fusion.3
  371.0 0.7 slice_bitcast_fusion.4
  371.7 1.5 slice_bitcast_fusion
  373.2 0.1 maximum_bitcast_fusion
  373.2 1.1 copy.28
  (37 shorter events, 0.2 us)
Async XLA Ops:
  14.7 4.2 %copy-start = (bf16[512,384]{1,0:T(8,128)(2,1)S(1)}, bf16[512,384]{1,0:T(8,128)(2,1)}, u32[]{:S(2)}) copy-start(bf16[512,384]{1,0:T(8,128)(2,1)} %concatenate.49.refs_0_) | copy-start | bytes 1179652
  14.7 6.3 %copy-start.13 = (f32[1,384]{1,0:T(1,128)S(1)}, f32[1,384]{1,0:T(1,128)}, u32[]{:S(2)}) copy-start(f32[1,384]{1,0:T(1,128)} %concatenate.50.refs_1_) | copy-start | bytes 4612
  14.7 6.9 %copy-start.14 = (f32[1,512]{1,0:T(1,128)S(1)}, f32[1,512]{1,0:T(1,128)}, u32[]{:S(2)}) copy-start(f32[1,512]{1,0:T(1,128)} %refs_4_.1) | copy-start | bytes 6148
  14.7 7.5 %copy-start.15 = (f32[1,512]{1,0:T(1,128)S(1)}, f32[1,512]{1,0:T(1,128)}, u32[]{:S(2)}) copy-start(f32[1,512]{1,0:T(1,128)} %refs_6_.1) | copy-start | bytes 6148
  14.7 8.1 %copy-start.11 = (f32[1,2,512]{2,1,0:T(2,128)S(1)}, f32[1,2,512]{2,1,0:T(2,128)}, u32[]{:S(2)}) copy-start(f32[1,2,512]{2,1,0:T(2,128)} %param.15) | copy-start | bytes 12292
  14.7 8.7 %copy-start.12 = (f32[1,2,512]{2,1,0:T(2,128)S(1)}, f32[1,2,512]{2,1,0:T(2,128)}, u32[]{:S(2)}) copy-start(f32[1,2,512]{2,1,0:T(2,128)} %param.16) | copy-start | bytes 12292
  14.7 9.3 %copy-start.7 = (bf16[1,128,512]{2,1,0:T(8,128)(2,1)S(1)}, bf16[1,128,512]{2,1,0:T(8,128)(2,1)}, u32[]{:S(2)}) copy-start(bf16[1,128,512]{2,1,0:T(8,128)(2,1)} %param.19) | copy-start | bytes 393220
  14.7 10.0 %copy-start.2 = (bf16[1,512,512]{2,1,0:T(8,128)(2,1)S(1)}, bf16[1,512,512]{2,1,0:T(8,128)(2,1)}, u32[]{:S(2)}) copy-start(bf16[1,512,512]{2,1,0:T(8,128)(2,1)} %param.20) | copy-start | bytes 1572868
  18.8 2.2 copy-start.20
  18.8 2.8 copy-start.19
  18.8 3.4 copy-start.18
  18.8 4.0 %copy-start.17 = (f32[2,512]{1,0:T(2,128)S(1)}, f32[2,512]{1,0:T(2,128)}, u32[]{:S(2)}) copy-start(f32[2,512]{1,0:T(2,128)} %get-tuple-element.52) | copy-start | bytes 12292
  18.8 4.6 %copy-start.16 = (f32[2,512]{1,0:T(2,128)S(1)}, f32[2,512]{1,0:T(2,128)}, u32[]{:S(2)}) copy-start(f32[2,512]{1,0:T(2,128)} %get-tuple-element.53) | copy-start | bytes 12292
  18.8 5.2 %copy-start.9 = (bf16[128,512]{1,0:T(8,128)(2,1)S(1)}, bf16[128,512]{1,0:T(8,128)(2,1)}, u32[]{:S(2)}) copy-start(bf16[128,512]{1,0:T(8,128)(2,1)} %get-tuple-element.47) | copy-start | bytes 393220
  18.8 5.9 %copy-start.6 = (bf16[512,512]{1,0:T(8,128)(2,1)S(1)}, bf16[512,512]{1,0:T(8,128)(2,1)}, u32[]{:S(2)}) copy-start(bf16[512,512]{1,0:T(8,128)(2,1)} %get-tuple-element.48) | copy-start | bytes 1572868
  21.0 4.8 %copy-start.3 = (bf16[1,512,512]{2,1,0:T(8,128)(2,1)S(1)}, bf16[1,512,512]{2,1,0:T(8,128)(2,1)}, u32[]{:S(2)}) copy-start(bf16[1,512,512]{2,1,0:T(8,128)(2,1)} %param.22) | copy-start | bytes 1572868
  21.0 4.8 %copy-start.5 = (bf16[512,512]{1,0:T(8,128)(2,1)S(1)}, bf16[512,512]{1,0:T(8,128)(2,1)}, u32[]{:S(2)}) copy-start(bf16[512,512]{1,0:T(8,128)(2,1)} %get-tuple-element.50) | copy-start | bytes 1572868
  231.0 68.0 %copy-start.8 = (bf16[128,512]{1,0:T(8,128)(2,1)S(1)}, bf16[128,512]{1,0:T(8,128)(2,1)}, u32[]{:S(2)}) copy-start(bf16[128,512]{1,0:T(8,128)(2,1)} %get-tuple-element.54.x_ref) | copy-start | bytes 393220
  231.0 69.6 %copy-start.4 = (bf16[128,512]{1,0:T(8,128)(2,1)S(1)}, bf16[128,512]{1,0:T(8,128)(2,1)}, u32[]{:S(2)}) copy-start(bf16[128,512]{1,0:T(8,128)(2,1)} %get-tuple-element.62.g_ref) | copy-start | bytes 393220
  231.0 69.6 %copy-start.10 = (bf16[128,512]{1,0:T(8,128)(2,1)S(1)}, bf16[128,512]{1,0:T(8,128)(2,1)}, u32[]{:S(2)}) copy-start(bf16[128,512]{1,0:T(8,128)(2,1)} %get-tuple-element.75) | copy-start | bytes 393220
  362.7 8.2 %copy-start.1 = (f32[1536,512]{1,0:T(8,128)S(1)}, f32[1536,512]{1,0:T(8,128)}, u32[]{:S(2)}) copy-start(f32[1536,512]{1,0:T(8,128)} %get-tuple-element.78) | copy-start | bytes 9437188

commit v2 on v0

v2 whole, which is shorter than its diff:
```python
from types import SimpleNamespace

import jax
import jax.numpy as jnp
from jax import lax
from jax.experimental import pallas as pl
from jax.experimental.pallas import tpu as pltpu
from jax.sharding import PartitionSpec as P

HEAD_DIM = 64
ROT = 16
MESH = pl.DeviceIdType.MESH
F32 = jnp.float32
BF16 = jnp.bfloat16
VMEM_LIMIT = 56 * 1024 * 1024
NCTX = 16
NTP = 4
BLK = 512
OWN = 128
D = 512
LANES = 128
MASKED = -1e30
LOWEST = -1e29


def dot_nn(a, b):
    return lax.dot_general(a, b, (((1,), (0,)), ((), ())), preferred_element_type=F32)


def dot_nt(a, b):
    return lax.dot_general(a, b, (((1,), (1,)), ((), ())), preferred_element_type=F32)


def dot_tn(a, b):
    return lax.dot_general(a, b, (((0,), (0,)), ((), ())), preferred_element_type=F32)


def phi(v):
    return 0.5 * (1.0 + lax.erf(v * (0.5**0.5)))


def gelu(v):
    return v * phi(v)


def gelu_slope(v):
    return phi(v) + v * jnp.exp(-0.5 * v * v) * 0.3989422804014327


def normed(rows):
    centre = rows - jnp.mean(rows, axis=-1, keepdims=True)
    spread = jnp.mean(centre * centre, axis=-1, keepdims=True)
    inverse = lax.rsqrt(spread + 1e-05)
    return centre * inverse, inverse


def remote(src, dst, send, recv, peer):
    return pltpu.make_async_remote_copy(
        src_ref=src, dst_ref=dst, send_sem=send, recv_sem=recv, device_id=peer, device_id_type=MESH
    )


def lanes(shape):
    return lax.broadcasted_iota(jnp.int32, shape, 1)


def turn(tile, cosine, sine):
    back = pltpu.roll(tile, LANES - 8, 1)
    ahead = pltpu.roll(tile, 8, 1)
    other = jnp.where(lanes(tile.shape) % HEAD_DIM < 8, back, ahead)
    return tile * cosine + other * sine


def turn_left(tile, cosine, sine):
    return jnp.where(lanes(tile.shape) < HEAD_DIM, turn(tile, cosine, sine), tile)


def my_head(tile, group, half):
    swapped = pltpu.roll(tile, HEAD_DIM, 1)
    chosen = jnp.where(group == half, tile, swapped)
    return jnp.where(lanes(tile.shape) // HEAD_DIM == half, chosen, 0.0)


def two_head_tile(rows, group):
    blank = jnp.zeros_like(rows)
    first = jnp.where(group == 0, rows, blank)
    second = jnp.where(group == 0, blank, rows)
    return jnp.concatenate([first, second], axis=0).T


def top_block(d):
    return jnp.maximum(d, NCTX - 1 - d)


def needs_mask(key_block, query_block):
    return (key_block == 0) | (key_block == query_block) | (query_block == NCTX - 1)


def span(index, size):
    return pl.ds(pl.multiple_of(index * size, size), size)


OUTPUTS = (
    ("out_rows", (2, OWN, D), BF16),
    ("out_grads", (2, OWN, D), BF16),
    ("out_ff", (2 * D, D), F32),
    ("out_wo", (OWN, D), F32),
    ("out_att", (3, D, OWN), F32),
    ("out_small", (8, D), F32),
)

SCRATCH = (
    ("watt", (2, D, 384), BF16),
    ("wo", (2, NTP, OWN, D), BF16),
    ("wup", (2, D, D), BF16),
    ("wdn", (2, D, D), BF16),
    ("vecs", (2, 8, D), F32),
    ("xown", (2, OWN, D), BF16),
    ("fo", (2, OWN, D), BF16),
    ("xg", (2, NTP, OWN, D), BF16),
    ("qpad", (2, 2, BLK, LANES), BF16),
    ("kvall", (2, NCTX, BLK, LANES), BF16),
    ("ot", (2, 2, HEAD_DIM, BLK), F32),
    ("lse", (2, 2, 1, BLK), F32),
    ("hid", (2, NTP, OWN, D), BF16),
    ("kvs", (2, 2, BLK, LANES), BF16),
    ("qs", (2, BLK, LANES), BF16),
    ("qin", (2, BLK, LANES), BF16),
    ("oout", (2, 2, BLK, LANES), BF16),
    ("oin", (2, BLK, LANES), BF16),
    ("oa", (2, NTP, OWN, LANES), BF16),
    ("ob", (2, NTP, OWN, LANES), BF16),
    ("ffs", (2, NTP - 1, OWN, D), BF16),
    ("ffr", (2, NTP - 1, OWN, D), BF16),
    ("gown", (2, OWN, D), BF16),
    ("go", (2, OWN, D), BF16),
    ("gg", (2, NTP, OWN, D), BF16),
    ("dos", (2, NTP, OWN, LANES), BF16),
    ("doa", (2, NTP, OWN, LANES), BF16),
    ("dob", (2, NTP, OWN, LANES), BF16),
    ("dkvo", (2, NCTX, BLK, LANES), BF16),
    ("dkvi", (2, NCTX, BLK, LANES), BF16),
    ("dqs", (2, BLK, LANES), BF16),
    ("dqi", (2, BLK, LANES), BF16),
    ("dxs", (2, NTP - 1, OWN, D), BF16),
    ("dxr", (2, NTP - 1, OWN, D), BF16),
    ("gwp", (2, 2 * D, D), BF16),
    ("gwq", (2, D, D), BF16),
    ("gv", (2, 8, D), F32),
    ("kvt", (LANES, BLK), BF16),
    ("acc", (2, LANES, BLK), F32),
    ("top", (2, 1, BLK), F32),
    ("ffo", (OWN, D), F32),
    ("dopad", (2, BLK, LANES), BF16),
    ("delta", (2, 1, BLK), F32),
    ("dqt", (2, LANES, BLK), F32),
    ("dkva", (BLK, LANES), F32),
    ("ain", (NTP, OWN, D), BF16),
    ("fin", (NTP, OWN, D), BF16),
    ("ugs", (NTP, OWN, D), BF16),
    ("dxh", (NTP, OWN, D), F32),
    ("dproj", (BLK, 384), BF16),
    ("crp", (2 * D, D), BF16),
    ("crq", (D, D), BF16),
    ("crv", (8, D), F32),
    ("sump", (NCTX, 64, D), BF16),
    ("sumq", (NCTX, 32, D), BF16),
    ("inp", (NCTX, 64, D), BF16),
    ("inq", (NCTX, 32, D), BF16),
    ("minep", (64, D), BF16),
    ("mineq", (32, D), BF16),
    ("gatp", (NCTX, 64, D), BF16),
    ("gatq", (NCTX, 32, D), BF16),
    ("allq", (D, D), F32),
    ("vec", (8, D), F32),
    ("vec_in", (NCTX, 8, D), F32),
    ("vec_tp", (8, D), F32),
    ("vec_tp_in", (NTP - 1, 8, D), F32),
)

INPUTS = ("xin", "gin", "own_watt", "own_wo", "own_wup", "own_wdn", "own_vecs", "rot", "place")

SEMAPHORES = {}
COPIES = 0
for name, count in (
    ("weights", 4),
    ("wo", 3),
    ("wo_pass", 1),
    ("rows", 1),
    ("grads", 1),
    ("cross", 3),
    ("ps", NCTX),
    ("pg", NCTX),
    ("qs", NCTX),
    ("qg", NCTX),
    ("vc", NCTX),
    ("vt", 3),
) + tuple(
    (f"{kind}{layer}", count)
    for layer in range(2)
    for kind, count in (
        ("x", 3),
        ("kv", NCTX),
        ("q", 1),
        ("oa", 3),
        ("ob", 4),
        ("ow", 1),
        ("ff", 3),
        ("g", 3),
        ("doa", 3),
        ("dob", 4),
        ("dkv", NCTX),
        ("dq", 1),
        ("dx", 3),
    )
):
    SEMAPHORES[name] = COPIES
    COPIES += count


def step_kernel(*refs):
    names = INPUTS + tuple(n for n, _, _ in OUTPUTS) + tuple(n for n, _, _ in SCRATCH)
    r_ = SimpleNamespace(**dict(zip(names, refs)))
    send_sems, recv_sems, load_sems = refs[len(names) :]
    s = lax.axis_index("section")
    c = lax.axis_index("ctx")
    t = lax.axis_index("tp")
    group = c // (NCTX // 2)
    partner = NCTX - 1 - c
    core = {"section": 1 - s}

    def ring(r):
        return lax.rem(t + r, NTP)

    def copy(kind, src, dst, peer, send=0, recv=None):
        base = SEMAPHORES[kind]
        recv = send if recv is None else recv
        return remote(src, dst, send_sems.at[base + send], recv_sems.at[base + recv], peer)

    sent = []

    def start(item):
        item.start()
        sent.append(item)
        return item

    def start_all(items):
        return [start(item) for item in items]

    peers = [core]
    peers += [{"tp": ring(r)} for r in range(1, NTP)]
    peers += [{"ctx": lax.rem(c + r, NCTX)} for r in range(1, NCTX)]
    peers += [{"ctx": partner, "tp": ring(r)} for r in range(1, NTP)]
    barrier = pltpu.get_barrier_semaphore()
    for peer in peers:
        pl.semaphore_signal(barrier, inc=1, device_id=peer, device_id_type=MESH)

    loads = [
        pltpu.make_async_copy(src, dst, load_sems.at[i])
        for i, (src, dst) in enumerate(
            (
                (r_.own_watt, r_.watt.at[s]),
                (r_.own_vecs, r_.vecs.at[s]),
                (r_.own_wup, r_.wup.at[s]),
                (r_.own_wdn, r_.wdn.at[s]),
                (r_.own_wo, r_.wo.at[s, t]),
            )
        )
    ]
    for load in loads:
        load.start()
    r_.xown[0] = r_.xin[s]
    r_.gown[1] = r_.gin[s]
    pl.semaphore_wait(barrier, len(peers))

    def gather_rows(kind, own, full):
        full[t] = own[...]
        return start_all(
            [copy(kind, own, full.at[t], {"tp": ring(r)}, r - 1) for r in range(1, NTP)]
        )

    x_copies = gather_rows("x0", r_.xown.at[0], r_.xg.at[0])
    weight_copies = start_all(
        [
            copy("weights", r_.own_vecs, r_.vecs.at[s], core, 0),
            copy("weights", r_.own_watt, r_.watt.at[s], core, 1),
            copy("weights", r_.own_wup, r_.wup.at[s], core, 2),
            copy("weights", r_.own_wdn, r_.wdn.at[s], core, 3),
        ]
    )
    wo_copies = start_all(
        [copy("wo", r_.own_wo, r_.wo.at[s, t], {"tp": ring(r)}, r - 1) for r in range(1, NTP)]
    )
    g_copies = gather_rows("g1", r_.gown.at[1], r_.gg.at[1])

    def vector(layer, row, width=D):
        return r_.vecs[layer, row : row + 1, 0:width]

    def norm_outputs(layer, xhat):
        first = xhat * vector(layer, 0) + vector(layer, 2)
        second = xhat * vector(layer, 1) + vector(layer, 3)
        return first.astype(BF16), second.astype(BF16)

    def key_mask(key_block, shape, slot):
        key = key_block * BLK + lax.broadcasted_iota(jnp.int32, shape, 0)
        return (key <= r_.place[slot, 0:1, :]) & (key >= r_.place[slot, 1:2, :])

    def visit_both(key_block, visit):
        @pl.loop(0, 2)
        def _(slot):
            query_block = jnp.where(slot == 0, c, partner)
            reached = key_block <= query_block
            edge = needs_mask(key_block, query_block)

            @pl.when(reached & edge)
            def _():
                visit(key_block, slot, True)

            @pl.when(reached & jnp.logical_not(edge))
            def _():
                visit(key_block, slot, False)


    def key_send(layer, r):
        d = lax.rem(c + r, NCTX)
        return c <= top_block(d), copy(
            f"kv{layer}",
            r_.kvs.at[layer, d // (NCTX // 2)],
            r_.kvall.at[layer, c],
            {"ctx": d},
            d,
            c,
        )

    def forward(layer, gathers, before_keys, after_keys, before_out):
        def project(part):
            xhat, _ = normed(r_.xg[layer, part].astype(F32))
            attention_in, _ = norm_outputs(layer, xhat)
            pre = dot_nn(attention_in, r_.watt[layer]) + vector(layer, 6, 384)
            rows = span(part, OWN)
            cosine, sine = r_.rot[0, 0, rows, :], r_.rot[0, 1, rows, :]
            query = turn(pre[:, 0:128], cosine, sine) * 0.125
            r_.qs[layer, rows, :] = query.astype(BF16)
            r_.kvs[layer, 0, rows, :] = turn_left(pre[:, 128:256], cosine, sine).astype(BF16)
            r_.kvs[layer, 1, rows, :] = turn_left(pre[:, 256:384], cosine, sine).astype(BF16)

        before_keys()
        project(t)
        for r, item in enumerate(gathers):
            item.wait_recv()
            project(lax.rem(t + NTP - 1 - r, NTP))

        query_copy = start(copy(f"q{layer}", r_.qs.at[layer], r_.qin.at[layer], {"ctx": partner}))

        @pl.loop(1, NCTX)
        def _(r):
            wanted, item = key_send(layer, r)

            @pl.when(wanted)
            def _():
                item.start()

        r_.kvall[layer, c] = r_.kvs[layer, group]
        after_keys()

        def feed_forward(part):
            xhat, _ = normed(r_.xg[layer, part].astype(F32))
            _, feed_in = norm_outputs(layer, xhat)
            hidden = gelu(dot_nn(feed_in, r_.wup[layer]) + vector(layer, 5)).astype(BF16)
            r_.hid[layer, part] = hidden
            return dot_nn(hidden, r_.wdn[layer])

        def feed_send(r):
            return copy(
                f"ff{layer}",
                r_.ffs.at[layer, r - 1],
                r_.ffr.at[layer, r - 1],
                {"tp": ring(r)},
                r - 1,
            )

        @pl.loop(1, NTP)
        def _(r):
            r_.ffs[layer, r - 1] = feed_forward(ring(r)).astype(BF16)
            feed_send(r).start()

        feed_copies = [feed_send(r) for r in range(1, NTP)]
        sent.extend(feed_copies)
        r_.ffo[...] = feed_forward(t)

        r_.qpad[layer, 0] = my_head(r_.qs[layer].astype(F32), group, 0).astype(BF16)
        query_copy.wait_recv()
        r_.qpad[layer, 1] = my_head(r_.qin[layer].astype(F32), group, 0).astype(BF16)
        r_.acc[...] = jnp.zeros_like(r_.acc)
        r_.top[...] = jnp.full_like(r_.top, LOWEST)

        def visit(key_block, slot, masked):
            scores = dot_nt(r_.kvall[layer, key_block], r_.qpad[layer, slot])
            if masked:
                scores = jnp.where(key_mask(key_block, scores.shape, slot), scores, MASKED)
            old = r_.top[slot]
            new = jnp.maximum(old, jnp.max(scores, axis=0, keepdims=True))
            weights = jnp.exp(scores - new).astype(BF16)
            r_.top[slot] = new
            r_.acc[slot] = r_.acc[slot] * jnp.exp(old - new) + dot_nn(r_.kvt[...], weights)

        @pl.loop(0, NCTX)
        def _(r):
            key_block = lax.rem(c + NCTX - r, NCTX)

            @pl.when(key_block <= top_block(c))
            def _():
                @pl.when(r > 0)
                def _():
                    copy(
                        f"kv{layer}",
                        r_.kvs.at[layer, 0],
                        r_.kvall.at[layer, key_block],
                        {"ctx": partner},
                        0,
                        key_block,
                    ).wait_recv()

                turned = r_.kvall[layer, key_block].astype(F32).T
                row = lax.broadcasted_iota(jnp.int32, turned.shape, 0)
                r_.kvt[...] = jnp.where(row < HEAD_DIM, 1.0, turned).astype(BF16)
                visit_both(key_block, visit)

        def finish(slot):
            total = r_.acc[slot, 0:HEAD_DIM, :]
            mean = r_.acc[slot, HEAD_DIM:, :] / total
            r_.ot[layer, slot] = mean
            r_.lse[layer, slot] = r_.top[slot] + jnp.log(total[0:1])
            r_.oout[layer, slot] = two_head_tile(mean, group).astype(BF16)

        finish(1)
        far = start_all(
            [
                copy(
                    f"ob{layer}",
                    r_.oout.at[layer, 1, span(ring(r), OWN), :],
                    r_.ob.at[layer, t],
                    {"ctx": partner, "tp": ring(r)},
                    r,
                )
                for r in range(NTP)
            ]
        )
        finish(0)
        near = start_all(
            [
                copy(
                    f"oa{layer}",
                    r_.oout.at[layer, 0, span(ring(r), OWN), :],
                    r_.oa.at[layer, t],
                    {"tp": ring(r)},
                    r - 1,
                )
                for r in range(1, NTP)
            ]
        )
        r_.oa[layer, t] = r_.oout[layer, 0, span(t, OWN), :]
        start(copy(f"ow{layer}", r_.oout.at[layer, 1], r_.oin.at[layer], {"ctx": partner}))

        result = r_.xown[layer].astype(F32) + vector(layer, 4) + r_.ffo[...]
        for r, item in enumerate(feed_copies):
            item.wait_recv()
            result = result + r_.ffr[layer, r].astype(F32)
        for item in far + near:
            item.wait_recv()
        before_out()
        heads = jnp.concatenate(
            [r_.oa[layer, p] + r_.ob[layer, p] for p in range(NTP)], axis=1
        )
        result = result + dot_nn(heads, r_.wo[layer].reshape(D, D))
        r_.fo[layer] = result.astype(BF16)


    def send_attention_grads(layer):
        tile = dot_nt(r_.gown[layer], r_.wo[layer].reshape(D, D)).astype(BF16)
        for p in range(NTP):
            r_.dos[layer, p] = tile[:, p * LANES : (p + 1) * LANES]
        far = start_all(
            [
                copy(
                    f"dob{layer}",
                    r_.dos.at[layer, ring(r)],
                    r_.dob.at[layer, t],
                    {"ctx": partner, "tp": ring(r)},
                    r,
                )
                for r in range(NTP)
            ]
        )
        near = start_all(
            [
                copy(
                    f"doa{layer}",
                    r_.dos.at[layer, ring(r)],
                    r_.doa.at[layer, t],
                    {"tp": ring(r)},
                    r - 1,
                )
                for r in range(1, NTP)
            ]
        )
        r_.doa[layer, t] = r_.dos[layer, t]
        return near + far

    def key_grad_send(layer, key_block):
        return copy(
            f"dkv{layer}",
            r_.dkvo.at[layer, key_block],
            r_.dkvi.at[layer, c],
            {"ctx": key_block},
            key_block,
            c,
        )

    def backward(layer, grad_copies, gathers, beside, after_feed):
        for item in grad_copies:
            item.wait_recv()

        def prepare(slot, tile):
            padded = my_head(tile.reshape(BLK, LANES).astype(F32), group, 1)
            r_.dopad[slot] = padded.astype(BF16)
            r_.delta[slot] = jnp.sum(
                padded.T[HEAD_DIM:, :] * r_.ot[layer, slot], axis=0, keepdims=True
            )

        prepare(0, r_.doa[layer])
        prepare(1, r_.dob[layer])
        r_.dqt[...] = jnp.zeros_like(r_.dqt)

        def visit(key_block, slot, masked):
            keys = r_.kvall[layer, key_block]
            queries, grads = r_.qpad[layer, slot], r_.dopad[slot]
            scores = dot_nt(keys, queries)
            weights = jnp.exp(scores - r_.lse[layer, slot])
            if masked:
                weights = jnp.where(key_mask(key_block, scores.shape, slot), weights, 0.0)
            weight_grad = dot_nt(keys, grads)
            score_grad = (weights * (weight_grad - r_.delta[slot])).astype(BF16)
            r_.dkva[...] += dot_nn(weights.astype(BF16), grads) + dot_nn(score_grad, queries)
            r_.dqt[slot] += dot_nn(r_.kvt[...], score_grad)

        @pl.loop(1, NCTX + 1)
        def _(r):
            key_block = lax.rem(c + r, NCTX)

            @pl.when(key_block <= top_block(c))
            def _():
                r_.kvt[...] = r_.kvall[layer, key_block].astype(F32).T.astype(BF16)
                r_.dkva[...] = jnp.zeros_like(r_.dkva)
                visit_both(key_block, visit)
                r_.dkvo[layer, key_block] = r_.dkva[...].astype(BF16)

                @pl.when(r < NCTX)
                def _():
                    key_grad_send(layer, key_block).start()

        def query_grad(slot):
            tile = two_head_tile(r_.dqt[slot, 0:HEAD_DIM, :] * 0.125, group)
            return turn(tile, r_.rot[slot, 0], -r_.rot[slot, 1]).astype(BF16)

        r_.dqs[layer] = query_grad(1)
        query_copy = start(copy(f"dq{layer}", r_.dqs.at[layer], r_.dqi.at[layer], {"ctx": partner}))
        r_.dproj[:, 0:128] = query_grad(0)

        for item in gathers:
            item.wait_recv()
        r_.gv[layer] = jnp.zeros((8, D), F32)
        own_sum = jnp.sum(r_.gown[layer].astype(F32), axis=0, keepdims=True)
        r_.gv[layer, 4:5, :] = own_sum

        def add_vector(row, value):
            r_.gv[layer, row : row + 1, :] += jnp.sum(value, axis=0, keepdims=True)

        @pl.loop(0, NTP)
        def _(part):
            xhat, _ = normed(r_.xg[layer, part].astype(F32))
            attention_in, feed_in = norm_outputs(layer, xhat)
            r_.ain[part] = attention_in
            r_.fin[part] = feed_in
            up_pre = dot_nn(feed_in, r_.wup[layer]) + vector(layer, 5)
            hidden_grad = dot_nt(r_.gg[layer, part], r_.wdn[layer])
            up_grad = (hidden_grad * gelu_slope(up_pre)).astype(BF16)
            r_.ugs[part] = up_grad
            add_vector(5, up_grad.astype(F32))
            feed_grad = dot_nt(up_grad, r_.wup[layer])
            add_vector(1, xhat * feed_grad)
            add_vector(3, feed_grad)
            r_.dxh[part] = feed_grad * vector(layer, 1)

        full_grad = r_.gg[layer].reshape(BLK, D)
        up_terms = dot_tn(r_.fin[...].reshape(BLK, D), r_.ugs[...].reshape(BLK, D))
        r_.gwp[layer, 0:D, :] = up_terms.astype(BF16)
        r_.gwp[layer, D:, :] = dot_tn(r_.hid[layer].reshape(BLK, D), full_grad).astype(BF16)
        after_feed()
        out_copy = copy(f"ow{layer}", r_.oout.at[layer, 1], r_.oin.at[layer], {"ctx": partner})
        out_copy.wait_recv()
        attention = r_.oout[layer, 0] + r_.oin[layer]
        r_.gwq[layer, 0:128, :] = dot_tn(attention, full_grad).astype(BF16)
        beside()

        def key_grad(half):
            r_.dkva[...] = jnp.zeros_like(r_.dkva)

            @pl.loop(0, NCTX // 2)
            def _(step):
                source = half * (NCTX // 2) + step

                @pl.when(source == c)
                def _():
                    r_.dkva[...] += r_.dkvo[layer, c].astype(F32)

                @pl.when((c <= top_block(source)) & (source != c))
                def _():
                    copy(
                        f"dkv{layer}",
                        r_.dkvo.at[layer, 0],
                        r_.dkvi.at[layer, source],
                        {"ctx": partner},
                        0,
                        source,
                    ).wait_recv()
                    r_.dkva[...] += r_.dkvi[layer, source].astype(F32)

            return turn_left(r_.dkva[...], r_.rot[0, 0], -r_.rot[0, 1]).astype(BF16)

        r_.dproj[:, 128:256] = key_grad(0)
        r_.dproj[:, 256:384] = key_grad(1)
        query_copy.wait_recv()
        r_.dproj[:, 0:128] += r_.dqi[layer]

        def input_part(part):
            xhat, _ = normed(r_.xg[layer, part].astype(F32))
            grad = dot_nt(r_.dproj[span(part, OWN), :], r_.watt[layer])
            add_vector(0, xhat * grad)
            add_vector(2, grad)
            return r_.dxh[part] + grad * vector(layer, 0)

        scatters = []
        for r in range(1, NTP):
            r_.dxs[layer, r - 1] = input_part(ring(r)).astype(BF16)
            item = copy(
                f"dx{layer}",
                r_.dxs.at[layer, r - 1],
                r_.dxr.at[layer, r - 1],
                {"tp": ring(r)},
                r - 1,
            )
            scatters.append(start(item))
        total = input_part(t)
        bias_sum = jnp.sum(r_.dproj[...].astype(F32), axis=0, keepdims=True)
        r_.gv[layer, 6:7, 0:384] = bias_sum
        terms = dot_tn(r_.dproj[...], r_.ain[...].reshape(BLK, D))
        r_.gwq[layer, 128:, :] = terms.astype(BF16)
        for r, item in enumerate(scatters):
            item.wait_recv()
            total = total + r_.dxr[layer, r].astype(F32)
        xhat, inverse = normed(r_.xown[layer].astype(F32))
        along = jnp.mean(total * xhat, axis=-1, keepdims=True)
        centred = total - jnp.mean(total, axis=-1, keepdims=True) - xhat * along
        r_.go[layer] = (r_.gown[layer].astype(F32) + centred * inverse).astype(BF16)


    def cross_copy(which, layer):
        src = (r_.gwp, r_.gwq, r_.gv)[which].at[layer]
        return copy("cross", src, (r_.crp, r_.crq, r_.crv)[which], core, which)

    def cross_start(which, layer):
        @pl.when(s != layer)
        def _():
            cross_copy(which, layer).start()

    wide_parts = (
        (r_.gwp, r_.crp, r_.sump, r_.inp, r_.minep, r_.gatp, "ps", "pg", 64),
        (r_.gwq, r_.crq, r_.sumq, r_.inq, r_.mineq, r_.gatq, "qs", "qg", 32),
    )

    def scatter_copy(which, r):
        _, _, sums, arrived, _, _, kind, _, _ = wide_parts[which]
        d = lax.rem(c + r, NCTX)
        return copy(kind, sums.at[d], arrived.at[r], {"ctx": d}, r)

    def gather_copy(which, r):
        _, _, _, _, mine, full, _, kind, _ = wide_parts[which]
        return copy(kind, mine, full.at[c], {"ctx": lax.rem(c + r, NCTX)}, r)

    def scatter_terms(which, layer):
        terms, crossed, sums, _, _, _, _, _, chunk = wide_parts[which]

        @pl.when(s == layer)
        def _():
            cross_copy(which, layer).wait_recv()

            @pl.loop(0, NCTX)
            def _(j):
                rows = span(j, chunk)
                pair = terms[layer, rows, :].astype(F32) + crossed[rows, :].astype(F32)
                sums[j] = pair.astype(BF16)

            @pl.loop(1, NCTX)
            def _(r):
                scatter_copy(which, r).start()

    def store_chunk(which, j, value):
        chunk = wide_parts[which][-1]
        target = (r_.out_ff, r_.allq)[which]
        target[span(j, chunk), :] = value

    def gather_sums(which, layer):
        _, _, sums, arrived, mine, _, _, _, _ = wide_parts[which]

        @pl.when(s == layer)
        def _():
            total = sums[c].astype(F32)
            for r in range(1, NCTX):
                scatter_copy(which, r).wait_recv()
                total = total + arrived[r].astype(F32)
            mine[...] = total.astype(BF16)

            @pl.loop(1, NCTX)
            def _(r):
                gather_copy(which, r).start()

            store_chunk(which, c, total)

    def store_sums(which, layer):
        _, _, _, _, mine, full, _, kind, _ = wide_parts[which]

        @pl.when(s == layer)
        def _():
            @pl.loop(1, NCTX)
            def _(r):
                source = lax.rem(c + NCTX - r, NCTX)
                copy(kind, mine, full.at[source], core, r).wait_recv()
                store_chunk(which, source, full[source].astype(F32))

    def vector_copy(r):
        return copy("vc", r_.vec, r_.vec_in.at[r], {"ctx": lax.rem(c + r, NCTX)}, r)

    def vector_tp_copy(r):
        return copy("vt", r_.vec_tp, r_.vec_tp_in.at[r - 1], {"tp": ring(r)}, r - 1)

    def vector_first(layer):
        @pl.when(s == layer)
        def _():
            cross_copy(2, layer).wait_recv()
            r_.vec[...] = r_.gv[layer] + r_.crv[...]

            @pl.loop(1, NCTX)
            def _(r):
                vector_copy(r).start()

    def vector_second(layer):
        @pl.when(s == layer)
        def _():
            total = r_.vec[...]
            for r in range(1, NCTX):
                vector_copy(r).wait_recv()
                total = total + r_.vec_in[r]
            r_.vec_tp[...] = total
            for r in range(1, NTP):
                vector_tp_copy(r).start()

    def vector_last(layer):
        @pl.when(s == layer)
        def _():
            total = r_.vec_tp[...]
            shared = total
            for r in range(1, NTP):
                vector_tp_copy(r).wait_recv()
                shared = shared + r_.vec_tp_in[r - 1]
            row = lax.broadcasted_iota(jnp.int32, shared.shape, 0)
            r_.out_small[...] = jnp.where(row < 5, shared, total)

    def store_attention():
        r_.out_wo[...] = r_.allq[0:128, :]
        turned = r_.allq[128:, :].T
        first, second = turned[:, 128:256], turned[:, 256:384]
        left = lanes(first.shape) < HEAD_DIM
        r_.out_att[0] = turned[:, 0:128]
        r_.out_att[1] = jnp.where(left, first, pltpu.roll(second, HEAD_DIM, 1))
        r_.out_att[2] = jnp.where(left, pltpu.roll(first, HEAD_DIM, 1), second)


    def nothing():
        pass

    def wait_first_weights():
        for load in loads:
            load.wait()
        weight_copies[0].wait_recv()
        weight_copies[1].wait_recv()

    def wait_other_weights():
        weight_copies[2].wait_recv()
        weight_copies[3].wait_recv()
        for item in wo_copies:
            item.wait_recv()
        start(wo_pass)

    wo_pass = copy("wo_pass", r_.wo.at[s], r_.wo.at[s], core)
    forward(0, x_copies, wait_first_weights, wait_other_weights, wo_pass.wait_recv)
    r_.xown[1] = r_.fo[0]
    x_copies = gather_rows("x1", r_.xown.at[1], r_.xg.at[1])
    grad_copies = send_attention_grads(1)
    forward(1, x_copies, nothing, nothing, nothing)

    rows_copy = start(copy("rows", r_.fo.at[1 - s], r_.out_rows.at[s], core))
    r_.out_rows[s] = r_.fo[s]

    backward(1, grad_copies, g_copies, nothing, lambda: cross_start(0, 1))
    r_.gown[0] = r_.go[1]
    g_copies = gather_rows("g0", r_.gown.at[0], r_.gg.at[0])
    grad_copies = send_attention_grads(0)
    cross_start(1, 1)
    cross_start(2, 1)
    scatter_terms(0, 1)

    def beside_last():
        scatter_terms(1, 1)
        vector_first(1)
        gather_sums(0, 1)
        scatter_terms(0, 0)

    backward(0, grad_copies, g_copies, beside_last, lambda: cross_start(0, 0))
    cross_start(1, 0)
    cross_start(2, 0)
    grads_copy = start(copy("grads", r_.go.at[1 - s], r_.out_grads.at[s], core))
    r_.out_grads[s] = r_.go[s]
    scatter_terms(1, 0)
    vector_first(0)
    gather_sums(0, 0)
    gather_sums(1, 1)
    vector_second(1)
    vector_second(0)
    gather_sums(1, 0)
    for layer in (1, 0):
        store_sums(0, layer)
        vector_last(layer)
        store_sums(1, layer)
    store_attention()
    rows_copy.wait_recv()
    grads_copy.wait_recv()


    for item in sent:
        item.wait_send()
    for layer in range(2):

        @pl.loop(1, NCTX)
        def _(r):
            wanted, item = key_send(layer, r)

            @pl.when(wanted)
            def _():
                item.wait_send()

            key_block = lax.rem(c + r, NCTX)

            @pl.when(key_block <= top_block(c))
            def _():
                key_grad_send(layer, key_block).wait_send()

        @pl.when(s != layer)
        def _():
            for which in range(3):
                cross_copy(which, layer).wait_send()

    @pl.loop(1, NCTX)
    def _(r):
        for which in range(2):
            scatter_copy(which, r).wait_send()
            gather_copy(which, r).wait_send()
        vector_copy(r).wait_send()

    for r in range(1, NTP):
        vector_tp_copy(r).wait_send()


def run_step(operands):
    vmem = pl.BlockSpec(memory_space=pltpu.VMEM)
    anywhere = pl.BlockSpec(memory_space=pl.ANY)
    dma = pltpu.SemaphoreType.DMA
    return pl.pallas_call(
        step_kernel,
        out_shape=[jax.ShapeDtypeStruct(shape, kind) for _, shape, kind in OUTPUTS],
        in_specs=[anywhere if name.startswith("own_") else vmem for name in INPUTS],
        out_specs=[vmem] * len(OUTPUTS),
        scratch_shapes=[pltpu.VMEM(shape, kind) for _, shape, kind in SCRATCH]
        + [dma((COPIES,)), dma((COPIES,)), dma((5,))],
        compiler_params=pltpu.CompilerParams(
            collective_id=0, has_side_effects=True, vmem_limit_bytes=VMEM_LIMIT
        ),
        name="train_step",
    )(*operands)


def sequence_starts(lengths, positions):
    ends = jnp.cumsum(lengths).astype(jnp.int32)
    before = jnp.where(ends[None, :] <= positions[:, None], lengths[None, :], 0)
    return jnp.sum(before, axis=1).astype(jnp.int32)


def rotary_lanes(offsets):
    rates = 1.0 / 10000.0 ** (jnp.arange(0, ROT, 2).astype(F32) / ROT)
    rest = jnp.zeros((HEAD_DIM - ROT,), F32)
    rates = jnp.concatenate([rates, rates, rest] * 2)
    signs = jnp.where(jnp.arange(LANES) % HEAD_DIM < ROT // 2, -1.0, 1.0)
    angles = offsets.astype(F32)[..., None] * rates
    return jnp.stack([jnp.cos(angles), jnp.sin(angles) * signs], axis=1)


def pack_attention(items):
    q, k, v = items
    half = HEAD_DIM
    return jnp.concatenate([q, k[:, :half], v[:, :half], k[:, half:], v[:, half:]], axis=1)


def local(
    block_input,
    output_grad,
    sequence_lengths,
    norm_gain,
    norm_bias,
    attention_weight,
    attention_bias,
    output_weight,
    up_weight,
    up_bias,
    down_weight,
    branch_bias,
):
    s = lax.axis_index("section")
    c = lax.axis_index("ctx")
    packed_bias = pack_attention([attention_bias[:, k] for k in range(3)])
    vectors = jnp.concatenate(
        [
            norm_gain[0],
            norm_bias[0],
            branch_bias,
            up_bias,
            jnp.pad(packed_bias, ((0, 0), (0, D - 384))),
            jnp.zeros((1, D), F32),
        ]
    )
    lengths = jnp.where(s == 0, sequence_lengths[0], sequence_lengths[1])
    steps = jnp.arange(BLK, dtype=jnp.int32)
    positions = jnp.stack([c * BLK + steps, (NCTX - 1 - c) * BLK + steps])
    starts = sequence_starts(lengths, positions.reshape(-1)).reshape(2, BLK)
    rows, grads, ff, wo, att, small = run_step(
        (
            block_input,
            output_grad,
            pack_attention([attention_weight[0, k] for k in range(3)]),
            output_weight[0],
            up_weight[0],
            down_weight[0],
            vectors,
            rotary_lanes(positions - starts),
            jnp.stack([positions, starts], axis=1),
        )
    )
    half = HEAD_DIM
    bias = small[6, 0:384]
    bias_parts = jnp.stack(
        [
            bias[0:128],
            jnp.concatenate([bias[128 : 128 + half], bias[256 : 256 + half]]),
            jnp.concatenate([bias[128 + half : 256], bias[256 + half :]]),
        ]
    )
    return (
        rows[None],
        grads[None],
        small[None, 0:2],
        small[None, 2:4],
        att[None],
        bias_parts[None],
        wo[None],
        ff[None, 0:D],
        small[5:6],
        ff[None, D:],
        small[4:5],
    )


def solution(mesh):
    placed = (
        P(None, ("ctx", "tp"), None),
        P(None, ("ctx", "tp"), None),
        P(),
        P("section", None, None),
        P("section", None, None),
        P("section", None, None, "tp"),
        P("section", None, "tp"),
        P("section", "tp", None),
        P("section", None, "tp"),
        P("section", "tp"),
        P("section", "tp", None),
        P("section", None),
    )
    return jax.shard_map(
        local,
        mesh=mesh,
        in_specs=placed,
        out_specs=(
            P("section", None, ("ctx", "tp"), None),
            P("section", None, ("ctx", "tp"), None),
            P("section", None, None),
            P("section", None, None),
            P("section", None, None, "tp"),
            P("section", None, "tp"),
            P("section", "tp", None),
            P("section", None, "tp"),
            P("section", "tp"),
            P("section", "tp", None),
            P("section", None),
        ),
        check_vma=False,
    )
```

time: 2330 us -> 263 us (0.11)
  waiting for transfers between devices: 1240 us -> 0 us
  blocking collectives: 508 us -> 0 us
  Pallas kernels: 0 us -> 241 us
  loops' own time: 196 us -> 0 us
  local copies, waits for them, and re-layouts: 202 us -> 15.5 us
  matrix products: 83.2 us -> 0 us
  other arithmetic: 57.8 us -> 5.53 us
    reduce_scatter x15 -> x0, waiting for transfers between devices: 1120 us -> none  [the longest x3 630 us: layer_backward(): lax.psum_scatter(key_grads.reshape(total_rows, -1).astype(jnp.bfloat16),...]
    psum x2 -> x0, blocking collectives: 388 us -> none  [the longest x1 347 us: local(): small_total = lax.psum(small_total, ('ctx', 'tp'))]
    pallas_call x0 -> x1, Pallas kernels: none -> 241 us  [run_step(): pl.pallas_call(step_kernel, out_shape=[jax.ShapeDtypeStruct(shape, kind)...]
    another operation x153 -> x0, loops' own time: 196 us -> none  [the longest x3 65.7 us: attend(): lax.fori_loop(0, blocks, collect_stats, (start_top, jnp.zeros((heads, cou...]
    slice x308 -> x5, local copies, waits for them, and re-layouts: 169 us -> 3.09 us  [the longest x1 1.38 us: local(): small[4:5]]
    all_gather x9 -> x0, blocking collectives: 119 us -> none  [the longest x3 40.3 us: layer_forward(): lax.all_gather(attention_in.astype(jnp.bfloat16), 'tp', axis=0, tiled=True)]
    all_gather x6 -> x0, waiting for transfers between devices: 117 us -> none  [the longest x3 94.7 us: layer_forward(): lax.all_gather(keys.reshape(width, -1), 'ctx', axis=0, tiled=True)]
    dot_general x47 -> x0, matrix products: 82 us -> none  [the longest x3 15.7 us: layer_forward(): jnp.dot(feed_in, up_weight, preferred_element_type=jnp.float32) + up_bias]
  transfers between devices with their start and end apart: 26 -> 0, of which waited for: 24 -> 0; matrix products, arithmetic and copies ran while one was open for 6% -> 0% of each run, Pallas kernels for 0% -> 0%
where the time goes in v2:
time: 263 us; the launch traced here: 262 us
  Pallas kernels  241 us (92%)
  local copies, waits for them, and re-layouts  15.5 us (6%)
  other arithmetic  5.53 us (2%)
    pallas_call x1, Pallas kernels, run_step(): pl.pallas_call(step_kernel, out_shape=[jax.ShapeDtypeStruct(shape, kind)...  241 us

profile of v2, /device:TPU:0, one launch (start us, length us, event | category | flops | bytes accessed | tf_op | source)
XLA Modules:
  0.0 262.4 jit_solution(5437896250402378834)
XLA Ops:
  0.7 0.8 fusion.7
  1.4 0.8 fusion.8
  2.2 0.2 reduce-window.8
  2.4 0.1 concatenate.25
  2.4 0.7 slice_bitcast_fusion.11
  3.1 0.1 fusion.5
  3.2 0.1 concatenate.23
  3.4 0.1 select_reduce_fusion
  3.5 0.6 pad_add_fusion.refs_8_
  4.1 1.4 concatenate.24.refs_6_
  5.5 1.1 slice_bitcast_fusion.2
  6.5 0.1 fusion.2
  6.7 1.0 concatenate.22.refs_2_
  7.7 1.9 multiply_cosine_fusion
  9.6 1.0 pad_maximum_fusion.refs_7_
  10.6 240.6 %train_step.1 = (bf16[2,128,512]{2,1,0:T(8,128)(2,1)}, bf16[2,128,512]{2,1,0:T(8,128)(2,1)}, f32[1024,512]{1,0:T(8,128)}, f32[128,512]{1,0:T(8,128)}, f32[3,512,128]{2,1,0:T(8,128)}, /*index=5*/f32[8,512]{1,0:T(8,128)}) custom-call(bf16[2,128,512]{2,1,0:T(8,128)(2,1)} %refs_0_.1, bf16[2,128,512]{2,1,0:T(8,128)(2,1)} %refs_1_.1, ...), custom_call_target="tpu_custom_call" | custom-call | tf_op jit(solution)/shard_map/train_step/pallas_call | solution.py:888
  251.2 0.7 slice.118
  251.9 0.8 slice_bitcast_fusion.10
  252.7 0.1 maximum_bitcast_fusion.1
  252.8 0.1 maximum_bitcast_fusion.2
  252.9 0.6 copy.24
  253.5 1.4 fusion.4
  254.8 1.4 slice_bitcast_fusion.5
  256.2 0.0 copy-start.3
  256.2 0.0 copy-start.2
  256.2 0.0 copy-start
  256.2 3.1 %slice_bitcast_fusion = (f32[1,512,512]{2,1,0:T(8,128)}, f32[1,512,512]{2,1,0:T(8,128)}) fusion(f32[1024,512]{1,0:T(8,128)} %get-tuple-element.22), kind=kLoop, calls=%fused_computation.1 | loop fusion | bytes 4194304 | tf_op jit(solution)/shard_map/broadcast_in_dim | solution.py:986
  259.4 0.0 copy-start.1
  259.4 0.0 copy-done.3
  259.4 0.7 copy.30
  260.1 0.0 copy-done.2
  260.1 0.7 copy.31
  260.8 0.0 copy-done
  260.8 0.9 copy.32
  261.7 0.0 copy-done.1
  261.7 0.7 copy.33
  (12 shorter events, 0.1 us)
Async XLA Ops:
  256.2 3.1 %copy-start.3 = (bf16[2,128,512]{2,1,0:T(8,128)(2,1)S(1)}, bf16[2,128,512]{2,1,0:T(8,128)(2,1)}, u32[]{:S(2)}) copy-start(bf16[2,128,512]{2,1,0:T(8,128)(2,1)} %get-tuple-element.17) | copy-start | bytes 786436
  256.2 3.8 %copy-start.2 = (bf16[2,128,512]{2,1,0:T(8,128)(2,1)S(1)}, bf16[2,128,512]{2,1,0:T(8,128)(2,1)}, u32[]{:S(2)}) copy-start(bf16[2,128,512]{2,1,0:T(8,128)(2,1)} %get-tuple-element.18) | copy-start | bytes 786436
  256.2 4.6 %copy-start = (f32[3,512,128]{2,1,0:T(8,128)S(1)}, f32[3,512,128]{2,1,0:T(8,128)}, u32[]{:S(2)}) copy-start(f32[3,512,128]{2,1,0:T(8,128)} %get-tuple-element.20) | copy-start | bytes 2359300
  259.4 2.3 copy-start.1

commit v3 on v2

--- a/solution.py
+++ b/solution.py
@@ -19,6 +19,11 @@
 OWN = 128
 D = 512
 LANES = 128
+STEPS = (
+    (0, 1), (1, 0), (0, 3), (3, 0), (1, 1), (3, 3), (1, 3), (3, 1),
+    (0, 2), (2, 0), (1, 2), (3, 2), (2, 1), (2, 3), (2, 2),
+)
+AHEAD = 5
 MASKED = -1e30
 LOWEST = -1e29
 
@@ -96,17 +101,39 @@
     return (key_block == 0) | (key_block == query_block) | (query_block == NCTX - 1)
 
 
+def wrap(index, count):
+    return jnp.where(index >= count, index - count, index)
+
+
+def stepped(c, index, sign):
+    z, y = c // 4, c % 4
+    dz, dy = 0, 0
+    for k, (along_z, along_y) in enumerate(STEPS):
+        dz = jnp.where(index == k, along_z, dz)
+        dy = jnp.where(index == k, along_y, dy)
+    return wrap(z + (dz if sign > 0 else 4 - dz), 4) * 4 + wrap(y + (dy if sign > 0 else 4 - dy), 4)
+
+
+def second_group(d):
+    return jnp.where(d >= NCTX // 2, 1, 0)
+
+
 def span(index, size):
     return pl.ds(pl.multiple_of(index * size, size), size)
 
 
 OUTPUTS = (
-    ("out_rows", (2, OWN, D), BF16),
-    ("out_grads", (2, OWN, D), BF16),
-    ("out_ff", (2 * D, D), F32),
-    ("out_wo", (OWN, D), F32),
-    ("out_att", (3, D, OWN), F32),
-    ("out_small", (8, D), F32),
+    ("out_rows", (1, 2, OWN, D), BF16),
+    ("out_grads", (1, 2, OWN, D), BF16),
+    ("out_gain", (1, 2, D), F32),
+    ("out_norm_bias", (1, 2, D), F32),
+    ("out_att", (1, 3, D, OWN), F32),
+    ("out_att_bias", (1, 3, OWN), F32),
+    ("out_wo", (1, OWN, D), F32),
+    ("out_up", (1, D, D), F32),
+    ("out_up_bias", (1, D), F32),
+    ("out_dn", (1, D, D), F32),
+    ("out_branch", (1, D), F32),
 )
 
 SCRATCH = (
@@ -115,6 +142,10 @@
     ("wup", (2, D, D), BF16),
     ("wdn", (2, D, D), BF16),
     ("vecs", (2, 8, D), F32),
+    ("vown", (8, D), F32),
+    ("place", (2, 2, BLK), jnp.int32),
+    ("cosine", (2, BLK, LANES), F32),
+    ("sine", (2, BLK, LANES), F32),
     ("xown", (2, OWN, D), BF16),
     ("fo", (2, OWN, D), BF16),
     ("xg", (2, NTP, OWN, D), BF16),
@@ -178,12 +209,25 @@
     ("vec_tp_in", (NTP - 1, 8, D), F32),
 )
 
-INPUTS = ("xin", "gin", "own_watt", "own_wo", "own_wup", "own_wdn", "own_vecs", "rot", "place")
+INPUTS = (
+    ("xin", pltpu.VMEM),
+    ("gin", pltpu.VMEM),
+    ("lengths", pltpu.SMEM),
+    ("gains", pltpu.VMEM),
+    ("biases", pltpu.VMEM),
+    ("own_watt", pl.ANY),
+    ("att_bias", pltpu.VMEM),
+    ("own_wo", pl.ANY),
+    ("own_wup", pl.ANY),
+    ("up_bias", pltpu.VMEM),
+    ("own_wdn", pl.ANY),
+    ("branch_bias", pltpu.VMEM),
+)
 
 SEMAPHORES = {}
 COPIES = 0
 for name, count in (
-    ("weights", 4),
+    ("weights", 6),
     ("wo", 3),
     ("wo_pass", 1),
     ("rows", 1),
@@ -219,18 +263,27 @@
 
 
 def step_kernel(*refs):
-    names = INPUTS + tuple(n for n, _, _ in OUTPUTS) + tuple(n for n, _, _ in SCRATCH)
+    names = tuple(n for n, _ in INPUTS) + tuple(n for n, _, _ in OUTPUTS) + tuple(n for n, _, _ in SCRATCH)
     r_ = SimpleNamespace(**dict(zip(names, refs)))
     send_sems, recv_sems, load_sems = refs[len(names) :]
     s = lax.axis_index("section")
     c = lax.axis_index("ctx")
     t = lax.axis_index("tp")
-    group = c // (NCTX // 2)
+    group = second_group(c)
     partner = NCTX - 1 - c
-    core = {"section": 1 - s}
+    core = {"section": 1 - s, "ctx": c, "tp": t}
+
+    def at_ctx(d):
+        return {"section": s, "ctx": d, "tp": t}
+
+    def at_tp(d):
+        return {"section": s, "ctx": c, "tp": d}
+
+    def at_partner(d):
+        return {"section": s, "ctx": partner, "tp": d}
 
     def ring(r):
-        return lax.rem(t + r, NTP)
+        return wrap(t + r, NTP)
 
     def copy(kind, src, dst, peer, send=0, recv=None):
         base = SEMAPHORES[kind]
@@ -248,27 +301,52 @@
         return [start(item) for item in items]
 
     peers = [core]
-    peers += [{"tp": ring(r)} for r in range(1, NTP)]
-    peers += [{"ctx": lax.rem(c + r, NCTX)} for r in range(1, NCTX)]
-    peers += [{"ctx": partner, "tp": ring(r)} for r in range(1, NTP)]
+    peers += [at_tp(ring(r)) for r in range(1, NTP)]
+    peers += [at_ctx(wrap(c + r, NCTX)) for r in range(1, NCTX)]
+    peers += [at_partner(ring(r)) for r in range(1, NTP)]
     barrier = pltpu.get_barrier_semaphore()
     for peer in peers:
         pl.semaphore_signal(barrier, inc=1, device_id=peer, device_id_type=MESH)
 
+    own_weights = [
+        (r_.own_watt.at[0, k], r_.watt.at[s, :, k * LANES : (k + 1) * LANES]) for k in range(3)
+    ]
+    own_weights += [(r_.own_wup.at[0], r_.wup.at[s]), (r_.own_wdn.at[0], r_.wdn.at[s])]
     loads = [
         pltpu.make_async_copy(src, dst, load_sems.at[i])
-        for i, (src, dst) in enumerate(
-            (
-                (r_.own_watt, r_.watt.at[s]),
-                (r_.own_vecs, r_.vecs.at[s]),
-                (r_.own_wup, r_.wup.at[s]),
-                (r_.own_wdn, r_.wdn.at[s]),
-                (r_.own_wo, r_.wo.at[s, t]),
-            )
-        )
+        for i, (src, dst) in enumerate(own_weights + [(r_.own_wo.at[0], r_.wo.at[s, t])])
     ]
     for load in loads:
         load.start()
+    r_.vown[...] = jnp.zeros((8, D), F32)
+    r_.vown[0:2, :] = r_.gains[0]
+    r_.vown[2:4, :] = r_.biases[0]
+    r_.vown[4:5, :] = r_.branch_bias[...]
+    r_.vown[5:6, :] = r_.up_bias[...]
+    for k in range(3):
+        r_.vown[6:7, k * LANES : (k + 1) * LANES] = r_.att_bias[0, k : k + 1, :]
+    r_.vecs[s] = r_.vown[...]
+    rate_row = lax.broadcasted_iota(jnp.int32, (ROT // 2, 1), 0)
+    rates = jnp.zeros((ROT // 2, 1), F32)
+    for i in range(ROT // 2):
+        rates = jnp.where(rate_row == i, 1.0 / 10000.0 ** (2 * i / ROT), rates)
+    for slot, block in ((0, c), (1, partner)):
+        place = block * BLK + lanes((1, BLK))
+        first = jnp.zeros((1, BLK), jnp.int32)
+        end = 0
+        for k in range(r_.lengths.shape[1]):
+            length = jnp.where(s == 0, r_.lengths[0, k], r_.lengths[1, k])
+            end = end + length
+            first = first + jnp.where(place >= end, length, 0)
+        r_.place[slot, 0:1, :] = place
+        r_.place[slot, 1:2, :] = first
+        angles = (place - first).astype(F32) * rates
+        cosine, sine = jnp.cos(angles), jnp.sin(angles)
+        still = jnp.zeros((HEAD_DIM - ROT, BLK), F32)
+        cosine = jnp.concatenate([cosine, cosine, still + 1.0], axis=0)
+        sine = jnp.concatenate([-sine, sine, still], axis=0)
+        r_.cosine[slot] = jnp.concatenate([cosine, cosine], axis=0).T
+        r_.sine[slot] = jnp.concatenate([sine, sine], axis=0).T
     r_.xown[0] = r_.xin[s]
     r_.gown[1] = r_.gin[s]
     pl.semaphore_wait(barrier, len(peers))
@@ -276,22 +354,16 @@
     def gather_rows(kind, own, full):
         full[t] = own[...]
         return start_all(
-            [copy(kind, own, full.at[t], {"tp": ring(r)}, r - 1) for r in range(1, NTP)]
+            [copy(kind, own, full.at[t], at_tp(ring(r)), r - 1) for r in range(1, NTP)]
         )
 
     x_copies = gather_rows("x0", r_.xown.at[0], r_.xg.at[0])
     weight_copies = start_all(
         [
-            copy("weights", r_.own_vecs, r_.vecs.at[s], core, 0),
-            copy("weights", r_.own_watt, r_.watt.at[s], core, 1),
-            copy("weights", r_.own_wup, r_.wup.at[s], core, 2),
-            copy("weights", r_.own_wdn, r_.wdn.at[s], core, 3),
+            copy("weights", src, dst, core, i)
+            for i, (src, dst) in enumerate([(r_.vown, r_.vecs.at[s])] + own_weights)
         ]
     )
-    wo_copies = start_all(
-        [copy("wo", r_.own_wo, r_.wo.at[s, t], {"tp": ring(r)}, r - 1) for r in range(1, NTP)]
-    )
-    g_copies = gather_rows("g1", r_.gown.at[1], r_.gg.at[1])
 
     def vector(layer, row, width=D):
         return r_.vecs[layer, row : row + 1, 0:width]
@@ -321,44 +393,60 @@
                 visit(key_block, slot, False)
 
 
-    def key_send(layer, r):
-        d = lax.rem(c + r, NCTX)
+    def key_send(layer, index, part=None):
+        d = stepped(c, index, 1)
+        rows = pl.ds(0, BLK) if part is None else span(part, OWN)
         return c <= top_block(d), copy(
             f"kv{layer}",
-            r_.kvs.at[layer, d // (NCTX // 2)],
-            r_.kvall.at[layer, c],
-            {"ctx": d},
+            r_.kvs.at[layer, second_group(d), rows, :],
+            r_.kvall.at[layer, c, rows, :],
+            at_ctx(d),
             d,
             c,
         )
 
-    def forward(layer, gathers, before_keys, after_keys, before_out):
+    def forward(layer, gathers, before_keys, after_keys, beside_keys, before_out):
         def project(part):
             xhat, _ = normed(r_.xg[layer, part].astype(F32))
             attention_in, _ = norm_outputs(layer, xhat)
             pre = dot_nn(attention_in, r_.watt[layer]) + vector(layer, 6, 384)
             rows = span(part, OWN)
-            cosine, sine = r_.rot[0, 0, rows, :], r_.rot[0, 1, rows, :]
+            cosine, sine = r_.cosine[0, rows, :], r_.sine[0, rows, :]
             query = turn(pre[:, 0:128], cosine, sine) * 0.125
             r_.qs[layer, rows, :] = query.astype(BF16)
-            r_.kvs[layer, 0, rows, :] = turn_left(pre[:, 128:256], cosine, sine).astype(BF16)
-            r_.kvs[layer, 1, rows, :] = turn_left(pre[:, 256:384], cosine, sine).astype(BF16)
+            key, value = turn(pre[:, 128:256], cosine, sine), pre[:, 256:384]
+            left = lanes(key.shape) < HEAD_DIM
+            first = jnp.where(left, key, pltpu.roll(value, HEAD_DIM, 1))
+            second = jnp.where(left, pltpu.roll(key, HEAD_DIM, 1), value)
+            r_.kvs[layer, 0, rows, :] = first.astype(BF16)
+            r_.kvs[layer, 1, rows, :] = second.astype(BF16)
+
+            copy(
+                f"q{layer}",
+                r_.qs.at[layer, rows, :],
+                r_.qin.at[layer, rows, :],
+                at_ctx(partner),
+            ).start()
+
+            @pl.loop(0, AHEAD)
+            def _(index):
+                send_keys(index, part)
+
+        def send_keys(index, part=None):
+            wanted, item = key_send(layer, index, part)
+
+            @pl.when(wanted)
+            def _():
+                item.start()
 
         before_keys()
         project(t)
         for r, item in enumerate(gathers):
             item.wait_recv()
-            project(lax.rem(t + NTP - 1 - r, NTP))
-
-        query_copy = start(copy(f"q{layer}", r_.qs.at[layer], r_.qin.at[layer], {"ctx": partner}))
-
-        @pl.loop(1, NCTX)
-        def _(r):
-            wanted, item = key_send(layer, r)
-
-            @pl.when(wanted)
-            def _():
-                item.start()
+            project(wrap(t + NTP - 1 - r, NTP))
+
+        query_copy = copy(f"q{layer}", r_.qs.at[layer], r_.qin.at[layer], at_ctx(partner))
+        sent.append(query_copy)
 
         r_.kvall[layer, c] = r_.kvs[layer, group]
         after_keys()
@@ -375,18 +463,20 @@
                 f"ff{layer}",
                 r_.ffs.at[layer, r - 1],
                 r_.ffr.at[layer, r - 1],
-                {"tp": ring(r)},
+                at_tp(ring(r)),
                 r - 1,
             )
 
-        @pl.loop(1, NTP)
-        def _(r):
-            r_.ffs[layer, r - 1] = feed_forward(ring(r)).astype(BF16)
-            feed_send(r).start()
-
         feed_copies = [feed_send(r) for r in range(1, NTP)]
         sent.extend(feed_copies)
-        r_.ffo[...] = feed_forward(t)
+
+        def feed_all():
+            @pl.loop(1, NTP)
+            def _(r):
+                r_.ffs[layer, r - 1] = feed_forward(ring(r)).astype(BF16)
+                feed_send(r).start()
+
+            r_.ffo[...] = feed_forward(t)
 
         r_.qpad[layer, 0] = my_head(r_.qs[layer].astype(F32), group, 0).astype(BF16)
         query_copy.wait_recv()
@@ -406,7 +496,19 @@
 
         @pl.loop(0, NCTX)
         def _(r):
-            key_block = lax.rem(c + NCTX - r, NCTX)
+            key_block = jnp.where(r == 0, c, stepped(c, r - 1, -1))
+
+            @pl.when((r > 0) & (r + AHEAD < NCTX))
+            def _():
+                send_keys(r + AHEAD - 1)
+
+            @pl.when(r == 1)
+            def _():
+                feed_all()
+
+            @pl.when(r == 6)
+            def _():
+                beside_keys()
 
             @pl.when(key_block <= top_block(c))
             def _():
@@ -416,7 +518,7 @@
                         f"kv{layer}",
                         r_.kvs.at[layer, 0],
                         r_.kvall.at[layer, key_block],
-                        {"ctx": partner},
+                        at_ctx(partner),
                         0,
                         key_block,
                     ).wait_recv()
@@ -440,7 +542,7 @@
                     f"ob{layer}",
                     r_.oout.at[layer, 1, span(ring(r), OWN), :],
                     r_.ob.at[layer, t],
-                    {"ctx": partner, "tp": ring(r)},
+                    at_partner(ring(r)),
                     r,
                 )
                 for r in range(NTP)
@@ -453,14 +555,14 @@
                     f"oa{layer}",
                     r_.oout.at[layer, 0, span(ring(r), OWN), :],
                     r_.oa.at[layer, t],
-                    {"tp": ring(r)},
+                    at_tp(ring(r)),
                     r - 1,
                 )
                 for r in range(1, NTP)
             ]
         )
         r_.oa[layer, t] = r_.oout[layer, 0, span(t, OWN), :]
-        start(copy(f"ow{layer}", r_.oout.at[layer, 1], r_.oin.at[layer], {"ctx": partner}))
+        start(copy(f"ow{layer}", r_.oout.at[layer, 1], r_.oin.at[layer], at_ctx(partner)))
 
         result = r_.xown[layer].astype(F32) + vector(layer, 4) + r_.ffo[...]
         for r, item in enumerate(feed_copies):
@@ -486,7 +588,7 @@
                     f"dob{layer}",
                     r_.dos.at[layer, ring(r)],
                     r_.dob.at[layer, t],
-                    {"ctx": partner, "tp": ring(r)},
+                    at_partner(ring(r)),
                     r,
                 )
                 for r in range(NTP)
@@ -498,7 +600,7 @@
                     f"doa{layer}",
                     r_.dos.at[layer, ring(r)],
                     r_.doa.at[layer, t],
-                    {"tp": ring(r)},
+                    at_tp(ring(r)),
                     r - 1,
                 )
                 for r in range(1, NTP)
@@ -512,12 +614,44 @@
             f"dkv{layer}",
             r_.dkvo.at[layer, key_block],
             r_.dkvi.at[layer, c],
-            {"ctx": key_block},
+            at_ctx(key_block),
             key_block,
             c,
         )
 
-    def backward(layer, grad_copies, gathers, beside, after_feed):
+    def add_vector(layer, row, value):
+        r_.gv[layer, row : row + 1, :] += jnp.sum(value, axis=0, keepdims=True)
+
+    def feed_backward(layer, gathers):
+        for item in gathers:
+            item.wait_recv()
+        r_.gv[layer] = jnp.zeros((8, D), F32)
+        own_sum = jnp.sum(r_.gown[layer].astype(F32), axis=0, keepdims=True)
+        r_.gv[layer, 4:5, :] = own_sum
+
+        @pl.loop(0, NTP)
+        def _(part):
+            xhat, _ = normed(r_.xg[layer, part].astype(F32))
+            attention_in, feed_in = norm_outputs(layer, xhat)
+            r_.ain[part] = attention_in
+            r_.fin[part] = feed_in
+            up_pre = dot_nn(feed_in, r_.wup[layer]) + vector(layer, 5)
+            hidden_grad = dot_nt(r_.gg[layer, part], r_.wdn[layer])
+            up_grad = (hidden_grad * gelu_slope(up_pre)).astype(BF16)
+            r_.ugs[part] = up_grad
+            add_vector(layer, 5, up_grad.astype(F32))
+            feed_grad = dot_nt(up_grad, r_.wup[layer])
+            add_vector(layer, 1, xhat * feed_grad)
+            add_vector(layer, 3, feed_grad)
+            r_.dxh[part] = feed_grad * vector(layer, 1)
+
+        full_grad = r_.gg[layer].reshape(BLK, D)
+        up_terms = dot_tn(r_.fin[...].reshape(BLK, D), r_.ugs[...].reshape(BLK, D))
+        r_.gwp[layer, 0:D, :] = up_terms.astype(BF16)
+        r_.gwp[layer, D:, :] = dot_tn(r_.hid[layer].reshape(BLK, D), full_grad).astype(BF16)
+
+    def backward(layer, grad_copies, before_keys, beside_keys, after_keys, before_end):
+        before_keys()
         for item in grad_copies:
             item.wait_recv()
 
@@ -544,9 +678,9 @@
             r_.dkva[...] += dot_nn(weights.astype(BF16), grads) + dot_nn(score_grad, queries)
             r_.dqt[slot] += dot_nn(r_.kvt[...], score_grad)
 
-        @pl.loop(1, NCTX + 1)
+        @pl.loop(0, NCTX)
         def _(r):
-            key_block = lax.rem(c + r, NCTX)
+            key_block = jnp.where(r == NCTX - 1, c, stepped(c, r, 1))
 
             @pl.when(key_block <= top_block(c))
             def _():
@@ -555,53 +689,24 @@
                 visit_both(key_block, visit)
                 r_.dkvo[layer, key_block] = r_.dkva[...].astype(BF16)
 
-                @pl.when(r < NCTX)
+                @pl.when(r < NCTX - 1)
                 def _():
                     key_grad_send(layer, key_block).start()
 
         def query_grad(slot):
             tile = two_head_tile(r_.dqt[slot, 0:HEAD_DIM, :] * 0.125, group)
-            return turn(tile, r_.rot[slot, 0], -r_.rot[slot, 1]).astype(BF16)
+            return turn(tile, r_.cosine[slot], -r_.sine[slot]).astype(BF16)
 
         r_.dqs[layer] = query_grad(1)
-        query_copy = start(copy(f"dq{layer}", r_.dqs.at[layer], r_.dqi.at[layer], {"ctx": partner}))
+        query_copy = start(copy(f"dq{layer}", r_.dqs.at[layer], r_.dqi.at[layer], at_ctx(partner)))
         r_.dproj[:, 0:128] = query_grad(0)
 
-        for item in gathers:
-            item.wait_recv()
-        r_.gv[layer] = jnp.zeros((8, D), F32)
-        own_sum = jnp.sum(r_.gown[layer].astype(F32), axis=0, keepdims=True)
-        r_.gv[layer, 4:5, :] = own_sum
-
-        def add_vector(row, value):
-            r_.gv[layer, row : row + 1, :] += jnp.sum(value, axis=0, keepdims=True)
-
-        @pl.loop(0, NTP)
-        def _(part):
-            xhat, _ = normed(r_.xg[layer, part].astype(F32))
-            attention_in, feed_in = norm_outputs(layer, xhat)
-            r_.ain[part] = attention_in
-            r_.fin[part] = feed_in
-            up_pre = dot_nn(feed_in, r_.wup[layer]) + vector(layer, 5)
-            hidden_grad = dot_nt(r_.gg[layer, part], r_.wdn[layer])
-            up_grad = (hidden_grad * gelu_slope(up_pre)).astype(BF16)
-            r_.ugs[part] = up_grad
-            add_vector(5, up_grad.astype(F32))
-            feed_grad = dot_nt(up_grad, r_.wup[layer])
-            add_vector(1, xhat * feed_grad)
-            add_vector(3, feed_grad)
-            r_.dxh[part] = feed_grad * vector(layer, 1)
-
-        full_grad = r_.gg[layer].reshape(BLK, D)
-        up_terms = dot_tn(r_.fin[...].reshape(BLK, D), r_.ugs[...].reshape(BLK, D))
-        r_.gwp[layer, 0:D, :] = up_terms.astype(BF16)
-        r_.gwp[layer, D:, :] = dot_tn(r_.hid[layer].reshape(BLK, D), full_grad).astype(BF16)
-        after_feed()
-        out_copy = copy(f"ow{layer}", r_.oout.at[layer, 1], r_.oin.at[layer], {"ctx": partner})
+        beside_keys()
+        out_copy = copy(f"ow{layer}", r_.oout.at[layer, 1], r_.oin.at[layer], at_ctx(partner))
         out_copy.wait_recv()
         attention = r_.oout[layer, 0] + r_.oin[layer]
+        full_grad = r_.gg[layer].reshape(BLK, D)
         r_.gwq[layer, 0:128, :] = dot_tn(attention, full_grad).astype(BF16)
-        beside()
 
         def key_grad(half):
             r_.dkva[...] = jnp.zeros_like(r_.dkva)
@@ -620,24 +725,29 @@
                         f"dkv{layer}",
                         r_.dkvo.at[layer, 0],
                         r_.dkvi.at[layer, source],
-                        {"ctx": partner},
+                        at_ctx(partner),
                         0,
                         source,
                     ).wait_recv()
                     r_.dkva[...] += r_.dkvi[layer, source].astype(F32)
 
-            return turn_left(r_.dkva[...], r_.rot[0, 0], -r_.rot[0, 1]).astype(BF16)
-
-        r_.dproj[:, 128:256] = key_grad(0)
-        r_.dproj[:, 256:384] = key_grad(1)
+            return turn_left(r_.dkva[...], r_.cosine[0], -r_.sine[0])
+
+        first, second = key_grad(0), key_grad(1)
+        left = lanes(first.shape) < HEAD_DIM
+        key = jnp.where(left, first, pltpu.roll(second, HEAD_DIM, 1))
+        value = jnp.where(left, pltpu.roll(first, HEAD_DIM, 1), second)
+        r_.dproj[:, 128:256] = key.astype(BF16)
+        r_.dproj[:, 256:384] = value.astype(BF16)
+        after_keys()
         query_copy.wait_recv()
         r_.dproj[:, 0:128] += r_.dqi[layer]
 
         def input_part(part):
             xhat, _ = normed(r_.xg[layer, part].astype(F32))
             grad = dot_nt(r_.dproj[span(part, OWN), :], r_.watt[layer])
-            add_vector(0, xhat * grad)
-            add_vector(2, grad)
+            add_vector(layer, 0, xhat * grad)
+            add_vector(layer, 2, grad)
             return r_.dxh[part] + grad * vector(layer, 0)
 
         scatters = []
@@ -647,7 +757,7 @@
                 f"dx{layer}",
                 r_.dxs.at[layer, r - 1],
                 r_.dxr.at[layer, r - 1],
-                {"tp": ring(r)},
+                at_tp(ring(r)),
                 r - 1,
             )
             scatters.append(start(item))
@@ -656,6 +766,7 @@
         r_.gv[layer, 6:7, 0:384] = bias_sum
         terms = dot_tn(r_.dproj[...], r_.ain[...].reshape(BLK, D))
         r_.gwq[layer, 128:, :] = terms.astype(BF16)
+        before_end()
         for r, item in enumerate(scatters):
             item.wait_recv()
             total = total + r_.dxr[layer, r].astype(F32)
@@ -681,12 +792,12 @@
 
     def scatter_copy(which, r):
         _, _, sums, arrived, _, _, kind, _, _ = wide_parts[which]
-        d = lax.rem(c + r, NCTX)
-        return copy(kind, sums.at[d], arrived.at[r], {"ctx": d}, r)
+        d = wrap(c + r, NCTX)
+        return copy(kind, sums.at[d], arrived.at[r], at_ctx(d), r)
 
     def gather_copy(which, r):
         _, _, _, _, mine, full, _, kind, _ = wide_parts[which]
-        return copy(kind, mine, full.at[c], {"ctx": lax.rem(c + r, NCTX)}, r)
+        return copy(kind, mine, full.at[c], at_ctx(wrap(c + r, NCTX)), r)
 
     def scatter_terms(which, layer):
         terms, crossed, sums, _, _, _, _, _, chunk = wide_parts[which]
@@ -707,8 +818,18 @@
 
     def store_chunk(which, j, value):
         chunk = wide_parts[which][-1]
-        target = (r_.out_ff, r_.allq)[which]
-        target[span(j, chunk), :] = value
+        if which == 1:
+            r_.allq[span(j, chunk), :] = value
+            return
+        half = D // chunk
+
+        @pl.when(j < half)
+        def _():
+            r_.out_up[0, span(j, chunk), :] = value
+
+        @pl.when(j >= half)
+        def _():
+            r_.out_dn[0, span(j - half, chunk), :] = value
 
     def gather_sums(which, layer):
         _, _, sums, arrived, mine, _, _, _, _ = wide_parts[which]
@@ -734,15 +855,15 @@
         def _():
             @pl.loop(1, NCTX)
             def _(r):
-                source = lax.rem(c + NCTX - r, NCTX)
+                source = wrap(c + NCTX - r, NCTX)
                 copy(kind, mine, full.at[source], core, r).wait_recv()
                 store_chunk(which, source, full[source].astype(F32))
 
     def vector_copy(r):
-        return copy("vc", r_.vec, r_.vec_in.at[r], {"ctx": lax.rem(c + r, NCTX)}, r)
+        return copy("vc", r_.vec, r_.vec_in.at[r], at_ctx(wrap(c + r, NCTX)), r)
 
     def vector_tp_copy(r):
-        return copy("vt", r_.vec_tp, r_.vec_tp_in.at[r - 1], {"tp": ring(r)}, r - 1)
+        return copy("vt", r_.vec_tp, r_.vec_tp_in.at[r - 1], at_tp(ring(r)), r - 1)
 
     def vector_first(layer):
         @pl.when(s == layer)
@@ -773,17 +894,19 @@
             for r in range(1, NTP):
                 vector_tp_copy(r).wait_recv()
                 shared = shared + r_.vec_tp_in[r - 1]
-            row = lax.broadcasted_iota(jnp.int32, shared.shape, 0)
-            r_.out_small[...] = jnp.where(row < 5, shared, total)
+            r_.out_gain[0] = shared[0:2, :]
+            r_.out_norm_bias[0] = shared[2:4, :]
+            r_.out_branch[...] = shared[4:5, :]
+            r_.out_up_bias[...] = total[5:6, :]
+            for k in range(3):
+                bias = total[6:7, k * LANES : (k + 1) * LANES]
+                r_.out_att_bias[0, k : k + 1, :] = bias
 
     def store_attention():
-        r_.out_wo[...] = r_.allq[0:128, :]
+        r_.out_wo[0] = r_.allq[0:128, :]
         turned = r_.allq[128:, :].T
-        first, second = turned[:, 128:256], turned[:, 256:384]
-        left = lanes(first.shape) < HEAD_DIM
-        r_.out_att[0] = turned[:, 0:128]
-        r_.out_att[1] = jnp.where(left, first, pltpu.roll(second, HEAD_DIM, 1))
-        r_.out_att[2] = jnp.where(left, pltpu.roll(first, HEAD_DIM, 1), second)
+        for k in range(3):
+            r_.out_att[0, k] = turned[:, k * LANES : (k + 1) * LANES]
 
 
     def nothing():
@@ -792,52 +915,83 @@
     def wait_first_weights():
         for load in loads:
             load.wait()
-        weight_copies[0].wait_recv()
-        weight_copies[1].wait_recv()
-
-    def wait_other_weights():
-        weight_copies[2].wait_recv()
-        weight_copies[3].wait_recv()
+        for item in weight_copies[:4]:
+            item.wait_recv()
+
+    wo_copies, g_copies = [], []
+
+    def start_later_gathers():
+        for r in range(1, NTP):
+            item = copy("wo", r_.own_wo.at[0], r_.wo.at[s, t], at_tp(ring(r)), r - 1)
+            wo_copies.append(start(item))
+        g_copies.extend(gather_rows("g1", r_.gown.at[1], r_.gg.at[1]))
+        for item in weight_copies[4:]:
+            item.wait_recv()
+
+    def pass_output_weight():
         for item in wo_copies:
             item.wait_recv()
         start(wo_pass)
 
     wo_pass = copy("wo_pass", r_.wo.at[s], r_.wo.at[s], core)
-    forward(0, x_copies, wait_first_weights, wait_other_weights, wo_pass.wait_recv)
+    forward(
+        0,
+        x_copies,
+        wait_first_weights,
+        start_later_gathers,
+        pass_output_weight,
+        wo_pass.wait_recv,
+    )
     r_.xown[1] = r_.fo[0]
     x_copies = gather_rows("x1", r_.xown.at[1], r_.xg.at[1])
     grad_copies = send_attention_grads(1)
-    forward(1, x_copies, nothing, nothing, nothing)
-
-    rows_copy = start(copy("rows", r_.fo.at[1 - s], r_.out_rows.at[s], core))
-    r_.out_rows[s] = r_.fo[s]
-
-    backward(1, grad_copies, g_copies, nothing, lambda: cross_start(0, 1))
+
+    def feed_ahead():
+        feed_backward(1, g_copies)
+        cross_start(0, 1)
+
+    forward(1, x_copies, nothing, nothing, feed_ahead, nothing)
+
+    rows_copy = start(copy("rows", r_.fo.at[1 - s], r_.out_rows.at[0, s], core))
+    r_.out_rows[0, s] = r_.fo[s]
+
+    def late_sums(layer):
+        cross_start(1, layer)
+        cross_start(2, layer)
+
+    backward(
+        1,
+        grad_copies,
+        lambda: scatter_terms(0, 1),
+        lambda: gather_sums(0, 1),
+        nothing,
+        lambda: late_sums(1),
+    )
     r_.gown[0] = r_.go[1]
+    grad_copies = send_attention_grads(0)
     g_copies = gather_rows("g0", r_.gown.at[0], r_.gg.at[0])
-    grad_copies = send_attention_grads(0)
-    cross_start(1, 1)
-    cross_start(2, 1)
-    scatter_terms(0, 1)
-
-    def beside_last():
+
+    def finish_second():
         scatter_terms(1, 1)
         vector_first(1)
-        gather_sums(0, 1)
-        scatter_terms(0, 0)
-
-    backward(0, grad_copies, g_copies, beside_last, lambda: cross_start(0, 0))
-    cross_start(1, 0)
-    cross_start(2, 0)
-    grads_copy = start(copy("grads", r_.go.at[1 - s], r_.out_grads.at[s], core))
-    r_.out_grads[s] = r_.go[s]
-    scatter_terms(1, 0)
-    vector_first(0)
-    gather_sums(0, 0)
-    gather_sums(1, 1)
-    vector_second(1)
+
+    def feed_last():
+        feed_backward(0, g_copies)
+        cross_start(0, 0)
+        gather_sums(1, 1)
+        vector_second(1)
+
+    def before_last():
+        late_sums(0)
+        gather_sums(0, 0)
+        scatter_terms(1, 0)
+        vector_first(0)
+
+    backward(0, grad_copies, finish_second, feed_last, lambda: scatter_terms(0, 0), before_last)
+    grads_copy = start(copy("grads", r_.go.at[1 - s], r_.out_grads.at[0, s], core))
+    r_.out_grads[0, s] = r_.go[s]
+    gather_sums(1, 0)
     vector_second(0)
-    gather_sums(1, 0)
     for layer in (1, 0):
         store_sums(0, layer)
         vector_last(layer)
@@ -853,13 +1007,13 @@
 
         @pl.loop(1, NCTX)
         def _(r):
-            wanted, item = key_send(layer, r)
+            wanted, item = key_send(layer, r - 1)
 
             @pl.when(wanted)
             def _():
                 item.wait_send()
 
-            key_block = lax.rem(c + r, NCTX)
+            key_block = wrap(c + r, NCTX)
 
             @pl.when(key_block <= top_block(c))
             def _():
@@ -883,15 +1037,14 @@
 
 def run_step(operands):
     vmem = pl.BlockSpec(memory_space=pltpu.VMEM)
-    anywhere = pl.BlockSpec(memory_space=pl.ANY)
     dma = pltpu.SemaphoreType.DMA
     return pl.pallas_call(
         step_kernel,
         out_shape=[jax.ShapeDtypeStruct(shape, kind) for _, shape, kind in OUTPUTS],
-        in_specs=[anywhere if name.startswith("own_") else vmem for name in INPUTS],
+        in_specs=[pl.BlockSpec(memory_space=space) for _, space in INPUTS],
         out_specs=[vmem] * len(OUTPUTS),
         scratch_shapes=[pltpu.VMEM(shape, kind) for _, shape, kind in SCRATCH]
-        + [dma((COPIES,)), dma((COPIES,)), dma((5,))],
+        + [dma((COPIES,)), dma((COPIES,)), dma((6,))],
         compiler_params=pltpu.CompilerParams(
             collective_id=0, has_side_effects=True, vmem_limit_bytes=VMEM_LIMIT
         ),
@@ -899,25 +1052,22 @@
     )(*operands)
 
 
-def sequence_starts(lengths, positions):
-    ends = jnp.cumsum(lengths).astype(jnp.int32)
-    before = jnp.where(ends[None, :] <= positions[:, None], lengths[None, :], 0)
-    return jnp.sum(before, axis=1).astype(jnp.int32)
-
-
-def rotary_lanes(offsets):
-    rates = 1.0 / 10000.0 ** (jnp.arange(0, ROT, 2).astype(F32) / ROT)
-    rest = jnp.zeros((HEAD_DIM - ROT,), F32)
-    rates = jnp.concatenate([rates, rates, rest] * 2)
-    signs = jnp.where(jnp.arange(LANES) % HEAD_DIM < ROT // 2, -1.0, 1.0)
-    angles = offsets.astype(F32)[..., None] * rates
-    return jnp.stack([jnp.cos(angles), jnp.sin(angles) * signs], axis=1)
-
-
-def pack_attention(items):
-    q, k, v = items
-    half = HEAD_DIM
-    return jnp.concatenate([q, k[:, :half], v[:, :half], k[:, half:], v[:, half:]], axis=1)
+def hand_over_kernel(*refs):
+    count = len(refs) // 2
+    for source, result in zip(refs[:count], refs[count:]):
+        result[...] = source[...]
+
+
+def hand_over(arrays):
+    vmem = [pl.BlockSpec(memory_space=pltpu.VMEM)] * len(arrays)
+    return pl.pallas_call(
+        hand_over_kernel,
+        out_shape=[jax.ShapeDtypeStruct(a.shape, a.dtype) for a in arrays],
+        in_specs=vmem,
+        out_specs=vmem,
+        compiler_params=pltpu.CompilerParams(vmem_limit_bytes=VMEM_LIMIT),
+        name="hand_over",
+    )(*arrays)
 
 
 def local(
@@ -934,58 +1084,23 @@
     down_weight,
     branch_bias,
 ):
-    s = lax.axis_index("section")
-    c = lax.axis_index("ctx")
-    packed_bias = pack_attention([attention_bias[:, k] for k in range(3)])
-    vectors = jnp.concatenate(
-        [
-            norm_gain[0],
-            norm_bias[0],
-            branch_bias,
-            up_bias,
-            jnp.pad(packed_bias, ((0, 0), (0, D - 384))),
-            jnp.zeros((1, D), F32),
-        ]
-    )
-    lengths = jnp.where(s == 0, sequence_lengths[0], sequence_lengths[1])
-    steps = jnp.arange(BLK, dtype=jnp.int32)
-    positions = jnp.stack([c * BLK + steps, (NCTX - 1 - c) * BLK + steps])
-    starts = sequence_starts(lengths, positions.reshape(-1)).reshape(2, BLK)
-    rows, grads, ff, wo, att, small = run_step(
+    results = run_step(
         (
             block_input,
             output_grad,
-            pack_attention([attention_weight[0, k] for k in range(3)]),
-            output_weight[0],
-            up_weight[0],
-            down_weight[0],
-            vectors,
-            rotary_lanes(positions - starts),
-            jnp.stack([positions, starts], axis=1),
+            sequence_lengths,
+            norm_gain,
+            norm_bias,
+            attention_weight,
+            attention_bias,
+            output_weight,
+            up_weight,
+            up_bias,
+            down_weight,
+            branch_bias,
         )
     )
-    half = HEAD_DIM
-    bias = small[6, 0:384]
-    bias_parts = jnp.stack(
-        [
-            bias[0:128],
-            jnp.concatenate([bias[128 : 128 + half], bias[256 : 256 + half]]),
-            jnp.concatenate([bias[128 + half : 256], bias[256 + half :]]),
-        ]
-    )
-    return (
-        rows[None],
-        grads[None],
-        small[None, 0:2],
-        small[None, 2:4],
-        att[None],
-        bias_parts[None],
-        wo[None],
-        ff[None, 0:D],
-        small[5:6],
-        ff[None, D:],
-        small[4:5],
-    )
+    return tuple(hand_over(results))
 
 
 def solution(mesh):

time: 263 us -> 240 us (0.913)
  local copies, waits for them, and re-layouts: 15.5 us -> 2.5 us
  other arithmetic: 5.53 us -> 0 us
  Pallas kernels: 241 us -> 237 us
    pallas_call x1, Pallas kernels: 241 us -> 233 us  [run_step(): pl.pallas_call(step_kernel, out_shape=[jax.ShapeDtypeStruct(shape, kind)...]
    broadcast_in_dim x4 -> x0, local copies, waits for them, and re-layouts: 4.53 us -> none  [the longest x1 3.13 us: local(): ff[None, D:]]
    pallas_call x0 -> x1, Pallas kernels: none -> 3.87 us  [hand_over(): pl.pallas_call(hand_over_kernel, out_shape=[jax.ShapeDtypeStruct(a.shape,...]
    slice x5 -> x0, local copies, waits for them, and re-layouts: 3.09 us -> none  [the longest x1 1.38 us: local(): small[4:5]]
    another operation x7 -> x0, other arithmetic: 2.75 us -> none  [the longest x1 1.04 us: rotary_lanes(): return jnp.stack([jnp.cos(angles), jnp.sin(angles) * signs], axis=1)]
where the time goes in v3:
time: 240 us
  Pallas kernels  237 us (99%)
  local copies, waits for them, and re-layouts  2.5 us (1%)
    pallas_call x1, Pallas kernels, run_step(): pl.pallas_call(step_kernel, out_shape=[jax.ShapeDtypeStruct(shape, kind)...  233 us

profile of v3, /device:TPU:0, one launch (start us, length us, event | category | flops | bytes accessed | tf_op | source)
XLA Modules:
  0.0 240.0 jit_solution(1119659085838234365)
XLA Ops:
  0.6 1.3 copy.23.refs_6_
  1.9 232.9 %train_step.1 = (bf16[1,2,128,512]{3,2,1,0:T(8,128)(2,1)}, bf16[1,2,128,512]{3,2,1,0:T(8,128)(2,1)}, f32[1,2,512]{2,1,0:T(2,128)}, f32[1,2,512]{2,1,0:T(2,128)},...) custom-call(bf16[2,128,512]{2,1,0:T(8,128)(2,1)} %refs_0_.1, ...), custom_call_target="tpu_custom_call" | custom-call | tf_op jit(solution)/shard_map/train_step/pallas_call | solution.py:1041
  234.9 3.9 %hand_over.1 = (bf16[1,2,128,512]{3,2,1,0:T(8,128)(2,1)}, bf16[1,2,128,512]{3,2,1,0:T(8,128)(2,1)}, f32[1,2,512]{2,1,0:T(2,128)}, f32[1,2,512]{2,1,0:T(2,128)}, ...) custom-call(bf16[1,2,128,512]{3,2,1,0:T(8,128)(2,1)} %get-tuple-elem, ...), custom_call_target="tpu_custom_call" | custom-call | tf_op jit(solution)/shard_map/hand_over/pallas_call | solution.py:1063
  238.7 0.0 copy-start
  238.7 0.7 copy-done
  239.4 0.6 copy.24
Async XLA Ops:
  238.7 0.7 copy-start

commit v4 on v3

--- a/solution.py
+++ b/solution.py
@@ -23,7 +23,7 @@
     (0, 1), (1, 0), (0, 3), (3, 0), (1, 1), (3, 3), (1, 3), (3, 1),
     (0, 2), (2, 0), (1, 2), (3, 2), (2, 1), (2, 3), (2, 2),
 )
-AHEAD = 5
+AHEAD = 8
 MASKED = -1e30
 LOWEST = -1e29
 
@@ -127,12 +127,10 @@
     ("out_grads", (1, 2, OWN, D), BF16),
     ("out_gain", (1, 2, D), F32),
     ("out_norm_bias", (1, 2, D), F32),
-    ("out_att", (1, 3, D, OWN), F32),
+    ("out_p", (NCTX, 64, D), BF16),
+    ("out_q", (NCTX, 32, D), BF16),
     ("out_att_bias", (1, 3, OWN), F32),
-    ("out_wo", (1, OWN, D), F32),
-    ("out_up", (1, D, D), F32),
     ("out_up_bias", (1, D), F32),
-    ("out_dn", (1, D, D), F32),
     ("out_branch", (1, D), F32),
 )
 
@@ -198,11 +196,6 @@
     ("sumq", (NCTX, 32, D), BF16),
     ("inp", (NCTX, 64, D), BF16),
     ("inq", (NCTX, 32, D), BF16),
-    ("minep", (64, D), BF16),
-    ("mineq", (32, D), BF16),
-    ("gatp", (NCTX, 64, D), BF16),
-    ("gatq", (NCTX, 32, D), BF16),
-    ("allq", (D, D), F32),
     ("vec", (8, D), F32),
     ("vec_in", (NCTX, 8, D), F32),
     ("vec_tp", (8, D), F32),
@@ -326,6 +319,24 @@
     for k in range(3):
         r_.vown[6:7, k * LANES : (k + 1) * LANES] = r_.att_bias[0, k : k + 1, :]
     r_.vecs[s] = r_.vown[...]
+    r_.xown[0] = r_.xin[s]
+    r_.gown[1] = r_.gin[s]
+    pl.semaphore_wait(barrier, len(peers))
+
+    def gather_rows(kind, own, full):
+        full[t] = own[...]
+        return start_all(
+            [copy(kind, own, full.at[t], at_tp(ring(r)), r - 1) for r in range(1, NTP)]
+        )
+
+    x_copies = gather_rows("x0", r_.xown.at[0], r_.xg.at[0])
+    weight_copies = start_all(
+        [
+            copy("weights", src, dst, core, i)
+            for i, (src, dst) in enumerate([(r_.vown, r_.vecs.at[s])] + own_weights)
+        ]
+    )
+
     rate_row = lax.broadcasted_iota(jnp.int32, (ROT // 2, 1), 0)
     rates = jnp.zeros((ROT // 2, 1), F32)
     for i in range(ROT // 2):
@@ -347,23 +358,6 @@
         sine = jnp.concatenate([-sine, sine, still], axis=0)
         r_.cosine[slot] = jnp.concatenate([cosine, cosine], axis=0).T
         r_.sine[slot] = jnp.concatenate([sine, sine], axis=0).T
-    r_.xown[0] = r_.xin[s]
-    r_.gown[1] = r_.gin[s]
-    pl.semaphore_wait(barrier, len(peers))
-
-    def gather_rows(kind, own, full):
-        full[t] = own[...]
-        return start_all(
-            [copy(kind, own, full.at[t], at_tp(ring(r)), r - 1) for r in range(1, NTP)]
-        )
-
-    x_copies = gather_rows("x0", r_.xown.at[0], r_.xg.at[0])
-    weight_copies = start_all(
-        [
-            copy("weights", src, dst, core, i)
-            for i, (src, dst) in enumerate([(r_.vown, r_.vecs.at[s])] + own_weights)
-        ]
-    )
 
     def vector(layer, row, width=D):
         return r_.vecs[layer, row : row + 1, 0:width]
@@ -650,7 +644,7 @@
         r_.gwp[layer, 0:D, :] = up_terms.astype(BF16)
         r_.gwp[layer, D:, :] = dot_tn(r_.hid[layer].reshape(BLK, D), full_grad).astype(BF16)
 
-    def backward(layer, grad_copies, before_keys, beside_keys, after_keys, before_end):
+    def backward(layer, grad_copies, before_keys, among_keys, beside_keys, after_keys, before_end):
         before_keys()
         for item in grad_copies:
             item.wait_recv()
@@ -681,6 +675,10 @@
         @pl.loop(0, NCTX)
         def _(r):
             key_block = jnp.where(r == NCTX - 1, c, stepped(c, r, 1))
+
+            @pl.when(r == AHEAD)
+            def _():
+                among_keys()
 
             @pl.when(key_block <= top_block(c))
             def _():
@@ -786,21 +784,21 @@
             cross_copy(which, layer).start()
 
     wide_parts = (
-        (r_.gwp, r_.crp, r_.sump, r_.inp, r_.minep, r_.gatp, "ps", "pg", 64),
-        (r_.gwq, r_.crq, r_.sumq, r_.inq, r_.mineq, r_.gatq, "qs", "qg", 32),
+        (r_.gwp, r_.crp, r_.sump, r_.inp, r_.out_p, "ps", "pg", 64),
+        (r_.gwq, r_.crq, r_.sumq, r_.inq, r_.out_q, "qs", "qg", 32),
     )
 
     def scatter_copy(which, r):
-        _, _, sums, arrived, _, _, kind, _, _ = wide_parts[which]
+        _, _, sums, arrived, _, kind, _, _ = wide_parts[which]
         d = wrap(c + r, NCTX)
         return copy(kind, sums.at[d], arrived.at[r], at_ctx(d), r)
 
     def gather_copy(which, r):
-        _, _, _, _, mine, full, _, kind, _ = wide_parts[which]
-        return copy(kind, mine, full.at[c], at_ctx(wrap(c + r, NCTX)), r)
+        _, _, _, _, full, _, kind, _ = wide_parts[which]
+        return copy(kind, full.at[c], full.at[c], at_ctx(wrap(c + r, NCTX)), r)
 
     def scatter_terms(which, layer):
-        terms, crossed, sums, _, _, _, _, _, chunk = wide_parts[which]
+        terms, crossed, sums, _, _, _, _, chunk = wide_parts[which]
 
         @pl.when(s == layer)
         def _():
@@ -816,23 +814,8 @@
             def _(r):
                 scatter_copy(which, r).start()
 
-    def store_chunk(which, j, value):
-        chunk = wide_parts[which][-1]
-        if which == 1:
-            r_.allq[span(j, chunk), :] = value
-            return
-        half = D // chunk
-
-        @pl.when(j < half)
-        def _():
-            r_.out_up[0, span(j, chunk), :] = value
-
-        @pl.when(j >= half)
-        def _():
-            r_.out_dn[0, span(j - half, chunk), :] = value
-
     def gather_sums(which, layer):
-        _, _, sums, arrived, mine, _, _, _, _ = wide_parts[which]
+        _, _, sums, arrived, full, _, _, _ = wide_parts[which]
 
         @pl.when(s == layer)
         def _():
@@ -840,24 +823,21 @@
             for r in range(1, NCTX):
                 scatter_copy(which, r).wait_recv()
                 total = total + arrived[r].astype(F32)
-            mine[...] = total.astype(BF16)
+            full[c] = total.astype(BF16)
 
             @pl.loop(1, NCTX)
             def _(r):
                 gather_copy(which, r).start()
 
-            store_chunk(which, c, total)
-
-    def store_sums(which, layer):
-        _, _, _, _, mine, full, _, kind, _ = wide_parts[which]
+    def await_sums(which, layer):
+        _, _, _, _, full, _, kind, _ = wide_parts[which]
 
         @pl.when(s == layer)
         def _():
             @pl.loop(1, NCTX)
             def _(r):
                 source = wrap(c + NCTX - r, NCTX)
-                copy(kind, mine, full.at[source], core, r).wait_recv()
-                store_chunk(which, source, full[source].astype(F32))
+                copy(kind, full.at[c], full.at[source], core, r).wait_recv()
 
     def vector_copy(r):
         return copy("vc", r_.vec, r_.vec_in.at[r], at_ctx(wrap(c + r, NCTX)), r)
@@ -902,12 +882,6 @@
                 bias = total[6:7, k * LANES : (k + 1) * LANES]
                 r_.out_att_bias[0, k : k + 1, :] = bias
 
-    def store_attention():
-        r_.out_wo[0] = r_.allq[0:128, :]
-        turned = r_.allq[128:, :].T
-        for k in range(3):
-            r_.out_att[0, k] = turned[:, k * LANES : (k + 1) * LANES]
-
 
     def nothing():
         pass
@@ -963,6 +937,7 @@
         1,
         grad_copies,
         lambda: scatter_terms(0, 1),
+        nothing,
         lambda: gather_sums(0, 1),
         nothing,
         lambda: late_sums(1),
@@ -978,25 +953,34 @@
     def feed_last():
         feed_backward(0, g_copies)
         cross_start(0, 0)
+
+    def sums_beside():
+        scatter_terms(0, 0)
         gather_sums(1, 1)
         vector_second(1)
 
     def before_last():
         late_sums(0)
-        gather_sums(0, 0)
         scatter_terms(1, 0)
         vector_first(0)
 
-    backward(0, grad_copies, finish_second, feed_last, lambda: scatter_terms(0, 0), before_last)
+    backward(
+        0,
+        grad_copies,
+        finish_second,
+        feed_last,
+        sums_beside,
+        lambda: gather_sums(0, 0),
+        before_last,
+    )
     grads_copy = start(copy("grads", r_.go.at[1 - s], r_.out_grads.at[0, s], core))
     r_.out_grads[0, s] = r_.go[s]
     gather_sums(1, 0)
     vector_second(0)
     for layer in (1, 0):
-        store_sums(0, layer)
+        await_sums(0, layer)
         vector_last(layer)
-        store_sums(1, layer)
-    store_attention()
+        await_sums(1, layer)
     rows_copy.wait_recv()
     grads_copy.wait_recv()
 
@@ -1052,19 +1036,47 @@
     )(*operands)
 
 
-def hand_over_kernel(*refs):
-    count = len(refs) // 2
-    for source, result in zip(refs[:count], refs[count:]):
-        result[...] = source[...]
+RESULTS = (
+    ((1, 2, OWN, D), BF16),
+    ((1, 2, OWN, D), BF16),
+    ((1, 2, D), F32),
+    ((1, 2, D), F32),
+    ((1, 3, D, OWN), F32),
+    ((1, 3, OWN), F32),
+    ((1, OWN, D), F32),
+    ((1, D, D), F32),
+    ((1, D), F32),
+    ((1, D, D), F32),
+    ((1, D), F32),
+)
+
+
+def hand_over_kernel(
+    rows_in, grads_in, gain_in, norm_bias_in, p_in, q_in, att_bias_in, up_bias_in, branch_in, *results
+):
+    rows, grads, gain, norm_bias, att, att_bias, wo, up, up_bias, dn, branch = results
+    rows[...] = rows_in[...]
+    grads[...] = grads_in[...]
+    gain[...] = gain_in[...]
+    norm_bias[...] = norm_bias_in[...]
+    att_bias[...] = att_bias_in[...]
+    up_bias[...] = up_bias_in[...]
+    branch[...] = branch_in[...]
+    up[0] = p_in[0:8].astype(F32).reshape(D, D)
+    dn[0] = p_in[8:16].astype(F32).reshape(D, D)
+    wo[0] = q_in[0:4].astype(F32).reshape(OWN, D)
+    turned = q_in[4:16].astype(F32).reshape(384, D).T
+    for k in range(3):
+        att[0, k] = turned[:, k * LANES : (k + 1) * LANES]
 
 
 def hand_over(arrays):
-    vmem = [pl.BlockSpec(memory_space=pltpu.VMEM)] * len(arrays)
+    vmem = pl.BlockSpec(memory_space=pltpu.VMEM)
     return pl.pallas_call(
         hand_over_kernel,
-        out_shape=[jax.ShapeDtypeStruct(a.shape, a.dtype) for a in arrays],
-        in_specs=vmem,
-        out_specs=vmem,
+        out_shape=[jax.ShapeDtypeStruct(shape, kind) for shape, kind in RESULTS],
+        in_specs=[vmem] * len(arrays),
+        out_specs=[vmem] * len(RESULTS),
         compiler_params=pltpu.CompilerParams(vmem_limit_bytes=VMEM_LIMIT),
         name="hand_over",
     )(*arrays)

time: 240 us -> 232 us (0.967)
  Pallas kernels: 237 us -> 228 us
    pallas_call x1, Pallas kernels: 233 us -> 225 us  [run_step(): pl.pallas_call(step_kernel, out_shape=[jax.ShapeDtypeStruct(shape, kind)...]
where the time goes in v4:
time: 232 us; the launch traced here: 231 us
  Pallas kernels  228 us (98%)
  local copies, waits for them, and re-layouts  2.5 us (1%)
    pallas_call x1, Pallas kernels, run_step(): pl.pallas_call(step_kernel, out_shape=[jax.ShapeDtypeStruct(shape, kind)...  225 us

profile of v4, /device:TPU:0, one launch (start us, length us, event | category | flops | bytes accessed | tf_op | source)
XLA Modules:
  0.0 231.4 jit_solution(12930804282132211652)
XLA Ops:
  0.6 1.3 copy.23.refs_6_
  1.9 224.7 %train_step.1 = (bf16[1,2,128,512]{3,2,1,0:T(8,128)(2,1)}, bf16[1,2,128,512]{3,2,1,0:T(8,128)(2,1)}, f32[1,2,512]{2,1,0:T(2,128)}, f32[1,2,512]{2,1,0:T(2,128)},...) custom-call(bf16[2,128,512]{2,1,0:T(8,128)(2,1)} %refs_0_.1, ...), custom_call_target="tpu_custom_call" | custom-call | tf_op jit(solution)/shard_map/train_step/pallas_call | solution.py:1025
  226.6 3.5 %hand_over.1 = (bf16[1,2,128,512]{3,2,1,0:T(8,128)(2,1)}, bf16[1,2,128,512]{3,2,1,0:T(8,128)(2,1)}, f32[1,2,512]{2,1,0:T(2,128)}, f32[1,2,512]{2,1,0:T(2,128)}, ...) custom-call(bf16[1,2,128,512]{3,2,1,0:T(8,128)(2,1)} %get-tuple-elem, ...), custom_call_target="tpu_custom_call" | custom-call | tf_op jit(solution)/shard_map/hand_over/pallas_call | solution.py:1075
  230.1 0.0 copy-start
  230.1 0.7 copy-done
  230.8 0.6 copy.24
Async XLA Ops:
  230.1 0.7 copy-start

commit v5 on v4

--- a/solution.py
+++ b/solution.py
@@ -129,7 +129,7 @@
     ("out_norm_bias", (1, 2, D), F32),
     ("out_p", (NCTX, 64, D), BF16),
     ("out_q", (NCTX, 32, D), BF16),
-    ("out_att_bias", (1, 3, OWN), F32),
+    ("out_att_bias", (3, 1, OWN), F32),
     ("out_up_bias", (1, D), F32),
     ("out_branch", (1, D), F32),
 )
@@ -317,7 +317,7 @@
     r_.vown[4:5, :] = r_.branch_bias[...]
     r_.vown[5:6, :] = r_.up_bias[...]
     for k in range(3):
-        r_.vown[6:7, k * LANES : (k + 1) * LANES] = r_.att_bias[0, k : k + 1, :]
+        r_.vown[6:7, k * LANES : (k + 1) * LANES] = r_.att_bias[k]
     r_.vecs[s] = r_.vown[...]
     r_.xown[0] = r_.xin[s]
     r_.gown[1] = r_.gin[s]
@@ -880,7 +880,7 @@
             r_.out_up_bias[...] = total[5:6, :]
             for k in range(3):
                 bias = total[6:7, k * LANES : (k + 1) * LANES]
-                r_.out_att_bias[0, k : k + 1, :] = bias
+                r_.out_att_bias[k] = bias
 
 
     def nothing():
@@ -1042,7 +1042,7 @@
     ((1, 2, D), F32),
     ((1, 2, D), F32),
     ((1, 3, D, OWN), F32),
-    ((1, 3, OWN), F32),
+    ((3, 1, OWN), F32),
     ((1, OWN, D), F32),
     ((1, D, D), F32),
     ((1, D), F32),
@@ -1104,7 +1104,7 @@
             norm_gain,
             norm_bias,
             attention_weight,
-            attention_bias,
+            jnp.swapaxes(attention_bias, 0, 1),
             output_weight,
             up_weight,
             up_bias,
@@ -1112,7 +1112,8 @@
             branch_bias,
         )
     )
-    return tuple(hand_over(results))
+    results = hand_over(results)
+    return tuple(results[:5]) + (jnp.swapaxes(results[5], 0, 1),) + tuple(results[6:])
 
 
 def solution(mesh):

time: 232 us -> 228 us (0.983)
  local copies, waits for them, and re-layouts: 2.5 us -> 0 us
where the time goes in v5:
time: 228 us
  Pallas kernels  227 us (100%)
    pallas_call x1, Pallas kernels, run_step(): pl.pallas_call(step_kernel, out_shape=[jax.ShapeDtypeStruct(shape, kind)...  224 us

profile of v5, /device:TPU:0, one launch (start us, length us, event | category | flops | bytes accessed | tf_op | source)
XLA Modules:
  0.0 227.7 jit_solution(15674166632668059620)
XLA Ops:
  0.6 223.5 %train_step.1 = (bf16[1,2,128,512]{3,2,1,0:T(8,128)(2,1)}, bf16[1,2,128,512]{3,2,1,0:T(8,128)(2,1)}, f32[1,2,512]{2,1,0:T(2,128)}, f32[1,2,512]{2,1,0:T(2,128)},...) custom-call(bf16[2,128,512]{2,1,0:T(8,128)(2,1)} %refs_0_.1, ...), custom_call_target="tpu_custom_call" | custom-call | tf_op jit(solution)/shard_map/train_step/pallas_call | solution.py:1025
  224.2 3.5 %hand_over.1 = (bf16[1,2,128,512]{3,2,1,0:T(8,128)(2,1)}, bf16[1,2,128,512]{3,2,1,0:T(8,128)(2,1)}, f32[1,2,512]{2,1,0:T(2,128)}, f32[1,2,512]{2,1,0:T(2,128)}, ...) custom-call(bf16[1,2,128,512]{3,2,1,0:T(8,128)(2,1)} %get-tuple-elem, ...), custom_call_target="tpu_custom_call" | custom-call | tf_op jit(solution)/shard_map/hand_over/pallas_call | solution.py:1075
